TPU v7x, 32 devices: a whole 2x2x4 slice. The times are simulated.
32 devices in a mesh: segment: 4 (over y, core), dp: 8 (over z, x).
Axes of the slice: x: 2, y: 2, z: 4, core: 2. Of those that a mesh axis runs over, the one named last changes fastest.
Arguments:
- images: bfloat16 [64, 256, 1024], P('dp'), may hold values from -6 to 6
- texts: bfloat16 [64, 64, 1536], P('dp'), may hold values from -6 to 6
- section_weights: bfloat16 [4, 21504, 128], P('segment'), may hold values from -0.15625 to 0.15625
- uniting_weights: bfloat16 [3584, 1024], P('dp'), may hold values from -0.125 to 0.125
- codebooks: float32 [8, 2, 256, 1024], P('dp'), may hold values from -3 to 3
- neg_bank: bfloat16 [8, 256, 1024], P('dp'), may hold values from -6 to 6
- item_cats: int32 [4, 16, 1], replicated, may hold values from 0 to 7; in each aligned block of 16 rows (0 to 15, 16 to 31, ..., all dimensions but the last counted through in order) at most 2 rows name the same one
- cat_slot: int32 [8], replicated, may hold values from 0 to 7, each once
- neg_index: int32 [4, 16, 128], replicated, may hold values from 0 to 255
Outputs:
- uniting_grad: float32 [3584, 1024], P('dp')
- codebook_grad: float32 [8, 2, 256, 1024], P('dp')
- owner_loss: float32 [8], P('dp')
Inputs may be any that keep to these rules, and one draw needn't show every extreme that they name: `item_cats`: within one row of 128 no category appears more than 2 times, and in some row some category appears exactly 2 times. `cat_slot`: A permutation: every category has its own slot; slot t lies with owner t.
All inputs are finite; a program needn't handle non-finite values.
Results may differ from a plain program's by a relative error of at most 0.028.
Values may be sent and summed in bfloat16 or wider, within the bound.
No kernel may reach another device: no remote copies, remote signals or barrier semaphores. Data moves between devices by JAX's collectives and lax.ppermute only.
A program may use at most 128 MiB of HBM per device.

v0:
```python
import math

import jax
import jax.numpy as jnp
from jax import lax
from jax.sharding import PartitionSpec as P

HEAD_IMG = 64
HEAD_TXT = 128
CAP = 2


norm_eps = 1e-06
rope_theta = 1000000.0
contrast_temp = 0.1
beta_weight = 1.0
highest = lax.Precision.HIGHEST


def gelu_value(inputs_f):
    return 0.5 * inputs_f * (1.0 + lax.erf(inputs_f / math.sqrt(2.0)))


def gelu_slope(inputs_f):
    return 0.5 * (1.0 + lax.erf(inputs_f / math.sqrt(2.0))) + inputs_f * jnp.exp(
        -0.5 * inputs_f * inputs_f
    ) / math.sqrt(2.0 * math.pi)


def rotate_pairs(tensor, positions):
    half_dim = tensor.shape[-1] // 2
    exponents = jnp.arange(half_dim).astype(jnp.float32) * (2.0 / tensor.shape[-1])
    inverse_freq = jnp.exp(-math.log(rope_theta) * exponents)
    angles = positions[:, None] * inverse_freq[None, :]
    cosine = jnp.concatenate([jnp.cos(angles), jnp.cos(angles)], axis=-1)[:, None, :]
    sine = jnp.concatenate([jnp.sin(angles), jnp.sin(angles)], axis=-1)[:, None, :]
    rotated = jnp.concatenate([-tensor[..., half_dim:], tensor[..., :half_dim]], axis=-1)
    return tensor * cosine + rotated * sine


def softmax_rows(scores):
    scores = scores - jnp.max(scores, axis=-1, keepdims=True)
    exp_scores = jnp.exp(scores)
    return (exp_scores / jnp.sum(exp_scores, axis=-1, keepdims=True)).astype(jnp.bfloat16)


def image_attention(images, flat_slot):
    item_count, patch_count, model_width = images.shape
    half_width = model_width // 2
    head_count = half_width // HEAD_IMG
    qkv_size = model_width * 3 * half_width
    w_qkv = flat_slot[:qkv_size].reshape(model_width, 3 * half_width)
    w_out = flat_slot[qkv_size : qkv_size + half_width * model_width].reshape(
        half_width, model_width
    )
    float_tokens = images.astype(jnp.float32)
    centred = float_tokens - jnp.mean(float_tokens, axis=-1, keepdims=True)
    variance = jnp.mean(centred * centred, axis=-1, keepdims=True)
    normed = (centred * lax.rsqrt(variance + norm_eps)).astype(jnp.bfloat16)
    projections = jnp.einsum(
        "bpd,de->bpe", normed, w_qkv, preferred_element_type=jnp.float32
    ).astype(jnp.bfloat16)
    queries = projections[..., :half_width].reshape(item_count, patch_count, head_count, HEAD_IMG)
    key_rows = projections[..., half_width : 2 * half_width].reshape(
        item_count, patch_count, head_count, HEAD_IMG
    )
    value_rows = projections[..., 2 * half_width :].reshape(
        item_count, patch_count, head_count, HEAD_IMG
    )
    scores = jnp.einsum(
        "bqhc,bkhc->bhqk", queries, key_rows, preferred_element_type=jnp.float32
    ) / math.sqrt(HEAD_IMG)
    probabilities = softmax_rows(scores)
    attended = jnp.einsum(
        "bhqk,bkhc->bqhc", probabilities, value_rows, preferred_element_type=jnp.float32
    ).astype(jnp.bfloat16)
    attended = attended.reshape(item_count, patch_count, half_width)
    projected = jnp.einsum("bpc,cd->bpd", attended, w_out, preferred_element_type=jnp.float32)
    return jnp.mean(projected, axis=1)


def text_attention(texts, flat_slot):
    item_count, token_count, model_width = texts.shape
    half_width = model_width // 2
    head_count = half_width // HEAD_TXT
    inner_width = half_width + 2 * HEAD_TXT
    qkv_size = model_width * inner_width
    w_qkv = flat_slot[:qkv_size].reshape(model_width, inner_width)
    w_out = flat_slot[qkv_size : qkv_size + half_width * model_width].reshape(
        half_width, model_width
    )
    float_tokens = texts.astype(jnp.float32)
    normed = (
        float_tokens
        * lax.rsqrt(jnp.mean(float_tokens * float_tokens, axis=-1, keepdims=True) + norm_eps)
    ).astype(jnp.bfloat16)
    projections = jnp.einsum("btd,de->bte", normed, w_qkv, preferred_element_type=jnp.float32)
    positions = jnp.arange(token_count).astype(jnp.float32)
    queries = rotate_pairs(
        projections[..., :half_width].reshape(item_count, token_count, head_count, HEAD_TXT),
        positions,
    ).astype(jnp.bfloat16)
    key_rows = rotate_pairs(
        projections[..., half_width : half_width + HEAD_TXT].reshape(
            item_count, token_count, 1, HEAD_TXT
        ),
        positions,
    )[:, :, 0, :].astype(jnp.bfloat16)
    value_rows = projections[..., half_width + HEAD_TXT :].astype(jnp.bfloat16)
    scores = jnp.einsum(
        "bqhc,bkc->bhqk", queries, key_rows, preferred_element_type=jnp.float32
    ) / math.sqrt(HEAD_TXT)
    causal = jnp.arange(token_count)[:, None] >= jnp.arange(token_count)[None, :]
    scores = jnp.where(causal, scores, -1e30)
    probabilities = softmax_rows(scores)
    attended = jnp.einsum(
        "bhqk,bkc->bqhc", probabilities, value_rows, preferred_element_type=jnp.float32
    ).astype(jnp.bfloat16)
    attended = attended.reshape(item_count, token_count, half_width)
    projected = jnp.einsum("btc,cd->btd", attended, w_out, preferred_element_type=jnp.float32)
    return jnp.mean(projected, axis=1)


def merge_forward(embedded, stacked):
    first_rows = embedded.shape[1]
    float_embed = embedded.astype(jnp.float32)
    normed = (
        float_embed
        * lax.rsqrt(jnp.mean(float_embed * float_embed, axis=1, keepdims=True) + norm_eps)
    ).astype(jnp.bfloat16)
    hidden = jnp.dot(normed, stacked[:first_rows], preferred_element_type=jnp.float32)
    activated = gelu_value(hidden).astype(jnp.bfloat16)
    merged = jnp.dot(activated, stacked[first_rows:], preferred_element_type=jnp.float32).astype(
        jnp.bfloat16
    )
    return (normed, hidden, activated, merged)


def merge_backward(hidden, stacked, out_grad, first_rows):
    w_second = stacked[first_rows:]
    act_grad = lax.dot_general(
        out_grad, w_second, (((1,), (1,)), ((), ())), preferred_element_type=jnp.float32
    )
    return (act_grad * gelu_slope(hidden)).astype(jnp.bfloat16)


def item_loss(merged_row, book_rows, negatives):
    emb_width = merged_row.shape[0]
    quant_tau = math.sqrt(emb_width) / 2.0
    residual = merged_row * lax.rsqrt(jnp.mean(merged_row * merged_row) + norm_eps)
    quantized = jnp.zeros_like(merged_row)
    for level_index in range(book_rows.shape[0]):
        code_rows = book_rows[level_index]
        cross_terms = jnp.dot(code_rows, residual, precision=highest)
        logits = (2.0 * cross_terms - jnp.sum(code_rows * code_rows, axis=1)) / quant_tau
        logits = logits - lax.stop_gradient(jnp.max(logits))
        exp_logits = jnp.exp(logits)
        chosen = jnp.dot(exp_logits / jnp.sum(exp_logits), code_rows, precision=highest)
        residual = residual - chosen
        quantized = quantized + chosen
    recon_error = jnp.mean(residual * residual)
    anchor = quantized * lax.rsqrt(jnp.mean(quantized * quantized) + norm_eps)
    candidates = jnp.concatenate([merged_row[None, :], negatives.astype(jnp.float32)], axis=0)
    cand_unit = candidates * lax.rsqrt(
        jnp.mean(candidates * candidates, axis=1, keepdims=True) + norm_eps
    )
    similarity = jnp.dot(cand_unit, anchor, precision=highest) / (emb_width * contrast_temp)
    top_score = lax.stop_gradient(jnp.max(similarity))
    contrast = top_score + jnp.log(jnp.sum(jnp.exp(similarity - top_score))) - similarity[0]
    return contrast + beta_weight * recon_error


def stacked_term(columns, first_grad, second_grad, in_first):
    contract = (((0,), (0,)), ((), ()))
    first_term = lax.dot_general(columns, first_grad, contract, preferred_element_type=jnp.float32)
    second_term = lax.dot_general(
        columns, second_grad, contract, preferred_element_type=jnp.float32
    )
    return jnp.where(in_first[:, None], first_term, second_term)


def per_device(
    images,
    texts,
    section_weights,
    uniting_weights,
    codebooks,
    neg_bank,
    item_cats,
    cat_slot,
    neg_index,
):
    segment_index = lax.axis_index("segment")
    segment_count = lax.axis_size("segment")
    dp_index = lax.axis_index("dp")
    dp_count = lax.axis_size("dp")
    group_index = segment_index % 2
    item_count = images.shape[0]
    flat_slot = section_weights.reshape(-1)
    residual_flag = jnp.where(group_index == 0, 1.0, 0.0).astype(jnp.float32)

    def image_branch(operands):
        image_rows, text_rows, slot_rows = operands
        pooled = image_attention(image_rows, slot_rows) + residual_flag * jnp.mean(
            image_rows.astype(jnp.float32), axis=1
        )
        return jnp.concatenate(
            [pooled, jnp.zeros((item_count, text_rows.shape[2]), jnp.float32)], axis=1
        )

    def text_branch(operands):
        image_rows, text_rows, slot_rows = operands
        pooled = text_attention(text_rows, slot_rows) + residual_flag * jnp.mean(
            text_rows.astype(jnp.float32), axis=1
        )
        return jnp.concatenate(
            [jnp.zeros((item_count, image_rows.shape[2]), jnp.float32), pooled], axis=1
        )

    packed = lax.cond(segment_index < 2, image_branch, text_branch, (images, texts, flat_slot))
    embedded = lax.psum_scatter(packed, "segment", scatter_dimension=0, tiled=True).astype(
        jnp.bfloat16
    )
    stacked = lax.all_gather(uniting_weights, "dp", axis=0, tiled=True)
    first_rows = embedded.shape[1]
    cat_per_dev = codebooks.shape[0]
    slot_count = cat_per_dev * CAP
    row_total = item_cats.shape[1]
    cats_all = item_cats.reshape(-1)
    entry_count = cats_all.shape[0]
    entry_ids = jnp.arange(entry_count)
    category_match = cats_all[:, None] == jnp.arange(cat_slot.shape[0])[None, :]
    entry_slots = jnp.sum(jnp.where(category_match, cat_slot[None, :], 0), axis=1)
    entry_owner = entry_slots // cat_per_dev
    entry_local = entry_slots % cat_per_dev
    entry_row = entry_ids // row_total
    earlier = entry_ids[None, :] < entry_ids[:, None]
    same_cat = (cats_all[:, None] == cats_all[None, :]) & (entry_row[:, None] == entry_row[None, :])
    entry_rank = jnp.sum(jnp.where(earlier & same_cat, 1, 0), axis=1)
    entry_place = entry_local * CAP + entry_rank
    entry_position = entry_row * slot_count + entry_place
    owned = entry_owner == dp_index
    all_slots = segment_count * slot_count
    slot_match_all = owned[None, :] & (entry_position[None, :] == jnp.arange(all_slots)[:, None])
    view_match = lax.dynamic_slice(
        slot_match_all,
        (segment_index * slot_count, segment_index * row_total),
        (slot_count, row_total),
    )
    view_base = segment_index * row_total
    view_slots = view_match.shape[0]
    selection = view_match.astype(jnp.bfloat16)
    valid = jnp.sum(view_match.astype(jnp.float32), axis=1)
    slot_item = jnp.sum(
        jnp.where(view_match, jnp.arange(view_match.shape[1])[None, :] + view_base, 0), axis=1
    )
    slot_negs = jnp.take(neg_index.reshape(entry_count, -1), slot_item, axis=0)
    slot_local = jnp.arange(view_slots) % slot_count // CAP
    bank_rows = neg_bank.reshape(-1, neg_bank.shape[2])
    negatives = jnp.take(bank_rows, slot_local[:, None] * neg_bank.shape[1] + slot_negs, axis=0)
    loss_scale = 1.0 / math.sqrt(dp_count * item_count)

    def owner_objective(merged_float, books):
        per_row = jax.vmap(item_loss)(merged_float, books[slot_local], negatives)
        return jnp.sum(per_row * valid) * loss_scale

    gathered = jnp.dot(
        selection,
        lax.all_gather(embedded, "dp", axis=0, tiled=True),
        preferred_element_type=jnp.float32,
    )
    gathered = gathered.astype(jnp.bfloat16)
    normed_all, hidden_all, activated_all, merged_all = merge_forward(gathered, stacked)
    loss_local, pullback = jax.vjp(owner_objective, merged_all.astype(jnp.float32), codebooks)
    grad_all, book_grad = pullback(jnp.ones((), jnp.float32))
    out_grad = grad_all.astype(jnp.bfloat16)
    hidden_grad = merge_backward(hidden_all, stacked, out_grad, first_rows)
    joined = jnp.concatenate([normed_all, activated_all], axis=1)
    book_total, loss_owner = lax.psum((book_grad, loss_local), "segment")
    shard_rows = uniting_weights.shape[0]
    shard_start = dp_index * shard_rows
    shard_first = shard_start + jnp.arange(shard_rows) < first_rows
    joined_piece = lax.all_gather(joined, "dp", axis=0, tiled=True)
    first_piece = lax.all_gather(hidden_grad, "dp", axis=0, tiled=True)
    second_piece = lax.all_gather(out_grad, "dp", axis=0, tiled=True)
    columns = lax.dynamic_slice_in_dim(joined_piece, shard_start, shard_rows, 1)
    segment_grad = stacked_term(columns, first_piece, second_piece, shard_first)
    uniting_grad = lax.psum(segment_grad, "segment")
    return (uniting_grad, book_total, loss_owner.reshape(1))


def solution(mesh):
    placed = (
        P("dp", None, None),
        P("dp", None, None),
        P("segment", None, None),
        P("dp", None),
        P("dp", None, None, None),
        P("dp", None, None),
        P(),
        P(),
        P(),
    )
    return jax.shard_map(
        per_device,
        mesh=mesh,
        in_specs=placed,
        out_specs=(P("dp", None), P("dp", None, None, None), P("dp")),
        check_vma=False,
    )
```

profile of v0, /device:TPU:0, one launch (start us, length us, event | category | flops | bytes accessed | tf_op | source)
XLA Modules:
  0.0 354.7 jit_solution(6353942272931626991)
XLA Ops:
  9.9 65.3 %conditional.1 = (f32[8,2560]{1,0:T(8,128)S(1)}) conditional(s32[]{:T(128)} %convert_element_type.98, (bf16[8,64,1536]{2,1,0:T(8,128)(2,1)}, bf16[2752512]{0:T(1024)(128)(2,1)}, f32[]{:T(128)}) %tuple.55, (bf16[8,256,1024]{2,1,0:T(8,128)(2,1)}, bf16[2752512]{0:T(1024)(128)(2,1)}, f32[]{:T(128)}) %tuple.56), branch_computations={%region_2.8_spmd, %region_8.15_spmd} | conditional | flops 9714018304 | bytes 131555384 | solution.py:220
  10.1 3.0 convert_reduce_fusion.2
  13.1 3.5 fusion.43
  16.6 1.8 slice.87
  18.4 6.9 %reshape.489 = bf16[1024,1536,1]{1,0,2:T(8,128)(2,1)} reshape(bf16[1572864]{0:T(1024)(128)(2,1)} %slice.87) | data formatting | bytes 6291456 | tf_op jit(solution)/shard_map/cond/branch_1_fun/slice | solution.py:52
  25.3 9.9 %convolution_convert_fusion.1 = bf16[8,256,1536]{2,1,0:T(8,128)(2,1)S(1)} fusion(bf16[1024,1536,1]{1,0,2:T(8,128)(2,1)} %reshape.489, bf16[8,256,1024]{2,1,0:T(8,128)(2,1)} %get-tuple-element.27, f32[8,256]{1,0:T(8,128)S(1)} %add_rsqrt_fusion.1, f32[8,256]{1,0:T(8,128)S(1)} %broadcast_multiply_fusion), kind=kOutput, calls=%fused_computation.65 | convolution fusion | flops 6453985280 | bytes 13647872 | tf_op jit(solution)/shard_map/cond/branch_1_fun/bpd,de->bpe/dot_general | solution.py:60
  35.2 2.8 fusion.166
  38.0 4.0 %copy.70 = bf16[8,256,512]{1,2,0:T(8,128)(2,1)} copy(bf16[8,256,512]{2,1,0:T(8,128)(2,1)} %get-tuple-element.63) | data formatting | bytes 4194304 | tf_op jit(solution)/shard_map/cond/branch_1_fun/slice | solution.py:63
  42.0 3.9 %copy.71 = bf16[8,256,512]{1,2,0:T(8,128)(2,1)} copy(bf16[8,256,512]{2,1,0:T(8,128)(2,1)} %get-tuple-element.62) | data formatting | bytes 4194304 | tf_op jit(solution)/shard_map/cond/branch_1_fun/slice | solution.py:64
  45.9 10.6 %fusion.167 = (f32[8,8,256]{2,1,0:T(8,128)S(1)}, f32[8,8,256,256]{2,3,1,0:T(8,128)}) fusion(bf16[8,256,8,64]{1,3,2,0:T(8,128)(2,1)} %bitcast.232, bf16[8,256,8,64]{1,3,2,0:T(8,128)(2,1)} %bitcast.233), kind=kOutput, calls=%fused_computation.282 | convolution fusion | flops 549454080 | bytes 21037056 | tf_op jit(solution)/shard_map/cond/branch_1_fun/sub | solution.py:42
  56.5 2.4 copy.69
  58.9 10.3 %fusion.52 = bf16[8,8,64,256]{3,2,1,0:T(8,128)(2,1)} fusion(bf16[8,256,8,64]{1,3,2,0:T(8,128)(2,1)} %bitcast.234, f32[8,8,256,256]{2,3,1,0:T(8,128)} %get-tuple-element.66, f32[8,8,256]{2,1,0:T(8,128)S(1)} %get-tuple-element.65), kind=kOutput, calls=%fused_computation.70 | convolution fusion | flops 546308096 | bytes 21037056 | tf_op jit(solution)/shard_map/cond/branch_1_fun/bhqk,bkhc->bqhc/dot_general | solution.py:74
  71.0 4.0 %convolution_reduce_fusion.1 = f32[8,1024]{1,0:T(8,128)S(1)} fusion(bf16[8,256,512]{1,2,0:T(8,128)(2,1)} %bitcast.244, bf16[512,1024,1]{1,0,2:T(8,128)(2,1)S(1)} %reshape.490), kind=kOutput, calls=%fused_computation.68 | convolution fusion | flops 2149572608 | bytes 3178496 | tf_op jit(solution)/shard_map/cond/branch_1_fun/bpc,cd->bpd/dot_general | solution.py:78
  75.2 12.1 %all-reduce.5 = bf16[8,2560]{1,0:T(8,128)(2,1)S(1)} all-reduce(f32[8,2560]{1,0:T(8,128)S(1)} %get-tuple-element.92), channel_id=2, replica_groups=mesh['segment'=4,'dp'=8] {'segment'}, use_global_device_ids=true, to_apply=%region_15.16.clone | all-reduce | flops 20480 | bytes 122880
  87.3 31.9 %all-gather = bf16[8,2,2560]{2,1,0:T(2,128)(2,1)S(1)} all-gather(bf16[1,2,2560]{2,1,0:T(2,128)(2,1)S(1)} %fusion.106), channel_id=1, replica_groups=mesh['segment'=4,'dp'=8] {'dp'}, dimensions={0}, use_global_device_ids=true | all-gather | bytes 92160 | tf_op jit(solution)/shard_map/all_gather | solution.py:269
  126.7 3.3 multiply_convert_fusion.1
  130.0 2.1 multiply_reduce_fusion.9
  132.2 1.7 fusion.98
  139.9 1.8 broadcast_multiply_fusion.2
  144.4 2.2 fusion.80
  146.8 1.9 fusion.86
  152.3 1.8 multiply_reduce_fusion.1
  156.2 2.2 fusion.77
  158.5 30.4 %all-gather.2 = bf16[8,2,1024]{2,1,0:T(2,128)(2,1)S(1)} all-gather(bf16[1,2,1024]{2,1,0:T(2,128)(2,1)S(1)} %fusion.77), channel_id=1, replica_groups=mesh['segment'=4,'dp'=8] {'dp'}, dimensions={0}, use_global_device_ids=true | all-gather | bytes 36864 | tf_op jit(solution)/shard_map/all_gather | solution.py:284
  188.9 30.6 %all-gather.1 = bf16[8,2,3584]{2,1,0:T(2,128)(2,1)S(1)} all-gather(bf16[1,2,3584]{2,1,0:T(2,128)(2,1)S(1)} %maximum_bitcast_fusion), channel_id=1, replica_groups=mesh['segment'=4,'dp'=8] {'dp'}, dimensions={0}, use_global_device_ids=true | all-gather | bytes 129024 | tf_op jit(solution)/shard_map/all_gather | solution.py:283
  219.6 30.4 %all-gather.3 = bf16[8,2,1024]{2,1,0:T(2,128)(2,1)S(1)} all-gather(bf16[1,2,1024]{2,1,0:T(2,128)(2,1)S(1)} %bitcast.242), channel_id=1, replica_groups=mesh['segment'=4,'dp'=8] {'dp'}, dimensions={0}, use_global_device_ids=true | all-gather | bytes 36864 | tf_op jit(solution)/shard_map/all_gather | solution.py:285
  251.1 2.2 pad_add_fusion
  253.5 4.5 %scatter_fusion = f32[2,256,1024,1]{2,1,3,0:T(8,128)S(1)} fusion(f32[2,256,1024,1]{2,1,3,0:T(8,128)S(1)} %broadcast.671, s32[2]{0:T(128)S(1)} %fusion.141, f32[2,2,256,1024]{3,2,1,0:T(8,128)} %pad_add_fusion), kind=kCustom, calls=%fused_computation.2 | custom fusion | flops 1048576 | bytes 12582920 | tf_op jit(solution)/shard_map/transpose(jvp())/scatter-add | solution.py:264
  258.5 1.8 convolution_select_fusion
  261.6 6.8 %psum.23 = f32[1]{0:T(128)} all-reduce(f32[1]{0:T(128)} %bitcast.56), channel_id=1, replica_groups=mesh['segment'=4,'dp'=8] {'segment'}, use_global_device_ids=true, to_apply=%region_40.41 | all-reduce | flops 1 | bytes 8 | tf_op jit(solution)/shard_map/psum | solution.py:279
  268.4 74.6 %all-reduce.9.cloned.1.call-done = (f32[448,1024]{1,0:T(8,128)}, f32[1,2,256,1024]{3,2,1,0:T(8,128)}) async-done(((f32[448,1024]{1,0:T(8,128)}, f32[1,2,256,1024]{3,2,1,0:T(8,128)}), (f32[448,1024]{1,0:T(8,128)}, f32[1,2,256,1024]{3,2,1,0:T(8,128)})) %all-reduce.9.cloned.1.call-update) | async-done | bytes 3932176 | tf_op jit(solution)/shard_map/psum | solution.py:288
  343.0 3.1 copy.189
  (135 shorter events, 29.7 us)
Async XLA Ops:
  7.2 115.6 %copy-start = (bf16[1,256,1024]{2,1,0:T(8,128)(2,1)S(1)}, bf16[1,256,1024]{2,1,0:T(8,128)(2,1)}, u32[]{:S(2)}) copy-start(bf16[1,256,1024]{2,1,0:T(8,128)(2,1)} %param.16) | copy-start | bytes 1572868
  7.2 119.5 %all-gather.6.cloned.1.call-start = ((), (), s32[]{:S(2)}) async-start(), calls=%async_computation | async-start | bytes 8257536 | tf_op jit(solution)/shard_map/all_gather | solution.py:224
  7.9 335.1 %all-reduce.9.cloned.1.call-start = ((), (), s32[]{:S(2)}) async-start(), calls=%async_computation.1 | async-start | bytes 7864320 | tf_op jit(solution)/shard_map/psum | solution.py:288
  9.9 109.8 %copy-start.11 = (s32[4,16,1]{1,2,0:T(1,128)S(1)}, s32[4,16,1]{1,2,0:T(1,128)}, u32[]{:S(2)}) copy-start(s32[4,16,1]{1,2,0:T(1,128)} %param.17) | copy-start | bytes 772
  9.9 110.6 %copy-start.12 = (s32[8]{0:T(128)S(1)}, s32[8]{0:T(128)}, u32[]{:S(2)}) copy-start(s32[8]{0:T(128)} %param.18) | copy-start | bytes 100
  10.1 6.5 %copy-start.4 = (bf16[2752512]{0:T(1024)(128)(2,1)S(1)}, bf16[2752512]{0:T(1024)(128)(2,1)}, u32[]{:S(2)}) copy-start(bf16[2752512]{0:T(1024)(128)(2,1)} %get-tuple-element.19) | copy-start | bytes 16515076 | tf_op jit(solution)/shard_map/cond
  122.8 1.6 copy-start.6
  123.9 2.5 copy-start.7
  132.2 6.8 %copy-start.2 = (f32[2,128,1024]{2,0,1:T(2,128)S(1)}, f32[2,128,1024]{2,0,1:T(2,128)}, u32[]{:S(2)}) copy-start(f32[2,128,1024]{2,0,1:T(2,128)} %fusion.100) | copy-start | bytes 3145732
  139.8 6.7 %copy-start.10 = (f32[2,129]{0,1:T(8,128)}, f32[2,129]{0,1:T(8,128)S(1)}, u32[]{:S(2)}) copy-start(f32[2,129]{0,1:T(8,128)S(1)} %copy.77) | copy-start | bytes 3100
  141.6 1.0 copy-start.5
  144.4 7.9 %copy-start.3 = (f32[2,128,1024]{2,0,1:T(2,128)S(1)}, f32[2,128,1024]{2,0,1:T(2,128)}, u32[]{:S(2)}) copy-start(f32[2,128,1024]{2,0,1:T(2,128)} %fusion.100) | copy-start | bytes 3145732
  150.2 5.2 %slice-start = ((f32[2,129]{0,1:T(8,128)}), f32[2,1]{0,1:T(1,128)S(1)}, s32[]{:S(2)}) async-start(f32[2,129]{0,1:T(8,128)} %copy-done.10), calls=%async_computation.2 | async-start | bytes 1024 | tf_op jit(solution)/shard_map/transpose(jvp(vmap()))/split | solution.py:163
  258.0 2.3 copy-start.1
  343.0 3.1 copy-start.8
Sparse Core Ops, SparseCore 0:
  10.2 115.5 all-gather.5
  260.5 82.4 all-reduce.8
where the time goes:
time: 361 us; the launch traced here: 355 us
  blocking collectives  142 us (39%)
  waiting for transfers between devices  75.3 us (21%)
  matrix products  59.8 us (17%)
  local copies, waits for them, and re-layouts  34.8 us (10%)
  other arithmetic  25.9 us (7%)
  between operations  16.2 us (4%)
    psum x1, waiting for transfers between devices, per_device(): uniting_grad = lax.psum(segment_grad, 'segment')  74.6 us
    all_gather x1, blocking collectives, per_device(): lax.all_gather(embedded, 'dp', axis=0, tiled=True)  31.9 us
    all_gather x1, blocking collectives, per_device(): joined_piece = lax.all_gather(joined, 'dp', axis=0, tiled=True)  30.6 us
    all_gather x1, blocking collectives, per_device(): first_piece = lax.all_gather(hidden_grad, 'dp', axis=0, tiled=True)  30.4 us
    all_gather x1, blocking collectives, per_device(): second_piece = lax.all_gather(out_grad, 'dp', axis=0, tiled=True)  30.4 us
    unnamed x1, blocking collectives  12.1 us
    sub x1, matrix products, softmax_rows(): scores = scores - jnp.max(scores, axis=-1, keepdims=True)  10.6 us
    dot_general x1, matrix products, image_attention(): jnp.einsum('bhqk,bkhc->bqhc', probabilities, value_rows, preferred_elemen...  10.3 us
  transfers between devices with their start and end apart: 2, of which 1 were waited for; matrix products, arithmetic and copies ran while one was open for 21% of the time, Pallas kernels for 0%

commit v1 on v0

--- a/solution.py
+++ b/solution.py
@@ -1,9 +1,16 @@
+import functools
 import math
 
 import jax
 import jax.numpy as jnp
+import numpy as np
 from jax import lax
+from jax.experimental import pallas as pl
+from jax.experimental.pallas import tpu as pltpu
 from jax.sharding import PartitionSpec as P
+
+F32 = jnp.float32
+BF16 = jnp.bfloat16
 
 HEAD_IMG = 64
 HEAD_TXT = 128
@@ -27,99 +34,168 @@
     ) / math.sqrt(2.0 * math.pi)
 
 
-def rotate_pairs(tensor, positions):
-    half_dim = tensor.shape[-1] // 2
-    exponents = jnp.arange(half_dim).astype(jnp.float32) * (2.0 / tensor.shape[-1])
-    inverse_freq = jnp.exp(-math.log(rope_theta) * exponents)
-    angles = positions[:, None] * inverse_freq[None, :]
-    cosine = jnp.concatenate([jnp.cos(angles), jnp.cos(angles)], axis=-1)[:, None, :]
-    sine = jnp.concatenate([jnp.sin(angles), jnp.sin(angles)], axis=-1)[:, None, :]
-    rotated = jnp.concatenate([-tensor[..., half_dim:], tensor[..., :half_dim]], axis=-1)
-    return tensor * cosine + rotated * sine
-
-
-def softmax_rows(scores):
-    scores = scores - jnp.max(scores, axis=-1, keepdims=True)
-    exp_scores = jnp.exp(scores)
-    return (exp_scores / jnp.sum(exp_scores, axis=-1, keepdims=True)).astype(jnp.bfloat16)
-
-
-def image_attention(images, flat_slot):
+def dot_nt(a, b):
+    return lax.dot_general(a, b, (((1,), (1,)), ((), ())), preferred_element_type=F32)
+
+def dot_nn(a, b):
+    return jnp.dot(a, b, preferred_element_type=F32)
+
+def two_parts(value):
+    high = value.astype(BF16)
+    return jnp.concatenate([high, (value - high.astype(F32)).astype(BF16)], axis=0)
+
+def dot_two(value, weights):
+    rows = value.shape[0]
+    both = dot_nn(two_parts(value), weights)
+    return both[:rows] + both[rows:]
+
+def unfold(slot_ref, first, out_ref, wide_ref, row_step):
+    rows, columns = out_ref.shape
+    blocks = columns // 128
+    def body(step, carry):
+        start = pl.multiple_of(step * row_step, row_step)
+        source = pl.multiple_of(first + step * (row_step * blocks), 16)
+        wide_ref[0 : row_step * blocks, :] = slot_ref[0, pl.ds(source, row_step * blocks), :].astype(F32)
+        for block in range(blocks):
+            piece = wide_ref[pl.ds(block, row_step, stride=blocks), :]
+            out_ref[pl.ds(start, row_step), block * 128 : (block + 1) * 128] = piece.astype(BF16)
+        return carry
+    lax.fori_loop(0, rows // row_step, body, 0)
+
+def image_kernel(flag_ref, image_ref, slot_ref, pooled_ref, w_in, w_out, wide, heads_mean):
+    step = pl.program_id(0)
+    item_count, model_width = pooled_ref.shape
+    half_width = model_width // 2
+    head_count = half_width // HEAD_IMG
+    patch_count = image_ref.shape[1]
+
+    @pl.when(step == 0)
+    def _():
+        unfold(slot_ref, 0, w_in, wide, 128)
+        unfold(slot_ref, model_width * 12, w_out, wide, 128)
+
+    tokens = image_ref[0].astype(F32)
+    centred = tokens - jnp.mean(tokens, axis=1, keepdims=True)
+    variance = jnp.mean(centred * centred, axis=1, keepdims=True)
+    normed = (centred * lax.rsqrt(variance + norm_eps)).astype(BF16)
+    queries = (dot_nn(normed, w_in[:, :half_width]).astype(BF16) * (1.0 / math.sqrt(HEAD_IMG))).astype(BF16)
+    keys = dot_nn(normed, w_in[:, half_width : 2 * half_width]).astype(BF16)
+    row_ids = lax.broadcasted_iota(jnp.int32, (head_count, patch_count), 0)
+    weights = jnp.zeros((head_count, patch_count), F32)
+    for head in range(head_count):
+        span = slice(head * HEAD_IMG, (head + 1) * HEAD_IMG)
+        scores = dot_nt(keys[:, span], queries[:, span])
+        exps = jnp.exp(scores - jnp.max(scores, axis=0, keepdims=True))
+        share = (1.0 / patch_count) / jnp.sum(exps, axis=0, keepdims=True)
+        share = jnp.where(row_ids == head, share, 0.0).astype(BF16)
+        weights = weights + dot_nt(share, exps.astype(BF16))
+    heads_mean[pl.ds(step * head_count, head_count), :] = dot_two(weights, normed)
+    residual = jnp.mean(tokens, axis=0, keepdims=True) * flag_ref[0].astype(F32)
+    pooled_ref[pl.ds(step, 1), :] = residual
+
+    @pl.when(step == item_count - 1)
+    def _():
+        values = dot_two(heads_mean[...], w_in[:, 2 * half_width :])
+        rows = lax.broadcasted_iota(jnp.int32, values.shape, 0)
+        columns = lax.broadcasted_iota(jnp.int32, values.shape, 1)
+        values = jnp.where(rows % head_count == columns // HEAD_IMG, values, 0.0)
+        attended = jnp.sum(values.reshape(item_count, head_count, half_width), axis=1)
+        pooled_ref[...] += dot_two(attended, w_out[...])
+
+def image_pooled(images, slot, flag):
     item_count, patch_count, model_width = images.shape
     half_width = model_width // 2
     head_count = half_width // HEAD_IMG
-    qkv_size = model_width * 3 * half_width
-    w_qkv = flat_slot[:qkv_size].reshape(model_width, 3 * half_width)
-    w_out = flat_slot[qkv_size : qkv_size + half_width * model_width].reshape(
-        half_width, model_width
-    )
-    float_tokens = images.astype(jnp.float32)
-    centred = float_tokens - jnp.mean(float_tokens, axis=-1, keepdims=True)
-    variance = jnp.mean(centred * centred, axis=-1, keepdims=True)
-    normed = (centred * lax.rsqrt(variance + norm_eps)).astype(jnp.bfloat16)
-    projections = jnp.einsum(
-        "bpd,de->bpe", normed, w_qkv, preferred_element_type=jnp.float32
-    ).astype(jnp.bfloat16)
-    queries = projections[..., :half_width].reshape(item_count, patch_count, head_count, HEAD_IMG)
-    key_rows = projections[..., half_width : 2 * half_width].reshape(
-        item_count, patch_count, head_count, HEAD_IMG
-    )
-    value_rows = projections[..., 2 * half_width :].reshape(
-        item_count, patch_count, head_count, HEAD_IMG
-    )
-    scores = jnp.einsum(
-        "bqhc,bkhc->bhqk", queries, key_rows, preferred_element_type=jnp.float32
-    ) / math.sqrt(HEAD_IMG)
-    probabilities = softmax_rows(scores)
-    attended = jnp.einsum(
-        "bhqk,bkhc->bqhc", probabilities, value_rows, preferred_element_type=jnp.float32
-    ).astype(jnp.bfloat16)
-    attended = attended.reshape(item_count, patch_count, half_width)
-    projected = jnp.einsum("bpc,cd->bpd", attended, w_out, preferred_element_type=jnp.float32)
-    return jnp.mean(projected, axis=1)
-
-
-def text_attention(texts, flat_slot):
+    return pl.pallas_call(
+        image_kernel,
+        grid=(item_count,),
+        in_specs=[
+            pl.BlockSpec(memory_space=pltpu.SMEM),
+            pl.BlockSpec((1, patch_count, model_width), lambda i: (i, 0, 0)),
+            pl.BlockSpec((1, 16 * model_width, 128), lambda i: (0, 0, 0), pipeline_mode=pl.Buffered(1)),
+        ],
+        out_specs=pl.BlockSpec((item_count, model_width), lambda i: (0, 0)),
+        out_shape=jax.ShapeDtypeStruct((item_count, model_width), F32),
+        scratch_shapes=[
+            pltpu.VMEM((model_width, 3 * half_width), BF16),
+            pltpu.VMEM((half_width, model_width), BF16),
+            pltpu.VMEM((128 * 12, 128), F32),
+            pltpu.VMEM((item_count * head_count, model_width), F32),
+        ],
+        compiler_params=pltpu.CompilerParams(vmem_limit_bytes=40 * 1024 * 1024),
+    )(flag, images, slot)
+
+def rope_tables(tokens, repeats):
+    half = HEAD_TXT // 2
+    exponents = np.arange(half).astype(np.float32) * np.float32(2.0 / HEAD_TXT)
+    inverse = np.exp(np.float32(-math.log(rope_theta)) * exponents).astype(np.float32)
+    angles = (np.arange(tokens).astype(np.float32)[:, None] * inverse[None, :]).astype(np.float32)
+    cosine = np.concatenate([np.cos(angles), np.cos(angles)], axis=1)
+    sine = np.concatenate([-np.sin(angles), np.sin(angles)], axis=1)
+    return np.tile(cosine, (repeats, 1)).astype(np.float32), np.tile(sine, (repeats, 1)).astype(np.float32)
+
+def text_kernel(flag_ref, text_ref, slot_ref, cos_ref, sin_ref, pooled_ref, w_in, w_out, wide, heads_mean):
+    item_count, token_count, model_width = text_ref.shape
+    half_width = model_width // 2
+    head_count = half_width // HEAD_TXT
+    unfold(slot_ref, 0, w_in, wide, 128)
+    unfold(slot_ref, model_width * 8, w_out, wide, 128)
+    tokens = text_ref[...].reshape(item_count * token_count, model_width).astype(F32)
+    normed = (tokens * lax.rsqrt(jnp.mean(tokens * tokens, axis=1, keepdims=True) + norm_eps)).astype(BF16)
+    residual = jnp.mean(tokens.reshape(item_count, token_count, model_width), axis=1)
+    cosine, sine = cos_ref[...], sin_ref[...]
+
+    def head_columns(head):
+        return dot_nn(normed, w_in[:, head * HEAD_TXT : (head + 1) * HEAD_TXT])
+
+    def turned(head, scale):
+        part = head_columns(head)
+        return ((part * cosine + pltpu.roll(part, HEAD_TXT // 2, 1) * sine).astype(BF16)).astype(F32) * scale
+
+    queries = [(turned(head, 1.0)).astype(BF16) for head in range(head_count)]
+    keys = turned(head_count, 1.0).astype(BF16)
+    values = head_columns(head_count + 1).astype(BF16)
+    wide_columns = head_count * token_count
+    key_ids = lax.broadcasted_iota(jnp.int32, (token_count, wide_columns), 0)
+    query_ids = lax.broadcasted_iota(jnp.int32, (token_count, wide_columns), 1) % token_count
+    allowed = key_ids <= query_ids
+    own_head = lax.broadcasted_iota(jnp.int32, (8, wide_columns), 0) == (
+        lax.broadcasted_iota(jnp.int32, (8, wide_columns), 1) // token_count
+    )
+    for item in range(item_count):
+        span = slice(item * token_count, (item + 1) * token_count)
+        asked = jnp.concatenate([query[span] for query in queries], axis=0)
+        scores = dot_nt(keys[span], asked) * (1.0 / math.sqrt(HEAD_TXT))
+        scores = jnp.where(allowed, scores, -1e30)
+        exps = jnp.exp(scores - jnp.max(scores, axis=0, keepdims=True))
+        share = (1.0 / token_count) / jnp.sum(exps, axis=0, keepdims=True)
+        share = jnp.where(own_head, share, 0.0).astype(BF16)
+        weights = dot_nt(share, exps.astype(BF16))
+        heads_mean[:, item, :] = dot_two(weights, values[span])
+    pooled = residual * flag_ref[0].astype(F32)
+    for head in range(head_count):
+        pooled = pooled + dot_two(heads_mean[head], w_out[head * HEAD_TXT : (head + 1) * HEAD_TXT, :])
+    pooled_ref[...] = pooled
+
+def text_pooled(texts, slot, flag):
     item_count, token_count, model_width = texts.shape
     half_width = model_width // 2
-    head_count = half_width // HEAD_TXT
-    inner_width = half_width + 2 * HEAD_TXT
-    qkv_size = model_width * inner_width
-    w_qkv = flat_slot[:qkv_size].reshape(model_width, inner_width)
-    w_out = flat_slot[qkv_size : qkv_size + half_width * model_width].reshape(
-        half_width, model_width
-    )
-    float_tokens = texts.astype(jnp.float32)
-    normed = (
-        float_tokens
-        * lax.rsqrt(jnp.mean(float_tokens * float_tokens, axis=-1, keepdims=True) + norm_eps)
-    ).astype(jnp.bfloat16)
-    projections = jnp.einsum("btd,de->bte", normed, w_qkv, preferred_element_type=jnp.float32)
-    positions = jnp.arange(token_count).astype(jnp.float32)
-    queries = rotate_pairs(
-        projections[..., :half_width].reshape(item_count, token_count, head_count, HEAD_TXT),
-        positions,
-    ).astype(jnp.bfloat16)
-    key_rows = rotate_pairs(
-        projections[..., half_width : half_width + HEAD_TXT].reshape(
-            item_count, token_count, 1, HEAD_TXT
-        ),
-        positions,
-    )[:, :, 0, :].astype(jnp.bfloat16)
-    value_rows = projections[..., half_width + HEAD_TXT :].astype(jnp.bfloat16)
-    scores = jnp.einsum(
-        "bqhc,bkc->bhqk", queries, key_rows, preferred_element_type=jnp.float32
-    ) / math.sqrt(HEAD_TXT)
-    causal = jnp.arange(token_count)[:, None] >= jnp.arange(token_count)[None, :]
-    scores = jnp.where(causal, scores, -1e30)
-    probabilities = softmax_rows(scores)
-    attended = jnp.einsum(
-        "bhqk,bkc->bqhc", probabilities, value_rows, preferred_element_type=jnp.float32
-    ).astype(jnp.bfloat16)
-    attended = attended.reshape(item_count, token_count, half_width)
-    projected = jnp.einsum("btc,cd->btd", attended, w_out, preferred_element_type=jnp.float32)
-    return jnp.mean(projected, axis=1)
-
+    inner = half_width + 2 * HEAD_TXT
+    cosine, sine = rope_tables(token_count, item_count)
+    vm = pl.BlockSpec(memory_space=pltpu.VMEM)
+    return pl.pallas_call(
+        text_kernel,
+        in_specs=[pl.BlockSpec(memory_space=pltpu.SMEM)] + [vm] * 4,
+        out_specs=vm,
+        out_shape=jax.ShapeDtypeStruct((item_count, model_width), F32),
+        scratch_shapes=[
+            pltpu.VMEM((model_width, inner), BF16),
+            pltpu.VMEM((half_width, model_width), BF16),
+            pltpu.VMEM((128 * 12, 128), F32),
+            pltpu.VMEM((8, item_count, HEAD_TXT), F32),
+        ],
+        compiler_params=pltpu.CompilerParams(vmem_limit_bytes=40 * 1024 * 1024),
+    )(flag, texts, slot, jnp.asarray(cosine), jnp.asarray(sine))
 
 def merge_forward(embedded, stacked):
     first_rows = embedded.shape[1]
@@ -179,7 +255,404 @@
     return jnp.where(in_first[:, None], first_term, second_term)
 
 
-def per_device(
+def first_rows_in(shard, shard_rows, first_rows):
+    return min(max(first_rows - shard * shard_rows, 0), shard_rows)
+
+
+def unit_groups(shard_count, shard_rows, first_rows, segment_count):
+    groups = []
+    for shard in range(shard_count):
+        inside = first_rows_in(shard, shard_rows, first_rows)
+        if inside < shard_rows:
+            share = (shard_rows - inside) // segment_count
+            groups.append((shard, inside, shard * shard_rows + inside - first_rows, share))
+    return groups
+
+
+def message_kernel(groups, place_ref, rows_ref, message_ref):
+    shard, segment = place_ref[0], place_ref[1]
+    row_count, width = rows_ref.shape
+    columns = message_ref.shape[1]
+    first_last = groups[0][0]
+
+    @pl.when(shard <= first_last)
+    def _():
+        wanted = lax.broadcasted_iota(jnp.int32, (width, columns), 1)
+        unit = jnp.zeros_like(wanted)
+        offset = 0
+        for _, _, base, share in groups:
+            inside = (wanted >= offset) & (wanted < offset + share)
+            unit = jnp.where(inside, wanted - offset + base + share * segment, unit)
+            offset += share
+        chosen = (lax.broadcasted_iota(jnp.int32, (width, columns), 0) == unit).astype(F32).astype(BF16)
+        message_ref[...] = dot_nn(rows_ref[...], chosen).astype(BF16)
+
+    for group_shard, inside, _, share in groups:
+
+        @pl.when(shard == group_shard)
+        def _(inside=inside, share=share):
+            start = pl.multiple_of(inside + share * segment, 16)
+            for block in range(width // columns):
+                message_ref[inside + block * share : inside + (block + 1) * share, :] = rows_ref[
+                    pl.ds(start, share), block * columns : (block + 1) * columns
+                ]
+
+
+def weight_message(uniting_weights, place, groups, columns):
+    vm = pl.BlockSpec(memory_space=pltpu.VMEM)
+    return pl.pallas_call(
+        functools.partial(message_kernel, groups),
+        in_specs=[pl.BlockSpec(memory_space=pltpu.SMEM), vm],
+        out_specs=vm,
+        out_shape=jax.ShapeDtypeStruct((uniting_weights.shape[0], columns), BF16),
+    )(place, uniting_weights)
+
+
+def forward_kernel(
+    groups,
+    first_rows,
+    place_ref,
+    embedded_ref,
+    own_ref,
+    *refs,
+):
+    shard_count = (len(refs) - 6)
+    piece_refs = refs[:shard_count]
+    blocks_ref, hidden_ref, active_ref, second_ref, partial_ref, kept = refs[shard_count:]
+    shard = place_ref[0]
+    source_count, source_items, width = embedded_ref.shape
+    items = source_count * source_items
+    shard_rows, columns = piece_refs[0].shape
+    embedded = embedded_ref[...].astype(F32).reshape(items, width)
+    normed = embedded * lax.rsqrt(jnp.mean(embedded * embedded, axis=1, keepdims=True) + norm_eps)
+    normed = normed.astype(BF16)
+    for block in range(shard_count):
+        inside = first_rows_in(block, shard_rows, first_rows)
+        start = block * shard_rows
+        if inside == shard_rows:
+            blocks_ref[block] = normed[:, start : start + shard_rows]
+        elif inside > 0:
+            blocks_ref[block] = jnp.concatenate(
+                [normed[:, start : start + inside], jnp.zeros((items, shard_rows - inside), BF16)], axis=1
+            )
+        else:
+            blocks_ref[block] = jnp.zeros((items, shard_rows), BF16)
+    hidden = jnp.zeros((items, columns), F32)
+    first_group = groups[0][0]
+    for turn in range(shard_count):
+        source = lax.rem(shard - turn + shard_count, shard_count)
+        hidden = hidden + dot_nn(blocks_ref[source], piece_refs[turn][...])
+
+        @pl.when(source >= first_group)
+        def _(turn=turn, source=source):
+            kept[source - first_group] = piece_refs[turn][...]
+
+    hidden_ref[...] = hidden
+    active = gelu_value(hidden).astype(BF16)
+    active_ref[...] = active
+    offset = 0
+    for index, (_, inside, _, share) in enumerate(groups):
+        for block in range(partial_ref.shape[1] // columns):
+            second_ref[offset : offset + share, block * columns : (block + 1) * columns] = kept[
+                index, inside + block * share : inside + (block + 1) * share, :
+            ]
+        offset += share
+    partial_ref[...] = dot_nn(dot_nn(own_ref[...], active).astype(BF16), second_ref[...])
+
+
+def merge_quarter(embedded_all, pieces, own, place, groups, first_rows, width):
+    shard_count, shard_rows, columns = len(pieces), pieces[0].shape[0], pieces[0].shape[1]
+    items = embedded_all.shape[0] * embedded_all.shape[1]
+    vm = pl.BlockSpec(memory_space=pltpu.VMEM)
+    return pl.pallas_call(
+        functools.partial(forward_kernel, groups, first_rows),
+        in_specs=[pl.BlockSpec(memory_space=pltpu.SMEM)] + [vm] * (2 + shard_count),
+        out_specs=[vm] * 5,
+        out_shape=[
+            jax.ShapeDtypeStruct((shard_count, items, shard_rows), BF16),
+            jax.ShapeDtypeStruct((items, columns), F32),
+            jax.ShapeDtypeStruct((items, columns), BF16),
+            jax.ShapeDtypeStruct((columns, width), BF16),
+            jax.ShapeDtypeStruct((own.shape[0], width), F32),
+        ],
+        scratch_shapes=[pltpu.VMEM((len(groups), shard_rows, columns), BF16)],
+        compiler_params=pltpu.CompilerParams(vmem_limit_bytes=32 * 1024 * 1024),
+    )(place, embedded_all, own, *pieces)
+
+
+def split(value):
+    high = value.astype(BF16)
+    return high, (value - high.astype(F32)).astype(BF16)
+
+
+def exact_nt(value, high, low):
+    first, second = split(value)
+    rows = value.shape[0]
+    both = dot_nt(jnp.concatenate([first, second], axis=0), high)
+    return both[:rows] + both[rows:] + dot_nt(first, low)
+
+
+def exact_nn(value, high, low):
+    first, second = split(value)
+    rows = value.shape[0]
+    both = dot_nn(jnp.concatenate([first, second], axis=0), high)
+    return both[:rows] + both[rows:] + dot_nn(first, low)
+
+
+def dot_tn(a, b):
+    return lax.dot_general(a, b, (((0,), (0,)), ((), ())), preferred_element_type=F32)
+
+
+def exact_tn(a, b):
+    a_high, a_low = split(a)
+    b_high, b_low = split(b)
+    return dot_tn(
+        jnp.concatenate([a_high, a_low, a_high], axis=0), jnp.concatenate([b_high, b_high, b_low], axis=0)
+    )
+
+
+def square_sums(value):
+    high, low = split(value * value)
+    ones = jnp.ones((8, value.shape[1]), BF16)
+    return (dot_nt(ones, high) + dot_nt(ones, low))[:1]
+
+
+def quantizer_kernel(loss_scale, merged_ref, book_ref, bank_ref, count_ref, book_grad_ref, merged_grad_ref, loss_ref, highs, lows):
+    width = merged_ref.shape[1]
+    levels = book_ref.shape[0]
+    inverse_tau = 2.0 / math.sqrt(width)
+    inverse_temp = 1.0 / (width * contrast_temp)
+    merged = merged_ref[...].astype(BF16).astype(F32)
+    merged_scale = lax.rsqrt(jnp.mean(merged * merged, axis=1, keepdims=True) + norm_eps)
+    residuals = [merged * merged_scale]
+    shares, chosen_rows = [], []
+    for level in range(levels):
+        codes = book_ref[level]
+        high, low = split(codes)
+        highs[level] = high
+        lows[level] = low
+        logits = (2.0 * exact_nt(residuals[level], high, low) - square_sums(codes)) * inverse_tau
+        exps = jnp.exp(logits - jnp.max(logits, axis=1, keepdims=True))
+        share = exps / jnp.sum(exps, axis=1, keepdims=True)
+        chosen = exact_nn(share, high, low)
+        shares.append(share)
+        chosen_rows.append(chosen)
+        residuals.append(residuals[level] - chosen)
+    last = residuals[levels]
+    quantized = chosen_rows[0]
+    for chosen in chosen_rows[1:]:
+        quantized = quantized + chosen
+    anchor_scale = lax.rsqrt(jnp.mean(quantized * quantized, axis=1, keepdims=True) + norm_eps)
+    anchor = quantized * anchor_scale
+    own = jnp.sum(anchor * residuals[0], axis=1, keepdims=True) * inverse_temp
+    bank = bank_ref[...]
+    bank_wide = bank.astype(F32)
+    bank_scale = lax.rsqrt(square_sums(bank_wide) * (1.0 / width) + norm_eps)
+    anchor_parts = jnp.concatenate(split(anchor), axis=0)
+    rows = anchor.shape[0]
+    both = dot_nt(anchor_parts, bank)
+    similar = (both[:rows] + both[rows:]) * bank_scale * inverse_temp
+    counts = count_ref[...]
+    named = counts > 0.0
+    top = jnp.maximum(jnp.max(jnp.where(named, similar, own), axis=1, keepdims=True), own)
+    bank_exps = jnp.where(named, jnp.exp(jnp.where(named, similar, top) - top), 0.0) * counts
+    own_exp = jnp.exp(own - top)
+    total = jnp.sum(bank_exps, axis=1, keepdims=True) + own_exp
+    item_losses = top + jnp.log(total) - own + jnp.mean(last * last, axis=1, keepdims=True)
+    loss_ref[...] = jnp.broadcast_to(jnp.sum(item_losses, axis=0, keepdims=True) * loss_scale, loss_ref.shape)
+
+    bank_weight = bank_exps / total * (loss_scale * inverse_temp)
+    own_weight = (own_exp / total - 1.0) * (loss_scale * inverse_temp)
+    weight_parts = jnp.concatenate(split(bank_weight * bank_scale), axis=0)
+    both = dot_nn(weight_parts, bank)
+    anchor_grad = both[:rows] + both[rows:] + own_weight * residuals[0]
+    unit_grad = own_weight * anchor
+    quantized_grad = anchor_scale * (anchor_grad - anchor * jnp.mean(anchor * anchor_grad, axis=1, keepdims=True))
+    residual_grad = last * (2.0 * loss_scale / width)
+    ones = jnp.ones((rows, 128), F32)
+    for level in reversed(range(levels)):
+        high, low = highs[level], lows[level]
+        chosen_grad = quantized_grad - residual_grad
+        share_grad = exact_nt(chosen_grad, high, low)
+        share = shares[level]
+        logit_grad = share * (share_grad - jnp.sum(share * share_grad, axis=1, keepdims=True)) * (2.0 * inverse_tau)
+        book_part = exact_tn(
+            jnp.concatenate([share, logit_grad], axis=0), jnp.concatenate([chosen_grad, residuals[level]], axis=0)
+        )
+        totals = exact_tn(logit_grad, ones)
+        for block in range(width // 128):
+            span = slice(block * 128, (block + 1) * 128)
+            book_grad_ref[level, :, span] = book_part[:, span] - totals * book_ref[level, :, span]
+        residual_grad = residual_grad + exact_nn(logit_grad, high, low)
+    unit_grad = unit_grad + residual_grad
+    unit = residuals[0]
+    merged_grad = merged_scale * (unit_grad - unit * jnp.mean(unit * unit_grad, axis=1, keepdims=True))
+    merged_grad_ref[...] = merged_grad.astype(BF16)
+
+
+def quantizer(merged, books, bank, counts, loss_scale):
+    vm = pl.BlockSpec(memory_space=pltpu.VMEM)
+    return pl.pallas_call(
+        functools.partial(quantizer_kernel, loss_scale),
+        in_specs=[vm] * 4,
+        out_specs=[vm] * 3,
+        out_shape=[
+            jax.ShapeDtypeStruct(books.shape, F32),
+            jax.ShapeDtypeStruct(merged.shape, BF16),
+            jax.ShapeDtypeStruct((8, 128), F32),
+        ],
+        scratch_shapes=[pltpu.VMEM(books.shape, BF16), pltpu.VMEM(books.shape, BF16)],
+        compiler_params=pltpu.CompilerParams(vmem_limit_bytes=32 * 1024 * 1024),
+    )(merged, books, bank, counts)
+
+
+def backward_kernel(gathered_ref, order_ref, hidden_ref, active_ref, second_ref, out_grad_ref, sent_ref):
+    owners, places, width = gathered_ref.shape
+    columns = hidden_ref.shape[1]
+    gathered = gathered_ref[...].astype(F32).reshape(owners * places, width).astype(BF16)
+    out_grad = dot_tn(order_ref[...], gathered).astype(BF16)
+    out_grad_ref[...] = out_grad
+    hidden_grad = dot_nt(out_grad, second_ref[...]) * gelu_slope(hidden_ref[...])
+    sent_ref[:, :columns] = hidden_grad.astype(BF16)
+    sent_ref[:, columns:] = active_ref[...]
+
+
+def backward_quarter(gathered, order, hidden, active, second):
+    items, columns = hidden.shape
+    vm = pl.BlockSpec(memory_space=pltpu.VMEM)
+    return pl.pallas_call(
+        backward_kernel,
+        in_specs=[vm] * 5,
+        out_specs=[vm] * 2,
+        out_shape=[
+            jax.ShapeDtypeStruct((items, gathered.shape[2]), BF16),
+            jax.ShapeDtypeStruct((items, 2 * columns), BF16),
+        ],
+        compiler_params=pltpu.CompilerParams(vmem_limit_bytes=32 * 1024 * 1024),
+    )(gathered, order, hidden, active, second)
+
+
+def weight_grad_kernel(groups, place_ref, block_ref, out_grad_ref, received_ref, grad_ref, hidden_grad, active):
+    shard = place_ref[0]
+    segment_count, items, doubled = received_ref.shape
+    columns = doubled // 2
+    shard_rows = block_ref.shape[1]
+    for segment in range(segment_count):
+        offset = 0
+        for _, _, base, share in groups:
+            spot = base + share * segment
+            hidden_grad[:, spot : spot + share] = received_ref[segment, :, offset : offset + share]
+            offset += share
+    grad_ref[...] = dot_tn(block_ref[...], hidden_grad[...])
+    for group_shard, inside, base, _ in groups:
+
+        @pl.when(shard == group_shard)
+        def _(inside=inside, base=base):
+            for segment in range(segment_count):
+                offset = columns
+                for _, _, other, share in groups:
+                    spot = other + share * segment
+                    active[:, spot : spot + share] = received_ref[segment, :, offset : offset + share]
+                    offset += share
+            wanted = active[:, base : base + shard_rows - inside]
+            grad_ref[inside:, :] = dot_tn(wanted, out_grad_ref[...])
+
+
+def weight_grad(place, block, out_grad, received, groups):
+    items, shard_rows = block.shape
+    width = out_grad.shape[1]
+    vm = pl.BlockSpec(memory_space=pltpu.VMEM)
+    return pl.pallas_call(
+        functools.partial(weight_grad_kernel, groups),
+        in_specs=[pl.BlockSpec(memory_space=pltpu.SMEM)] + [vm] * 3,
+        out_specs=vm,
+        out_shape=jax.ShapeDtypeStruct((shard_rows, width), F32),
+        scratch_shapes=[pltpu.VMEM((items, width), BF16), pltpu.VMEM((items, width), BF16)],
+        compiler_params=pltpu.CompilerParams(vmem_limit_bytes=32 * 1024 * 1024),
+    )(place, block, out_grad, received)
+
+
+def spread(rows, axis_name, count):
+    return lax.all_to_all(
+        jnp.broadcast_to(rows[None], (count,) + rows.shape), axis_name, 0, 0, tiled=True
+    )
+
+
+def per_device_quarters(
+    images, texts, section_weights, uniting_weights, codebooks, neg_bank, item_cats, cat_slot, neg_index
+):
+    segment_index = lax.axis_index("segment")
+    segment_count = lax.axis_size("segment")
+    dp_index = lax.axis_index("dp")
+    dp_count = lax.axis_size("dp")
+    item_count, _, image_width = images.shape
+    text_width = texts.shape[2]
+    first_rows = image_width + text_width
+    shard_rows, width = uniting_weights.shape
+    columns = width // segment_count
+    groups = unit_groups(dp_count, shard_rows, first_rows, segment_count)
+    place = jnp.stack([dp_index, segment_index]).astype(jnp.int32)
+    message = weight_message(uniting_weights, place, groups, columns)
+    pieces = [message] + [
+        lax.ppermute(message, "dp", [(i, (i + turn) % dp_count) for i in range(dp_count)])
+        for turn in range(1, dp_count)
+    ]
+    flag = (1 - segment_index % 2).astype(jnp.int32).reshape(1)
+    pooled = pooled_features(images, texts, section_weights, segment_index, flag)
+    pooled = pooled + lax.ppermute(pooled, "segment", [(i, i ^ 1) for i in range(segment_count)])
+    mine = pooled.astype(BF16)
+    other = lax.ppermute(mine, "segment", [(i, i ^ 2) for i in range(segment_count)])
+    is_image = segment_index < 2
+    embedded = jnp.concatenate(
+        [jnp.where(is_image, mine, other)[:, :image_width], jnp.where(is_image, other, mine)], axis=1
+    )
+    embedded_all = spread(embedded, "dp", dp_count)
+
+    pair = item_cats.shape[1] // dp_count
+    cats = item_cats.reshape(segment_count, dp_count, pair).transpose(1, 0, 2).reshape(-1)
+    items = cats.shape[0]
+    slots = jnp.sum(
+        jnp.where(cats[:, None] == jnp.arange(cat_slot.shape[0])[None, :], cat_slot[None, :], 0), axis=1
+    )
+    ids = jnp.arange(items)
+    rank = jnp.sum(jnp.where((slots[None, :] == slots[:, None]) & (ids[None, :] < ids[:, None]), 1, 0), axis=1)
+    owned = segment_count * CAP
+    order = (ids[:, None] == (slots * owned + rank)[None, :]).astype(BF16)
+    own = lax.dynamic_slice_in_dim(order, dp_index * owned, owned, 0)
+    negatives = neg_index.reshape(segment_count, dp_count, pair, -1).transpose(1, 0, 2, 3).reshape(items, -1)
+    own_negatives = jnp.dot(own.astype(F32), negatives.astype(F32), precision=highest)
+    bank = neg_bank[0]
+    bank_ids = jnp.arange(bank.shape[0]).astype(F32)
+    counts = jnp.sum((own_negatives[:, :, None] == bank_ids[None, None, :]).astype(F32), axis=1)
+
+    blocks, hidden, active, second, partial = merge_quarter(
+        embedded_all, pieces, own, place, groups, first_rows, width
+    )
+    partial = partial + lax.ppermute(partial, "segment", [(i, i ^ 1) for i in range(segment_count)])
+    merged = partial + lax.ppermute(partial, "segment", [(i, i ^ 2) for i in range(segment_count)])
+    book_grad, merged_grad, loss = quantizer(merged, codebooks[0], bank, counts, 1.0 / math.sqrt(items))
+    gathered = spread(merged_grad, "dp", dp_count)
+    out_grad, sent = backward_quarter(gathered, order, hidden, active, second)
+    received = lax.all_gather(sent, "segment", axis=0)
+    block = lax.dynamic_index_in_dim(blocks, dp_index, 0, keepdims=False)
+    uniting_grad = weight_grad(place, block, out_grad, received, groups)
+    return (uniting_grad, book_grad[None], loss[0, :1])
+
+
+def pooled_features(images, texts, section_weights, segment_index, flag):
+    image_width, text_width = images.shape[2], texts.shape[2]
+
+    def image_branch(operands):
+        pooled = image_pooled(operands[0], operands[2], flag)
+        return jnp.pad(pooled, ((0, 0), (0, text_width - image_width)))
+
+    def text_branch(operands):
+        return text_pooled(operands[1], operands[2], flag)
+
+    return lax.cond(segment_index < 2, image_branch, text_branch, (images, texts, section_weights))
+
+
+def per_device_gathered(
     images,
     texts,
     section_weights,
@@ -196,28 +669,14 @@
     dp_count = lax.axis_size("dp")
     group_index = segment_index % 2
     item_count = images.shape[0]
-    flat_slot = section_weights.reshape(-1)
-    residual_flag = jnp.where(group_index == 0, 1.0, 0.0).astype(jnp.float32)
-
-    def image_branch(operands):
-        image_rows, text_rows, slot_rows = operands
-        pooled = image_attention(image_rows, slot_rows) + residual_flag * jnp.mean(
-            image_rows.astype(jnp.float32), axis=1
-        )
-        return jnp.concatenate(
-            [pooled, jnp.zeros((item_count, text_rows.shape[2]), jnp.float32)], axis=1
-        )
-
-    def text_branch(operands):
-        image_rows, text_rows, slot_rows = operands
-        pooled = text_attention(text_rows, slot_rows) + residual_flag * jnp.mean(
-            text_rows.astype(jnp.float32), axis=1
-        )
-        return jnp.concatenate(
-            [jnp.zeros((item_count, image_rows.shape[2]), jnp.float32), pooled], axis=1
-        )
-
-    packed = lax.cond(segment_index < 2, image_branch, text_branch, (images, texts, flat_slot))
+
+    flag = (1 - group_index).astype(jnp.int32).reshape(1)
+    pooled = pooled_features(images, texts, section_weights, segment_index, flag)
+    image_width = images.shape[2]
+    is_image = segment_index < 2
+    packed = jnp.concatenate(
+        [jnp.where(is_image, pooled[:, :image_width], 0.0), jnp.where(is_image, 0.0, pooled)], axis=1
+    )
     embedded = lax.psum_scatter(packed, "segment", scatter_dimension=0, tiled=True).astype(
         jnp.bfloat16
     )
@@ -289,6 +748,20 @@
     return (uniting_grad, book_total, loss_owner.reshape(1))
 
 
+def per_device(*operands):
+    images, texts, _, uniting_weights = operands[:4]
+    segment_count, dp_count = lax.axis_size("segment"), lax.axis_size("dp")
+    shard_rows = uniting_weights.shape[0]
+    first_rows = images.shape[2] + texts.shape[2]
+    groups = unit_groups(dp_count, shard_rows, first_rows, segment_count)
+    whole_tiles = all(
+        (shard_rows - inside) % (16 * segment_count) == 0 and inside % 16 == 0 for _, inside, _, _ in groups
+    )
+    if whole_tiles:
+        return per_device_quarters(*operands)
+    return per_device_gathered(*operands)
+
+
 def solution(mesh):
     placed = (
         P("dp", None, None),

time: 361 us -> 109 us (0.30); the launches traced: 355 us -> 108 us
  blocking collectives: 142 us -> 5.79 us
  matrix products: 59.8 us -> 0.13 us
  waiting for transfers between devices: 75.3 us -> 28.3 us
  Pallas kernels: 0 us -> 35.6 us
  starting transfers between devices: 0.08 us -> 24.1 us
  other arithmetic: 25.9 us -> 1.9 us
  local copies, waits for them, and re-layouts: 34.8 us -> 11.5 us
  between operations: 16.2 us -> 0.78 us
    all_gather x4 -> x1, blocking collectives: 123 us -> 5.79 us  [per_device_quarters(): received = lax.all_gather(sent, 'segment', axis=0)]
    psum x1 -> x0, waiting for transfers between devices: 74.6 us -> none  [per_device(): uniting_grad = lax.psum(segment_grad, 'segment')]
    dot_general x19 -> x1, matrix products: 49.2 us -> 0.13 us  [per_device_quarters(): jnp.dot(own.astype(F32), negatives.astype(F32), precision=highest)]
    pallas_call x0 -> x6, Pallas kernels: none -> 35.6 us  [the longest x1 21.1 us: image_pooled(): pl.pallas_call(image_kernel, grid=(item_count,), in_specs=[pl.BlockSpec(m...]
    slice x9 -> x1, local copies, waits for them, and re-layouts: 23.7 us -> 0.51 us  [per_device_quarters(): return (uniting_grad, book_grad[None], loss[0, :1])]
    ppermute x0 -> x11, waiting for transfers between devices: none -> 22.3 us  [the longest x7 13.3 us: per_device_quarters(): lax.ppermute(message, 'dp', [(i, (i + turn) % dp_count) for i in range(dp...]
    ppermute x0 -> x11, starting transfers between devices: none -> 13.3 us  [the longest x7 12.9 us: per_device_quarters(): lax.ppermute(message, 'dp', [(i, (i + turn) % dp_count) for i in range(dp...]
    unnamed x1 -> x0, blocking collectives: 12.1 us -> none
  transfers between devices with their start and end apart: 2 -> 13, of which waited for: 1 -> 6; matrix products, arithmetic and copies ran while one was open for 21% -> 4% of each run, Pallas kernels for 0% -> 19%
where the time goes in v1:
time: 109 us; the launch traced here: 108 us
  Pallas kernels  35.6 us (33%)
  waiting for transfers between devices  28.3 us (26%)
  starting transfers between devices  24.1 us (22%)
  local copies, waits for them, and re-layouts  11.5 us (11%)
  blocking collectives  5.79 us (5%)
  other arithmetic  1.9 us (2%)
    pallas_call x1, Pallas kernels, image_pooled(): pl.pallas_call(image_kernel, grid=(item_count,), in_specs=[pl.BlockSpec(m...  21.1 us
    ppermute x7, waiting for transfers between devices, per_device_quarters(): lax.ppermute(message, 'dp', [(i, (i + turn) % dp_count) for i in range(dp...  13.3 us
    ppermute x7, starting transfers between devices, per_device_quarters(): lax.ppermute(message, 'dp', [(i, (i + turn) % dp_count) for i in range(dp...  12.9 us
    all_to_all x2, starting transfers between devices, spread(): lax.all_to_all(jnp.broadcast_to(rows[None], (count,) + rows.shape), axis_...  10.8 us
    unnamed x31, local copies, waits for them, and re-layouts  8.5 us
    pallas_call x1, Pallas kernels, quantizer(): pl.pallas_call(functools.partial(quantizer_kernel, loss_scale), in_specs=...  6.62 us
    all_to_all x2, waiting for transfers between devices, spread(): lax.all_to_all(jnp.broadcast_to(rows[None], (count,) + rows.shape), axis_...  5.99 us
    all_gather x1, blocking collectives, per_device_quarters(): received = lax.all_gather(sent, 'segment', axis=0)  5.79 us
  transfers between devices with their start and end apart: 13, of which 6 were waited for; matrix products, arithmetic and copies ran while one was open for 4% of the time, Pallas kernels for 19%

profile of v1, /device:TPU:0, one launch (start us, length us, event | category | flops | bytes accessed | tf_op | source)
XLA Modules:
  0.0 108.1 jit_solution(10606876622829483604)
XLA Ops:
  1.2 2.3 %shard_map.137.refs_0_ = bf16[448,256]{1,0:T(8,128)(2,1)} custom-call(s32[2]{0:T(128)} %pad_add_fusion.place_ref, bf16[448,1024]{1,0:T(8,128)(2,1)} %rows_ref.1), custom_call_target="tpu_custom_call" | custom-call | tf_op jit(solution)/shard_map/pallas_call | solution.py:303
  3.6 5.6 %collective-permute-start.8 = (bf16[448,256]{1,0:T(8,128)(2,1)}, bf16[448,256]{1,0:T(8,128)(2,1)S(1)}, u32[]{:S(2)}, u32[]{:S(2)}) collective-permute-start(bf16[448,256]{1,0:T(8,128)(2,1)} %shard_map.137.refs_0_), channel_id=1, source_target_pairs={{0,7},{1,0},{2,1},{3,2},{4,3},{5,4},{6,5},{7,6},{8,15},{9,8},{10,9... | collective-permute-start | bytes 688136 | tf_op jit(solution)/shard_map/ppermute | solution.py:597
  9.2 0.8 collective-permute-start.7
  10.0 2.6 %collective-permute-start.5 = (bf16[448,256]{1,0:T(8,128)(2,1)}, bf16[448,256]{1,0:T(8,128)(2,1)}, u32[]{:S(2)}, u32[]{:S(2)}) collective-permute-start(bf16[448,256]{1,0:T(8,128)(2,1)} %shard_map.137.refs_0_), channel_id=1, source_target_pairs={{0,4},{1,5},{2,6},{3,7},{4,0},{5,1},{6,2},{7,3},{8,12},{9,13},{10,... | collective-permute-start | bytes 688136 | tf_op jit(solution)/shard_map/ppermute | solution.py:597
  12.6 21.1 %conditional.1 = (f32[8,1536]{1,0:T(8,128)S(1)}) conditional(s32[]{:T(128)} %convert_element_type.34, (s32[1]{0:T(128)}, bf16[8,64,1536]{2,1,0:T(8,128)(2,1)}, bf16[1,21504,128]{2,1,0:T(8,128)(2,1)}) %tuple.20, (s32[1]{0:T(128)}, bf16[8,256,1024]{2,1,0:T(8,128)(2,1)}, bf16[1,21504,128]{2,1,0:T(8,128)(2,1)}) %tuple.15), branch_computations={%region_0.1_spmd.clone, %region_1.2_spmd} | conditional | bytes 2097216 | solution.py:652
  12.6 21.1 %branch_1_fun.1 = f32[8,1024]{1,0:T(8,128)S(1)} custom-call(s32[1]{0:T(128)} %get-tuple-element.24.flag_ref, bf16[8,256,1024]{2,1,0:T(8,128)(2,1)} %get-tuple-element.57.image_ref, bf16[1,21504,128]{2,1,0:T(8,128)(2,1)} %get-tuple-element.26.slot_ref), custom_call_target="tpu_custom_call" | custom-call | tf_op jit(solution)/shard_map/cond/branch_1_fun/pallas_call | solution.py:109
  34.3 0.8 collective-permute-done
  35.3 3.6 %collective-permute-done.1 = bf16[8,1536]{1,0:T(8,128)(2,1)S(1)} collective-permute-done((bf16[8,1536]{1,0:T(8,128)(2,1)S(1)}, bf16[8,1536]{1,0:T(8,128)(2,1)S(1)}, u32[]{:S(2)}, u32[]{:S(2)}) %collective-permute-start.1) | collective-permute-done | bytes 24608 | tf_op jit(solution)/shard_map/ppermute | solution.py:604
  39.3 0.7 broadcast_in_dim.26
  40.0 5.7 %all-to-all-start = ((bf16[8,8,2560]{2,1,0:T(8,128)(2,1)}), bf16[8,8,2560]{2,1,0:T(8,128)(2,1)S(1)}, u32[]{:S(2)}, u32[]{:S(2)}) async-start(bf16[8,8,2560]{2,1,0:T(8,128)(2,1)} %broadcast_in_dim.26), calls=%async_computation | async-start | bytes 655360 | tf_op jit(solution)/shard_map/all_to_all | solution.py:576
  45.8 2.1 %collective-permute-start.3 = (bf16[448,256]{1,0:T(8,128)(2,1)S(1)}, bf16[448,256]{1,0:T(8,128)(2,1)S(1)}, u32[]{:S(2)}, u32[]{:S(2)}) collective-permute-start(bf16[448,256]{1,0:T(8,128)(2,1)S(1)} %copy-done.1), channel_id=1, source_target_pairs={{0,2},{1,3},{2,4},{3,5},{4,6},{5,7},{6,0},{7,1},{8,10},{9,11},{10,... | collective-permute-start | bytes 688136 | tf_op jit(solution)/shard_map/ppermute | solution.py:597
  47.9 0.7 copy-done.5
  48.6 1.5 %collective-permute-start.2 = (bf16[448,256]{1,0:T(8,128)(2,1)S(1)}, bf16[448,256]{1,0:T(8,128)(2,1)S(1)}, u32[]{:S(2)}, u32[]{:S(2)}) collective-permute-start(bf16[448,256]{1,0:T(8,128)(2,1)S(1)} %copy-done.1), channel_id=1, source_target_pairs={{0,1},{1,2},{2,3},{3,4},{4,5},{5,6},{6,7},{7,0},{8,9},{9,10},{10,1... | collective-permute-start | bytes 688136 | tf_op jit(solution)/shard_map/ppermute | solution.py:597
  50.0 0.8 convert_element_type.37
  50.9 0.7 copy-done.7
  51.7 13.3 %collective-permute-done.4.refs_3_ = bf16[448,256]{1,0:T(8,128)(2,1)} collective-permute-done((bf16[448,256]{1,0:T(8,128)(2,1)S(1)}, bf16[448,256]{1,0:T(8,128)(2,1)}, u32[]{:S(2)}, u32[]{:S(2)}) %collective-permute-start.4) | collective-permute-done | bytes 229408 | tf_op jit(solution)/shard_map/ppermute | solution.py:597
  64.9 0.7 copy-done.9
  66.3 0.9 copy-done.6
  67.2 0.9 copy-done.8
  68.2 0.9 copy-done.10
  69.1 0.9 copy-done.12
  70.1 2.9 %shard_map.138 = (bf16[8,64,448]{2,1,0:T(8,128)(2,1)S(1)}, f32[64,256]{1,0:T(8,128)S(1)}, bf16[64,256]{1,0:T(8,128)(2,1)S(1)}, bf16[256,1024]{1,0:T(8,128)(2,1)S(1)}, f32[8,1024]{1,0:T(8,128)S(1)}) custom-call(s32[2]{0:T(128)S(1)} %copy-done.14, bf16[8,8,2560]{2,1,0:T(8,128)(2,1)S(1)} %all-to-all-done.embedded_ref, ...), custom_call_target="tpu_custom_call" | custom-call | tf_op jit(solution)/shard_map/pallas_call | solution.py:367
  73.0 0.8 copy-done.13
  73.8 1.2 %collective-permute-done.9 = f32[8,1024]{1,0:T(8,128)S(1)} collective-permute-done((f32[8,1024]{1,0:T(8,128)S(1)}, f32[8,1024]{1,0:T(8,128)S(1)}, u32[]{:S(2)}, u32[]{:S(2)}) %collective-permute-start.9) | collective-permute-done | bytes 32800 | tf_op jit(solution)/shard_map/ppermute | solution.py:631
  75.5 3.4 %collective-permute-done.10 = f32[8,1024]{1,0:T(8,128)S(1)} collective-permute-done((f32[8,1024]{1,0:T(8,128)S(1)}, f32[8,1024]{1,0:T(8,128)S(1)}, u32[]{:S(2)}, u32[]{:S(2)}) %collective-permute-start.10) | collective-permute-done | bytes 32800 | tf_op jit(solution)/shard_map/ppermute | solution.py:632
  78.9 1.0 copy-done.2
  80.0 6.6 %shard_map.139 = (f32[2,256,1024]{2,1,0:T(8,128)}, bf16[8,1024]{1,0:T(8,128)(2,1)S(1)}, f32[8,128]{1,0:T(8,128)S(1)}) custom-call(f32[8,1024]{1,0:T(8,128)S(1)} %add.35.merged_ref, f32[2,256,1024]{2,1,0:T(8,128)S(1)} %bitcast.18, bf16[256,1024]{1,0:T(8,128)(2,1)S(1)} %bitcast.20, f32[8,256]{1,0:T(8,128)S(1)} %convert_reduce_fusion.count_ref), custom_call_target="tpu_custom_call" | custom-call | tf_op jit(solution)/shard_map/pallas_call | solution.py:495
  87.2 5.0 %all-to-all-start.1 = ((bf16[8,8,1024]{2,1,0:T(8,128)(2,1)}), bf16[8,8,1024]{2,1,0:T(8,128)(2,1)S(1)}, u32[]{:S(2)}, u32[]{:S(2)}) async-start(bf16[8,8,1024]{2,1,0:T(8,128)(2,1)} %broadcast_in_dim.50), calls=%async_computation.1 | async-start | bytes 262144 | tf_op jit(solution)/shard_map/all_to_all | solution.py:576
  92.3 0.8 dynamic-slice_bitcast_fusion.block_ref
  93.6 6.0 %all-to-all-done.1.gathered_ref = bf16[8,8,1024]{2,1,0:T(8,128)(2,1)S(1)} async-done(((bf16[8,8,1024]{2,1,0:T(8,128)(2,1)}), bf16[8,8,1024]{2,1,0:T(8,128)(2,1)S(1)}, u32[]{:S(2)}, u32[]{:S(2)}) %all-to-all-start.1) | async-done | bytes 131104 | tf_op jit(solution)/shard_map/all_to_all | solution.py:576
  100.0 5.8 %all-gather = bf16[256,512]{1,0:T(8,128)(2,1)S(1)} all-gather(bf16[64,512]{1,0:T(8,128)(2,1)S(1)} %get-tuple-element.47), channel_id=2, replica_groups=mesh['segment'=4,'dp'=8] {'segment'}, dimensions={0}, use_global_device_ids=true | all-gather | bytes 327680 | tf_op jit(solution)/shard_map/all_gather | solution.py:636
  105.8 2.3 %shard_map.141 = f32[448,1024]{1,0:T(8,128)} custom-call(s32[2]{0:T(128)S(1)} %copy-done.14, bf16[64,448]{1,0:T(8,128)(2,1)S(1)} %dynamic-slice_bitcast_fusion.block_ref, bf16[64,1024]{1,0:T(8,128)(2,1)S(1)} %get-tuple-element.46.out_grad_ref, bf16[4,64,512]{2,1,0:T(8,128)(2,1)S(1)} %bitcast.19), custom_call_target="tpu_custom_call" | custom-call | tf_op jit(solution)/shard_map/pallas_call | solution.py:565
  (57 shorter events, 4.7 us)
Async XLA Ops:
  1.2 32.6 %copy-start.15 = (s32[4,16,1]{1,2,0:T(1,128)S(1)}, s32[4,16,1]{1,2,0:T(1,128)}, u32[]{:S(2)}) copy-start(s32[4,16,1]{1,2,0:T(1,128)} %param.19) | copy-start | bytes 772
  1.2 32.9 %copy-start.16 = (s32[8]{0:T(128)S(1)}, s32[8]{0:T(128)}, u32[]{:S(2)}) copy-start(s32[8]{0:T(128)} %param.20) | copy-start | bytes 100
  1.2 65.1 %copy-start.14 = (s32[2]{0:T(128)S(1)}, s32[2]{0:T(128)}, u32[]{:S(2)}) copy-start(s32[2]{0:T(128)} %pad_add_fusion.place_ref) | copy-start | bytes 28
  3.6 42.2 %collective-permute-start.8 = (bf16[448,256]{1,0:T(8,128)(2,1)}, bf16[448,256]{1,0:T(8,128)(2,1)S(1)}, u32[]{:S(2)}, u32[]{:S(2)}) collective-permute-start(bf16[448,256]{1,0:T(8,128)(2,1)} %shard_map.137.refs_0_), channel_id=1, source_target_pairs={{0,7},{1,0},{2,1},{3,2},{4,3},{5,4},{6,5},{7,6},{8,15},{9,8},{10,9... | collective-permute-start | bytes 688136 | tf_op jit(solution)/shard_map/ppermute | solution.py:597
  9.2 38.7 %collective-permute-start.7 = (bf16[448,256]{1,0:T(8,128)(2,1)}, bf16[448,256]{1,0:T(8,128)(2,1)S(1)}, u32[]{:S(2)}, u32[]{:S(2)}) collective-permute-start(bf16[448,256]{1,0:T(8,128)(2,1)} %shard_map.137.refs_0_), channel_id=1, source_target_pairs={{0,6},{1,7},{2,0},{3,1},{4,2},{5,3},{6,4},{7,5},{8,14},{9,15},{10,... | collective-permute-start | bytes 688136 | tf_op jit(solution)/shard_map/ppermute | solution.py:597
  10.0 40.9 %collective-permute-start.6 = (bf16[448,256]{1,0:T(8,128)(2,1)}, bf16[448,256]{1,0:T(8,128)(2,1)S(1)}, u32[]{:S(2)}, u32[]{:S(2)}) collective-permute-start(bf16[448,256]{1,0:T(8,128)(2,1)} %shard_map.137.refs_0_), channel_id=1, source_target_pairs={{0,5},{1,6},{2,7},{3,0},{4,1},{5,2},{6,3},{7,4},{8,13},{9,14},{10,... | collective-permute-start | bytes 688136 | tf_op jit(solution)/shard_map/ppermute | solution.py:597
  10.0 41.6 %collective-permute-start.5 = (bf16[448,256]{1,0:T(8,128)(2,1)}, bf16[448,256]{1,0:T(8,128)(2,1)}, u32[]{:S(2)}, u32[]{:S(2)}) collective-permute-start(bf16[448,256]{1,0:T(8,128)(2,1)} %shard_map.137.refs_0_), channel_id=1, source_target_pairs={{0,4},{1,5},{2,6},{3,7},{4,0},{5,1},{6,2},{7,3},{8,12},{9,13},{10,... | collective-permute-start | bytes 688136 | tf_op jit(solution)/shard_map/ppermute | solution.py:597
  12.6 26.3 %copy-start.1 = (bf16[448,256]{1,0:T(8,128)(2,1)S(1)}, bf16[448,256]{1,0:T(8,128)(2,1)}, u32[]{:S(2)}) copy-start(bf16[448,256]{1,0:T(8,128)(2,1)} %shard_map.137.refs_0_) | copy-start | bytes 688132
  33.7 45.2 %copy-start = (f32[1,2,256,1024]{3,2,1,0:T(8,128)S(1)}, f32[1,2,256,1024]{3,2,1,0:T(8,128)}, u32[]{:S(2)}) copy-start(f32[1,2,256,1024]{3,2,1,0:T(8,128)} %param.17) | copy-start | bytes 6291460
  33.7 1.3 %collective-permute-start = (f32[8,1536]{1,0:T(8,128)S(1)}, f32[8,1536]{1,0:T(8,128)S(1)}, u32[]{:S(2)}, u32[]{:S(2)}) collective-permute-start(f32[8,1536]{1,0:T(8,128)S(1)} %get-tuple-element.66), channel_id=1, source_target_pairs={{0,8},{8,0},{16,24},{24,16},{1,9},{9,1},{17,25},{25,17},{2,10},{10... | collective-permute-start | bytes 147464 | tf_op jit(solution)/shard_map/ppermute | solution.py:602
  35.0 3.9 %collective-permute-start.1 = (bf16[8,1536]{1,0:T(8,128)(2,1)S(1)}, bf16[8,1536]{1,0:T(8,128)(2,1)S(1)}, u32[]{:S(2)}, u32[]{:S(2)}) collective-permute-start(bf16[8,1536]{1,0:T(8,128)(2,1)S(1)} %add_convert_fusion), channel_id=1, source_target_pairs={{0,16},{8,24},{16,0},{24,8},{1,17},{9,25},{17,1},{25,9},{2,18},{10... | collective-permute-start | bytes 73736 | tf_op jit(solution)/shard_map/ppermute | solution.py:604
  38.9 26.0 %collective-permute-start.4 = (bf16[448,256]{1,0:T(8,128)(2,1)S(1)}, bf16[448,256]{1,0:T(8,128)(2,1)}, u32[]{:S(2)}, u32[]{:S(2)}) collective-permute-start(bf16[448,256]{1,0:T(8,128)(2,1)S(1)} %copy-done.1), channel_id=1, source_target_pairs={{0,3},{1,4},{2,5},{3,6},{4,7},{5,0},{6,1},{7,2},{8,11},{9,12},{10,... | collective-permute-start | bytes 688136 | tf_op jit(solution)/shard_map/ppermute | solution.py:597
  40.0 26.3 %all-to-all-start = ((bf16[8,8,2560]{2,1,0:T(8,128)(2,1)}), bf16[8,8,2560]{2,1,0:T(8,128)(2,1)S(1)}, u32[]{:S(2)}, u32[]{:S(2)}) async-start(bf16[8,8,2560]{2,1,0:T(8,128)(2,1)} %broadcast_in_dim.26), calls=%async_computation | async-start | bytes 655360 | tf_op jit(solution)/shard_map/all_to_all | solution.py:576
  45.8 19.1 %collective-permute-start.3 = (bf16[448,256]{1,0:T(8,128)(2,1)S(1)}, bf16[448,256]{1,0:T(8,128)(2,1)S(1)}, u32[]{:S(2)}, u32[]{:S(2)}) collective-permute-start(bf16[448,256]{1,0:T(8,128)(2,1)S(1)} %copy-done.1), channel_id=1, source_target_pairs={{0,2},{1,3},{2,4},{3,5},{4,6},{5,7},{6,0},{7,1},{8,10},{9,11},{10,... | collective-permute-start | bytes 688136 | tf_op jit(solution)/shard_map/ppermute | solution.py:597
  47.9 0.7 copy-start.5
  48.6 17.0 %collective-permute-start.2 = (bf16[448,256]{1,0:T(8,128)(2,1)S(1)}, bf16[448,256]{1,0:T(8,128)(2,1)S(1)}, u32[]{:S(2)}, u32[]{:S(2)}) collective-permute-start(bf16[448,256]{1,0:T(8,128)(2,1)S(1)} %copy-done.1), channel_id=1, source_target_pairs={{0,1},{1,2},{2,3},{3,4},{4,5},{5,6},{6,7},{7,0},{8,9},{9,10},{10,1... | collective-permute-start | bytes 688136 | tf_op jit(solution)/shard_map/ppermute | solution.py:597
  50.9 0.7 copy-start.7
  64.9 0.7 copy-start.9
  65.6 0.7 copy-start.11
  66.3 0.9 copy-start.6
  67.2 0.9 copy-start.8
  68.2 0.9 copy-start.10
  69.1 0.9 copy-start.12
  73.0 0.8 copy-start.13
  73.8 1.2 %collective-permute-start.9 = (f32[8,1024]{1,0:T(8,128)S(1)}, f32[8,1024]{1,0:T(8,128)S(1)}, u32[]{:S(2)}, u32[]{:S(2)}) collective-permute-start(f32[8,1024]{1,0:T(8,128)S(1)} %get-tuple-element.41), channel_id=1, source_target_pairs={{0,8},{8,0},{16,24},{24,16},{1,9},{9,1},{17,25},{25,17},{2,10},{10... | collective-permute-start | bytes 98312 | tf_op jit(solution)/shard_map/ppermute | solution.py:631
  75.0 3.9 %collective-permute-start.10 = (f32[8,1024]{1,0:T(8,128)S(1)}, f32[8,1024]{1,0:T(8,128)S(1)}, u32[]{:S(2)}, u32[]{:S(2)}) collective-permute-start(f32[8,1024]{1,0:T(8,128)S(1)} %add.34), channel_id=1, source_target_pairs={{0,16},{8,24},{16,0},{24,8},{1,17},{9,25},{17,1},{25,9},{2,18},{10... | collective-permute-start | bytes 98312 | tf_op jit(solution)/shard_map/ppermute | solution.py:632
  78.9 1.0 copy-start.2
  87.2 12.4 %all-to-all-start.1 = ((bf16[8,8,1024]{2,1,0:T(8,128)(2,1)}), bf16[8,8,1024]{2,1,0:T(8,128)(2,1)S(1)}, u32[]{:S(2)}, u32[]{:S(2)}) async-start(bf16[8,8,1024]{2,1,0:T(8,128)(2,1)} %broadcast_in_dim.50), calls=%async_computation.1 | async-start | bytes 262144 | tf_op jit(solution)/shard_map/all_to_all | solution.py:576

commit v2 on v1

--- a/solution.py
+++ b/solution.py
@@ -15,6 +15,8 @@
 HEAD_IMG = 64
 HEAD_TXT = 128
 CAP = 2
+SIDES = 2
+TILE = 16
 
 
 norm_eps = 1e-06
@@ -260,51 +262,84 @@
 
 
 def unit_groups(shard_count, shard_rows, first_rows, segment_count):
-    groups = []
+    shards = []
     for shard in range(shard_count):
         inside = first_rows_in(shard, shard_rows, first_rows)
         if inside < shard_rows:
-            share = (shard_rows - inside) // segment_count
-            groups.append((shard, inside, shard * shard_rows + inside - first_rows, share))
+            shards.append((shard, inside, shard * shard_rows + inside - first_rows, shard_rows - inside))
+    tiles = [rows // (TILE * segment_count) for _, _, _, rows in shards]
+    room = sum(tiles) // SIDES
+    taken = [count // SIDES for count in tiles]
+    for index, count in enumerate(tiles):
+        if count % SIDES and sum(taken) < room:
+            taken[index] += 1
+    sides = [taken, [count - mine for count, mine in zip(tiles, taken)]]
+    groups = []
+    for index, (shard, inside, base, _) in enumerate(shards):
+        starts, shares, start = [], [], 0
+        for side in range(SIDES):
+            share = sides[side][index] * TILE
+            starts.append(start)
+            shares.append(share)
+            start += share * segment_count
+        groups.append((shard, inside, base, tuple(starts), tuple(shares)))
     return groups
+
+
+def even_units(groups, shard_rows, segment_count, width):
+    return all(
+        inside % TILE == 0 and sum(shares) * segment_count == shard_rows - inside and min(shares) > 0
+        for _, inside, _, _, shares in groups
+    ) and all(sum(group[4][side] for group in groups) * segment_count * SIDES == width for side in range(SIDES))
+
+
+def piece_rows(groups, shard_rows, width, columns):
+    return max([shard_rows] + [inside + width // columns * max(shares) for _, inside, _, _, shares in groups])
 
 
 def message_kernel(groups, place_ref, rows_ref, message_ref):
     shard, segment = place_ref[0], place_ref[1]
     row_count, width = rows_ref.shape
-    columns = message_ref.shape[1]
+    copies, _, columns = message_ref.shape
     first_last = groups[0][0]
 
     @pl.when(shard <= first_last)
     def _():
-        wanted = lax.broadcasted_iota(jnp.int32, (width, columns), 1)
+        wanted = lax.broadcasted_iota(jnp.int32, (width, SIDES * columns), 1)
         unit = jnp.zeros_like(wanted)
         offset = 0
-        for _, _, base, share in groups:
-            inside = (wanted >= offset) & (wanted < offset + share)
-            unit = jnp.where(inside, wanted - offset + base + share * segment, unit)
-            offset += share
-        chosen = (lax.broadcasted_iota(jnp.int32, (width, columns), 0) == unit).astype(F32).astype(BF16)
-        message_ref[...] = dot_nn(rows_ref[...], chosen).astype(BF16)
-
-    for group_shard, inside, _, share in groups:
+        for side in range(SIDES):
+            for _, _, base, starts, shares in groups:
+                inside = (wanted >= offset) & (wanted < offset + shares[side])
+                unit = jnp.where(inside, wanted - offset + base + starts[side] + shares[side] * segment, unit)
+                offset += shares[side]
+        chosen = (lax.broadcasted_iota(jnp.int32, (width, SIDES * columns), 0) == unit).astype(F32).astype(BF16)
+        message = dot_nn(rows_ref[...], chosen).astype(BF16)
+        for copy in range(copies):
+            side = copy % SIDES
+            message_ref[copy, :row_count, :] = message[:, side * columns : (side + 1) * columns]
+
+    for group_shard, inside, _, starts, shares in groups:
 
         @pl.when(shard == group_shard)
-        def _(inside=inside, share=share):
-            start = pl.multiple_of(inside + share * segment, 16)
-            for block in range(width // columns):
-                message_ref[inside + block * share : inside + (block + 1) * share, :] = rows_ref[
-                    pl.ds(start, share), block * columns : (block + 1) * columns
-                ]
-
-
-def weight_message(uniting_weights, place, groups, columns):
+        def _(inside=inside, starts=starts, shares=shares):
+            for side in range(SIDES):
+                share = shares[side]
+                start = pl.multiple_of(inside + starts[side] + share * segment, TILE)
+                for block in range(width // columns):
+                    piece = rows_ref[pl.ds(start, share), block * columns : (block + 1) * columns]
+                    for copy in range(side, copies, SIDES):
+                        message_ref[copy, inside + block * share : inside + (block + 1) * share, :] = piece
+
+
+def weight_message(uniting_weights, place, groups, copies, columns):
+    shard_rows, width = uniting_weights.shape
     vm = pl.BlockSpec(memory_space=pltpu.VMEM)
     return pl.pallas_call(
         functools.partial(message_kernel, groups),
         in_specs=[pl.BlockSpec(memory_space=pltpu.SMEM), vm],
         out_specs=vm,
-        out_shape=jax.ShapeDtypeStruct((uniting_weights.shape[0], columns), BF16),
+        out_shape=jax.ShapeDtypeStruct((copies, piece_rows(groups, shard_rows, width, columns), columns), BF16),
     )(place, uniting_weights)
 
 
@@ -314,59 +349,58 @@
     place_ref,
     embedded_ref,
     own_ref,
-    *refs,
+    weights,
+    blocks_ref,
+    hidden_ref,
+    active_ref,
+    second_ref,
+    partial_ref,
 ):
-    shard_count = (len(refs) - 6)
-    piece_refs = refs[:shard_count]
-    blocks_ref, hidden_ref, active_ref, second_ref, partial_ref, kept = refs[shard_count:]
-    shard = place_ref[0]
+    shard_count, _, columns = weights.shape
+    shard_rows = blocks_ref.shape[2]
     source_count, source_items, width = embedded_ref.shape
     items = source_count * source_items
-    shard_rows, columns = piece_refs[0].shape
     embedded = embedded_ref[...].astype(F32).reshape(items, width)
     normed = embedded * lax.rsqrt(jnp.mean(embedded * embedded, axis=1, keepdims=True) + norm_eps)
     normed = normed.astype(BF16)
+    hidden = jnp.zeros((items, columns), F32)
     for block in range(shard_count):
         inside = first_rows_in(block, shard_rows, first_rows)
         start = block * shard_rows
-        if inside == shard_rows:
-            blocks_ref[block] = normed[:, start : start + shard_rows]
-        elif inside > 0:
-            blocks_ref[block] = jnp.concatenate(
-                [normed[:, start : start + inside], jnp.zeros((items, shard_rows - inside), BF16)], axis=1
-            )
+        if inside > 0:
+            rows = normed[:, start : start + inside]
+            hidden = hidden + dot_nn(rows, weights[block, :inside])
+            if inside < shard_rows:
+                rows = jnp.concatenate([rows, jnp.zeros((items, shard_rows - inside), BF16)], axis=1)
+            blocks_ref[block] = rows
         else:
             blocks_ref[block] = jnp.zeros((items, shard_rows), BF16)
-    hidden = jnp.zeros((items, columns), F32)
-    first_group = groups[0][0]
-    for turn in range(shard_count):
-        source = lax.rem(shard - turn + shard_count, shard_count)
-        hidden = hidden + dot_nn(blocks_ref[source], piece_refs[turn][...])
-
-        @pl.when(source >= first_group)
-        def _(turn=turn, source=source):
-            kept[source - first_group] = piece_refs[turn][...]
-
     hidden_ref[...] = hidden
     active = gelu_value(hidden).astype(BF16)
     active_ref[...] = active
-    offset = 0
-    for index, (_, inside, _, share) in enumerate(groups):
-        for block in range(partial_ref.shape[1] // columns):
-            second_ref[offset : offset + share, block * columns : (block + 1) * columns] = kept[
-                index, inside + block * share : inside + (block + 1) * share, :
-            ]
-        offset += share
+    for side in range(SIDES):
+
+        @pl.when(lax.rem(place_ref[0], SIDES) == side)
+        def _(side=side):
+            offset = 0
+            for block, inside, _, _, shares in groups:
+                share = shares[side]
+                for part in range(partial_ref.shape[1] // columns):
+                    second_ref[offset : offset + share, part * columns : (part + 1) * columns] = weights[
+                        block, inside + part * share : inside + (part + 1) * share, :
+                    ]
+                offset += share
+
     partial_ref[...] = dot_nn(dot_nn(own_ref[...], active).astype(BF16), second_ref[...])
 
 
-def merge_quarter(embedded_all, pieces, own, place, groups, first_rows, width):
-    shard_count, shard_rows, columns = len(pieces), pieces[0].shape[0], pieces[0].shape[1]
+def merge_part(embedded_all, pieces, own, place, groups, shard_rows, first_rows, width):
+    shard_count, _, columns = pieces.shape
     items = embedded_all.shape[0] * embedded_all.shape[1]
     vm = pl.BlockSpec(memory_space=pltpu.VMEM)
     return pl.pallas_call(
         functools.partial(forward_kernel, groups, first_rows),
-        in_specs=[pl.BlockSpec(memory_space=pltpu.SMEM)] + [vm] * (2 + shard_count),
+        in_specs=[pl.BlockSpec(memory_space=pltpu.SMEM), vm, vm, vm],
         out_specs=[vm] * 5,
         out_shape=[
             jax.ShapeDtypeStruct((shard_count, items, shard_rows), BF16),
@@ -375,9 +409,8 @@
             jax.ShapeDtypeStruct((columns, width), BF16),
             jax.ShapeDtypeStruct((own.shape[0], width), F32),
         ],
-        scratch_shapes=[pltpu.VMEM((len(groups), shard_rows, columns), BF16)],
         compiler_params=pltpu.CompilerParams(vmem_limit_bytes=32 * 1024 * 1024),
-    )(place, embedded_all, own, *pieces)
+    )(place, embedded_all, own, pieces)
 
 
 def split(value):
@@ -517,7 +550,7 @@
     sent_ref[:, columns:] = active_ref[...]
 
 
-def backward_quarter(gathered, order, hidden, active, second):
+def backward_part(gathered, order, hidden, active, second):
     items, columns = hidden.shape
     vm = pl.BlockSpec(memory_space=pltpu.VMEM)
     return pl.pallas_call(
@@ -532,44 +565,50 @@
     )(gathered, order, hidden, active, second)
 
 
-def weight_grad_kernel(groups, place_ref, block_ref, out_grad_ref, received_ref, grad_ref, hidden_grad, active):
+def weight_grad_kernel(
+    groups, place_ref, block_ref, out_grad_ref, near_ref, across_ref, grad_ref, hidden_grad, active
+):
     shard = place_ref[0]
-    segment_count, items, doubled = received_ref.shape
+    segment_count, items, doubled = near_ref.shape
     columns = doubled // 2
     shard_rows = block_ref.shape[1]
-    for segment in range(segment_count):
-        offset = 0
-        for _, _, base, share in groups:
-            spot = base + share * segment
-            hidden_grad[:, spot : spot + share] = received_ref[segment, :, offset : offset + share]
-            offset += share
+    here = lax.rem(shard, SIDES)
+
+    def place_units(target, first):
+        for side in range(SIDES):
+            for segment in range(segment_count):
+                near = near_ref[segment, :, first : first + columns]
+                across = across_ref[segment, :, first : first + columns]
+                part = jnp.where(here == side, near, across)
+                offset = 0
+                for _, _, base, starts, shares in groups:
+                    spot = base + starts[side] + shares[side] * segment
+                    target[:, spot : spot + shares[side]] = part[:, offset : offset + shares[side]]
+                    offset += shares[side]
+
+    place_units(hidden_grad, 0)
     grad_ref[...] = dot_tn(block_ref[...], hidden_grad[...])
-    for group_shard, inside, base, _ in groups:
+    for group_shard, inside, base, _, _ in groups:
 
         @pl.when(shard == group_shard)
         def _(inside=inside, base=base):
-            for segment in range(segment_count):
-                offset = columns
-                for _, _, other, share in groups:
-                    spot = other + share * segment
-                    active[:, spot : spot + share] = received_ref[segment, :, offset : offset + share]
-                    offset += share
+            place_units(active, columns)
             wanted = active[:, base : base + shard_rows - inside]
             grad_ref[inside:, :] = dot_tn(wanted, out_grad_ref[...])
 
 
-def weight_grad(place, block, out_grad, received, groups):
+def weight_grad(place, block, out_grad, near, across, groups):
     items, shard_rows = block.shape
     width = out_grad.shape[1]
     vm = pl.BlockSpec(memory_space=pltpu.VMEM)
     return pl.pallas_call(
         functools.partial(weight_grad_kernel, groups),
-        in_specs=[pl.BlockSpec(memory_space=pltpu.SMEM)] + [vm] * 3,
+        in_specs=[pl.BlockSpec(memory_space=pltpu.SMEM)] + [vm] * 4,
         out_specs=vm,
         out_shape=jax.ShapeDtypeStruct((shard_rows, width), F32),
         scratch_shapes=[pltpu.VMEM((items, width), BF16), pltpu.VMEM((items, width), BF16)],
         compiler_params=pltpu.CompilerParams(vmem_limit_bytes=32 * 1024 * 1024),
-    )(place, block, out_grad, received)
+    )(place, block, out_grad, near, across)
 
 
 def spread(rows, axis_name, count):
@@ -578,7 +617,7 @@
     )
 
 
-def per_device_quarters(
+def per_device_parts(
     images, texts, section_weights, uniting_weights, codebooks, neg_bank, item_cats, cat_slot, neg_index
 ):
     segment_index = lax.axis_index("segment")
@@ -589,14 +628,11 @@
     text_width = texts.shape[2]
     first_rows = image_width + text_width
     shard_rows, width = uniting_weights.shape
-    columns = width // segment_count
+    columns = width // (SIDES * segment_count)
     groups = unit_groups(dp_count, shard_rows, first_rows, segment_count)
     place = jnp.stack([dp_index, segment_index]).astype(jnp.int32)
-    message = weight_message(uniting_weights, place, groups, columns)
-    pieces = [message] + [
-        lax.ppermute(message, "dp", [(i, (i + turn) % dp_count) for i in range(dp_count)])
-        for turn in range(1, dp_count)
-    ]
+    message = weight_message(uniting_weights, place, groups, dp_count, columns)
+    pieces = lax.all_to_all(message, "dp", 0, 0, tiled=True)
     flag = (1 - segment_index % 2).astype(jnp.int32).reshape(1)
     pooled = pooled_features(images, texts, section_weights, segment_index, flag)
     pooled = pooled + lax.ppermute(pooled, "segment", [(i, i ^ 1) for i in range(segment_count)])
@@ -606,6 +642,7 @@
     embedded = jnp.concatenate(
         [jnp.where(is_image, mine, other)[:, :image_width], jnp.where(is_image, other, mine)], axis=1
     )
+    embedded, pieces = lax.optimization_barrier((embedded, pieces))
     embedded_all = spread(embedded, "dp", dp_count)
 
     pair = item_cats.shape[1] // dp_count
@@ -619,23 +656,27 @@
     owned = segment_count * CAP
     order = (ids[:, None] == (slots * owned + rank)[None, :]).astype(BF16)
     own = lax.dynamic_slice_in_dim(order, dp_index * owned, owned, 0)
+    across_own = lax.dynamic_slice_in_dim(order, (dp_index ^ 1) * owned, owned, 0)
+    both_own = jnp.concatenate([own, across_own], axis=0)
     negatives = neg_index.reshape(segment_count, dp_count, pair, -1).transpose(1, 0, 2, 3).reshape(items, -1)
     own_negatives = jnp.dot(own.astype(F32), negatives.astype(F32), precision=highest)
     bank = neg_bank[0]
     bank_ids = jnp.arange(bank.shape[0]).astype(F32)
     counts = jnp.sum((own_negatives[:, :, None] == bank_ids[None, None, :]).astype(F32), axis=1)
 
-    blocks, hidden, active, second, partial = merge_quarter(
-        embedded_all, pieces, own, place, groups, first_rows, width
+    blocks, hidden, active, second, partial = merge_part(
+        embedded_all, pieces, both_own, place, groups, shard_rows, first_rows, width
     )
     partial = partial + lax.ppermute(partial, "segment", [(i, i ^ 1) for i in range(segment_count)])
-    merged = partial + lax.ppermute(partial, "segment", [(i, i ^ 2) for i in range(segment_count)])
+    partial = partial + lax.ppermute(partial, "segment", [(i, i ^ 2) for i in range(segment_count)])
+    merged = partial[:owned] + lax.ppermute(partial[owned:], "dp", [(i, i ^ 1) for i in range(dp_count)])
     book_grad, merged_grad, loss = quantizer(merged, codebooks[0], bank, counts, 1.0 / math.sqrt(items))
     gathered = spread(merged_grad, "dp", dp_count)
-    out_grad, sent = backward_quarter(gathered, order, hidden, active, second)
-    received = lax.all_gather(sent, "segment", axis=0)
+    out_grad, sent = backward_part(gathered, order, hidden, active, second)
+    near = lax.all_gather(sent, "segment", axis=0)
+    across = lax.ppermute(near, "dp", [(i, i ^ 1) for i in range(dp_count)])
     block = lax.dynamic_index_in_dim(blocks, dp_index, 0, keepdims=False)
-    uniting_grad = weight_grad(place, block, out_grad, received, groups)
+    uniting_grad = weight_grad(place, block, out_grad, near, across, groups)
     return (uniting_grad, book_grad[None], loss[0, :1])
 
 
@@ -754,11 +795,8 @@
     shard_rows = uniting_weights.shape[0]
     first_rows = images.shape[2] + texts.shape[2]
     groups = unit_groups(dp_count, shard_rows, first_rows, segment_count)
-    whole_tiles = all(
-        (shard_rows - inside) % (16 * segment_count) == 0 and inside % 16 == 0 for _, inside, _, _ in groups
-    )
-    if whole_tiles:
-        return per_device_quarters(*operands)
+    if dp_count % SIDES == 0 and even_units(groups, shard_rows, segment_count, uniting_weights.shape[1]):
+        return per_device_parts(*operands)
     return per_device_gathered(*operands)
 
 

time: 109 us -> 96.5 us (0.89)
  blocking collectives: 5.79 us -> 16.2 us
  local copies, waits for them, and re-layouts: 11.5 us -> 2.52 us
  starting transfers between devices: 24.1 us -> 15.3 us
  waiting for transfers between devices: 28.3 us -> 25.3 us
    ppermute x11 -> x6, starting transfers between devices: 13.3 us -> 2.25 us  [the longest x1 1.56 us: per_device_parts(): lax.ppermute(partial[owned:], 'dp', [(i, i ^ 1) for i in range(dp_count)])]
    all_to_all x0 -> x1, blocking collectives: none -> 10.8 us  [spread(): lax.all_to_all(jnp.broadcast_to(rows[None], (count,) + rows.shape), axis_...]
    unnamed x31 -> x17, local copies, waits for them, and re-layouts: 8.5 us -> 0.12 us
    all_to_all x0 -> x1, starting transfers between devices: none -> 7.09 us  [per_device_parts(): pieces = lax.all_to_all(message, 'dp', 0, 0, tiled=True)]
    ppermute x11 -> x6, waiting for transfers between devices: 22.3 us -> 15.9 us  [the longest x1 4.17 us: per_device_parts(): across = lax.ppermute(near, 'dp', [(i, i ^ 1) for i in range(dp_count)])]
    all_to_all x2 -> x1, starting transfers between devices: 10.8 us -> 5.98 us  [spread(): lax.all_to_all(jnp.broadcast_to(rows[None], (count,) + rows.shape), axis_...]
    all_to_all x2 -> x1, waiting for transfers between devices: 5.99 us -> 9.4 us  [spread(): lax.all_to_all(jnp.broadcast_to(rows[None], (count,) + rows.shape), axis_...]
    pallas_call x2, Pallas kernels: 3.31 us -> 1.85 us  [the longest x1 1.49 us: merge_part(): pl.pallas_call(functools.partial(forward_kernel, groups, first_rows), in_...]
  transfers between devices with their start and end apart: 13 -> 8, of which waited for: 6 -> 7; matrix products, arithmetic and copies ran while one was open for 4% -> 2% of each run, Pallas kernels for 19% -> 22%
where the time goes in v2:
time: 96.5 us; the launch traced here: 96 us
  Pallas kernels  34.6 us (36%)
  waiting for transfers between devices  25.3 us (26%)
  blocking collectives  16.2 us (17%)
  starting transfers between devices  15.3 us (16%)
  local copies, waits for them, and re-layouts  2.52 us (3%)
  other arithmetic  1.14 us (1%)
    pallas_call x1, Pallas kernels, image_pooled(): pl.pallas_call(image_kernel, grid=(item_count,), in_specs=[pl.BlockSpec(m...  21.1 us
    all_to_all x1, blocking collectives, spread(): lax.all_to_all(jnp.broadcast_to(rows[None], (count,) + rows.shape), axis_...  10.8 us
    all_to_all x1, waiting for transfers between devices, spread(): lax.all_to_all(jnp.broadcast_to(rows[None], (count,) + rows.shape), axis_...  9.4 us
    all_to_all x1, starting transfers between devices, per_device_parts(): pieces = lax.all_to_all(message, 'dp', 0, 0, tiled=True)  7.09 us
    pallas_call x1, Pallas kernels, quantizer(): pl.pallas_call(functools.partial(quantizer_kernel, loss_scale), in_specs=...  6.7 us
    all_to_all x1, starting transfers between devices, spread(): lax.all_to_all(jnp.broadcast_to(rows[None], (count,) + rows.shape), axis_...  5.98 us
    all_gather x1, blocking collectives, per_device_parts(): near = lax.all_gather(sent, 'segment', axis=0)  5.43 us
    ppermute x1, waiting for transfers between devices, per_device_parts(): across = lax.ppermute(near, 'dp', [(i, i ^ 1) for i in range(dp_count)])  4.17 us
  transfers between devices with their start and end apart: 8, of which 7 were waited for; matrix products, arithmetic and copies ran while one was open for 2% of the time, Pallas kernels for 22%

profile of v2, /device:TPU:0, one launch (start us, length us, event | category | flops | bytes accessed | tf_op | source)
XLA Modules:
  0.0 96.0 jit_solution(9403150387164621048)
XLA Ops:
  0.6 0.6 pad_add_fusion.place_ref
  1.2 2.6 %shard_map.137 = bf16[8,512,128]{2,1,0:T(8,128)(2,1)} custom-call(s32[2]{0:T(128)} %pad_add_fusion.place_ref, bf16[448,1024]{1,0:T(8,128)(2,1)} %rows_ref.1), custom_call_target="tpu_custom_call" | custom-call | tf_op jit(solution)/shard_map/pallas_call | solution.py:338
  3.8 7.1 %all-to-all-start = ((bf16[8,512,128]{2,1,0:T(8,128)(2,1)}), bf16[8,512,128]{2,1,0:T(8,128)(2,1)S(1)}, u32[]{:S(2)}, u32[]{:S(2)}) async-start(bf16[8,512,128]{2,1,0:T(8,128)(2,1)} %shard_map.137), calls=%async_computation | async-start | bytes 2097152 | tf_op jit(solution)/shard_map/all_to_all | solution.py:635
  11.0 21.1 %conditional.1 = (f32[8,1536]{1,0:T(8,128)S(1)}) conditional(s32[]{:T(128)} %convert_element_type.34, (s32[1]{0:T(128)}, bf16[8,64,1536]{2,1,0:T(8,128)(2,1)S(1)}, bf16[1,21504,128]{2,1,0:T(8,128)(2,1)}) %tuple.27, (s32[1]{0:T(128)}, bf16[8,256,1024]{2,1,0:T(8,128)(2,1)}, bf16[1,21504,128]{2,1,0:T(8,128)(2,1)}) %tuple.16), branch_computations={%region_0.1_spmd.clone, %region_1.2_spmd} | conditional | bytes 2097216 | solution.py:693
  11.0 21.1 %branch_1_fun.1 = f32[8,1024]{1,0:T(8,128)S(1)} custom-call(s32[1]{0:T(128)} %get-tuple-element.24.flag_ref, bf16[8,256,1024]{2,1,0:T(8,128)(2,1)} %get-tuple-element.61.image_ref, bf16[1,21504,128]{2,1,0:T(8,128)(2,1)} %get-tuple-element.26.slot_ref), custom_call_target="tpu_custom_call" | custom-call | tf_op jit(solution)/shard_map/cond/branch_1_fun/pallas_call | solution.py:111
  32.2 0.1 copy.26
  32.3 0.1 copy.27
  32.4 0.1 eq.59
  32.5 0.1 select_reduce_fusion.1
  32.6 0.8 collective-permute-done
  33.5 0.2 select_reduce_fusion
  33.7 3.6 %collective-permute-done.1 = bf16[8,1536]{1,0:T(8,128)(2,1)S(1)} collective-permute-done((bf16[8,1536]{1,0:T(8,128)(2,1)S(1)}, bf16[8,1536]{1,0:T(8,128)(2,1)S(1)}, u32[]{:S(2)}, u32[]{:S(2)}) %collective-permute-start.1) | collective-permute-done | bytes 24608 | tf_op jit(solution)/shard_map/ppermute | solution.py:640
  37.3 0.7 broadcast_in_dim.26
  38.1 6.0 %all-to-all-start.1 = ((bf16[8,8,2560]{2,1,0:T(8,128)(2,1)}), bf16[8,8,2560]{2,1,0:T(8,128)(2,1)S(1)}, u32[]{:S(2)}, u32[]{:S(2)}) async-start(bf16[8,8,2560]{2,1,0:T(8,128)(2,1)} %broadcast_in_dim.26), calls=%async_computation.1 | async-start | bytes 655360 | tf_op jit(solution)/shard_map/all_to_all | solution.py:615
  44.1 9.4 %all-to-all-done.1.embedded_ref = bf16[8,8,2560]{2,1,0:T(8,128)(2,1)S(1)} async-done(((bf16[8,8,2560]{2,1,0:T(8,128)(2,1)}), bf16[8,8,2560]{2,1,0:T(8,128)(2,1)S(1)}, u32[]{:S(2)}, u32[]{:S(2)}) %all-to-all-start.1) | async-done | bytes 327712 | tf_op jit(solution)/shard_map/all_to_all | solution.py:615
  53.5 1.5 %shard_map.138 = (bf16[8,64,448]{2,1,0:T(8,128)(2,1)S(1)}, f32[64,128]{1,0:T(8,128)S(1)}, bf16[64,128]{1,0:T(8,128)(2,1)S(1)}, bf16[128,1024]{1,0:T(8,128)(2,1)S(1)}, f32[16,1024]{1,0:T(8,128)S(1)}) custom-call(s32[2]{0:T(128)S(1)} %copy-done.5, bf16[8,8,2560]{2,1,0:T(8,128)(2,1)S(1)} %all-to-all-done.1.embedded_ref, ...), custom_call_target="tpu_custom_call" | custom-call | tf_op jit(solution)/shard_map/pallas_call | solution.py:401
  55.0 0.1 fusion.1
  55.1 1.1 %collective-permute-done.2 = f32[16,1024]{1,0:T(8,128)S(1)} collective-permute-done((f32[16,1024]{1,0:T(8,128)S(1)}, f32[16,1024]{1,0:T(8,128)S(1)}, u32[]{:S(2)}, u32[]{:S(2)}) %collective-permute-start.2) | collective-permute-done | bytes 65568 | tf_op jit(solution)/shard_map/ppermute | solution.py:670
  56.3 0.3 collective-permute-start.3
  56.6 4.0 %collective-permute-done.3 = f32[16,1024]{1,0:T(8,128)S(1)} collective-permute-done((f32[16,1024]{1,0:T(8,128)S(1)}, f32[16,1024]{1,0:T(8,128)S(1)}, u32[]{:S(2)}, u32[]{:S(2)}) %collective-permute-start.3) | collective-permute-done | bytes 65568 | tf_op jit(solution)/shard_map/ppermute | solution.py:671
  60.6 1.6 %collective-permute-start.4 = (f32[8,1024]{1,0:T(8,128)S(1)}, f32[8,1024]{1,0:T(8,128)S(1)}, u32[]{:S(2)}, u32[]{:S(2)}) collective-permute-start(f32[8,1024]{1,0:T(8,128)S(1)} %slice.19), channel_id=1, source_target_pairs={{0,1},{1,0},{2,3},{3,2},{4,5},{5,4},{6,7},{7,6},{8,9},{9,8},{10,11... | collective-permute-start | bytes 98312 | tf_op jit(solution)/shard_map/ppermute | solution.py:672
  62.2 0.2 convert_reduce_fusion.count_ref
  62.4 2.2 %collective-permute-done.4 = f32[8,1024]{1,0:T(8,128)S(1)} collective-permute-done((f32[8,1024]{1,0:T(8,128)S(1)}, f32[8,1024]{1,0:T(8,128)S(1)}, u32[]{:S(2)}, u32[]{:S(2)}) %collective-permute-start.4) | collective-permute-done | bytes 32800 | tf_op jit(solution)/shard_map/ppermute | solution.py:672
  64.6 6.7 %shard_map.139 = (f32[2,256,1024]{2,1,0:T(8,128)}, bf16[8,1024]{1,0:T(8,128)(2,1)S(1)}, f32[8,128]{1,0:T(8,128)S(1)}) custom-call(f32[8,1024]{1,0:T(8,128)S(1)} %slice_add_fusion.merged_ref, f32[2,256,1024]{2,1,0:T(8,128)S(1)} %bitcast.18, bf16[256,1024]{1,0:T(8,128)(2,1)S(1)} %bitcast.21, f32[8,256]{1,0:T(8,128)S(1)} %convert_reduce_fusion.count_ref), custom_call_target="tpu_custom_call" | custom-call | tf_op jit(solution)/shard_map/pallas_call | solution.py:528
  71.4 10.8 %all_to_all.15.gathered_ref = bf16[8,8,1024]{2,1,0:T(8,128)(2,1)S(1)} all-to-all(bf16[8,8,1024]{2,1,0:T(8,128)(2,1)S(1)} %broadcast_in_dim.50), channel_id=1, replica_groups=mesh['segment'=4,'dp'=8] {'dp'}, dimensions={0} | all-to-all | bytes 262144 | tf_op jit(solution)/shard_map/all_to_all | solution.py:615
  82.1 0.4 shard_map.140
  82.5 5.4 %all-gather = bf16[256,256]{1,0:T(8,128)(2,1)S(1)} all-gather(bf16[64,256]{1,0:T(8,128)(2,1)S(1)} %get-tuple-element.51), channel_id=2, replica_groups=mesh['segment'=4,'dp'=8] {'segment'}, dimensions={0}, use_global_device_ids=true | all-gather | bytes 163840 | tf_op jit(solution)/shard_map/all_gather | solution.py:676
  87.9 0.2 collective-permute-start.5
  88.1 0.8 dynamic-slice_bitcast_fusion.block_ref
  89.0 0.5 slice.15
  89.5 4.2 %collective-permute-done.5.across_ref = bf16[4,64,256]{2,1,0:T(8,128)(2,1)S(1)} collective-permute-done((bf16[4,64,256]{2,1,0:T(8,128)(2,1)S(1)}, bf16[4,64,256]{2,1,0:T(8,128)(2,1)S(1)}, u32[]{:S(2)}, u32[]{:S(2)}) %collective-permute-start.5) | collective-permute-done | bytes 131104 | tf_op jit(solution)/shard_map/ppermute | solution.py:677
  93.7 2.4 %shard_map.141 = f32[448,1024]{1,0:T(8,128)} custom-call(s32[2]{0:T(128)S(1)} %copy-done.5, bf16[64,448]{1,0:T(8,128)(2,1)S(1)} %dynamic-slice_bitcast_fusion.block_ref, bf16[64,1024]{1,0:T(8,128)(2,1)S(1)} %get-tuple-element.50.out_grad_ref, bf16[4,64,256]{2,1,0:T(8,128)(2,1)S(1)} %bitcast.20, bf16[4,64,256]{2,1,0:T(8,128)(2,1)S(1)} %collective-permute-done.5.across_ref), custom_call_target="tpu_custom_call" | custom-call | tf_op jit(solution)/shard_map/pallas_call | solution.py:604
  (37 shorter events, 0.3 us)
Async XLA Ops:
  0.6 10.3 %copy-start.6 = (bf16[8,64,1536]{2,1,0:T(8,128)(2,1)S(1)}, bf16[8,64,1536]{2,1,0:T(8,128)(2,1)}, u32[]{:S(2)}) copy-start(bf16[8,64,1536]{2,1,0:T(8,128)(2,1)} %param.14) | copy-start | bytes 4718596
  3.8 29.8 %copy-start.7 = (s32[4,16,128]{2,1,0:T(8,128)S(1)}, s32[4,16,128]{2,1,0:T(8,128)}, u32[]{:S(2)}) copy-start(s32[4,16,128]{2,1,0:T(8,128)} %param.21) | copy-start | bytes 98308
  3.8 33.5 %all-to-all-start = ((bf16[8,512,128]{2,1,0:T(8,128)(2,1)}), bf16[8,512,128]{2,1,0:T(8,128)(2,1)S(1)}, u32[]{:S(2)}, u32[]{:S(2)}) async-start(bf16[8,512,128]{2,1,0:T(8,128)(2,1)} %shard_map.137), calls=%async_computation | async-start | bytes 2097152 | tf_op jit(solution)/shard_map/all_to_all | solution.py:635
  10.9 21.2 %copy-start.8 = (s32[4,16,1]{1,2,0:T(1,128)S(1)}, s32[4,16,1]{1,2,0:T(1,128)}, u32[]{:S(2)}) copy-start(s32[4,16,1]{1,2,0:T(1,128)} %param.19) | copy-start | bytes 772
  10.9 21.6 %copy-start.9 = (s32[8]{0:T(128)S(1)}, s32[8]{0:T(128)}, u32[]{:S(2)}) copy-start(s32[8]{0:T(128)} %param.20) | copy-start | bytes 100
  10.9 42.6 %copy-start.5 = (s32[2]{0:T(128)S(1)}, s32[2]{0:T(128)}, u32[]{:S(2)}) copy-start(s32[2]{0:T(128)} %pad_add_fusion.place_ref) | copy-start | bytes 28
  32.1 32.6 %copy-start = (f32[1,2,256,1024]{3,2,1,0:T(8,128)S(1)}, f32[1,2,256,1024]{3,2,1,0:T(8,128)}, u32[]{:S(2)}) copy-start(f32[1,2,256,1024]{3,2,1,0:T(8,128)} %param.17) | copy-start | bytes 6291460
  32.1 1.3 %collective-permute-start = (f32[8,1536]{1,0:T(8,128)S(1)}, f32[8,1536]{1,0:T(8,128)S(1)}, u32[]{:S(2)}, u32[]{:S(2)}) collective-permute-start(f32[8,1536]{1,0:T(8,128)S(1)} %get-tuple-element.72), channel_id=1, source_target_pairs={{0,8},{8,0},{16,24},{24,16},{1,9},{9,1},{17,25},{25,17},{2,10},{10... | collective-permute-start | bytes 147464 | tf_op jit(solution)/shard_map/ppermute | solution.py:638
  33.4 3.9 %collective-permute-start.1 = (bf16[8,1536]{1,0:T(8,128)(2,1)S(1)}, bf16[8,1536]{1,0:T(8,128)(2,1)S(1)}, u32[]{:S(2)}, u32[]{:S(2)}) collective-permute-start(bf16[8,1536]{1,0:T(8,128)(2,1)S(1)} %add_convert_fusion), channel_id=1, source_target_pairs={{0,16},{8,24},{16,0},{24,8},{1,17},{9,25},{17,1},{25,9},{2,18},{10... | collective-permute-start | bytes 73736 | tf_op jit(solution)/shard_map/ppermute | solution.py:640
  38.1 15.4 %all-to-all-start.1 = ((bf16[8,8,2560]{2,1,0:T(8,128)(2,1)}), bf16[8,8,2560]{2,1,0:T(8,128)(2,1)S(1)}, u32[]{:S(2)}, u32[]{:S(2)}) async-start(bf16[8,8,2560]{2,1,0:T(8,128)(2,1)} %broadcast_in_dim.26), calls=%async_computation.1 | async-start | bytes 655360 | tf_op jit(solution)/shard_map/all_to_all | solution.py:615
  53.5 11.1 %copy-start.1 = (bf16[1,256,1024]{2,1,0:T(8,128)(2,1)S(1)}, bf16[1,256,1024]{2,1,0:T(8,128)(2,1)}, u32[]{:S(2)}) copy-start(bf16[1,256,1024]{2,1,0:T(8,128)(2,1)} %param.18) | copy-start | bytes 1572868
  55.0 32.9 %copy-start.4 = (bf16[8,64,448]{2,1,0:T(8,128)(2,1)}, bf16[8,64,448]{2,1,0:T(8,128)(2,1)S(1)}, u32[]{:S(2)}) copy-start(bf16[8,64,448]{2,1,0:T(8,128)(2,1)S(1)} %get-tuple-element.44) | copy-start | bytes 1376260
  55.0 1.3 %collective-permute-start.2 = (f32[16,1024]{1,0:T(8,128)S(1)}, f32[16,1024]{1,0:T(8,128)S(1)}, u32[]{:S(2)}, u32[]{:S(2)}) collective-permute-start(f32[16,1024]{1,0:T(8,128)S(1)} %get-tuple-element.45), channel_id=1, source_target_pairs={{0,8},{8,0},{16,24},{24,16},{1,9},{9,1},{17,25},{25,17},{2,10},{10... | collective-permute-start | bytes 196616 | tf_op jit(solution)/shard_map/ppermute | solution.py:670
  56.3 4.3 %collective-permute-start.3 = (f32[16,1024]{1,0:T(8,128)S(1)}, f32[16,1024]{1,0:T(8,128)S(1)}, u32[]{:S(2)}, u32[]{:S(2)}) collective-permute-start(f32[16,1024]{1,0:T(8,128)S(1)} %add.41), channel_id=1, source_target_pairs={{0,16},{8,24},{16,0},{24,8},{1,17},{9,25},{17,1},{25,9},{2,18},{10... | collective-permute-start | bytes 196616 | tf_op jit(solution)/shard_map/ppermute | solution.py:671
  60.6 4.0 %collective-permute-start.4 = (f32[8,1024]{1,0:T(8,128)S(1)}, f32[8,1024]{1,0:T(8,128)S(1)}, u32[]{:S(2)}, u32[]{:S(2)}) collective-permute-start(f32[8,1024]{1,0:T(8,128)S(1)} %slice.19), channel_id=1, source_target_pairs={{0,1},{1,0},{2,3},{3,2},{4,5},{5,4},{6,7},{7,6},{8,9},{9,8},{10,11... | collective-permute-start | bytes 98312 | tf_op jit(solution)/shard_map/ppermute | solution.py:672
  87.9 5.7 %collective-permute-start.5 = (bf16[4,64,256]{2,1,0:T(8,128)(2,1)S(1)}, bf16[4,64,256]{2,1,0:T(8,128)(2,1)S(1)}, u32[]{:S(2)}, u32[]{:S(2)}) collective-permute-start(bf16[4,64,256]{2,1,0:T(8,128)(2,1)S(1)} %bitcast.19), channel_id=1, source_target_pairs={{0,1},{1,0},{2,3},{3,2},{4,5},{5,4},{6,7},{7,6},{8,9},{9,8},{10,11... | collective-permute-start | bytes 393224 | tf_op jit(solution)/shard_map/ppermute | solution.py:677

commit v3 on v2

--- a/solution.py
+++ b/solution.py
@@ -15,6 +15,8 @@
 HEAD_IMG = 64
 HEAD_TXT = 128
 CAP = 2
+IMAGE_GROUP = 4
+LOG2_E = 1.4426950408889634
 SIDES = 2
 TILE = 16
 
@@ -69,33 +71,36 @@
     item_count, model_width = pooled_ref.shape
     half_width = model_width // 2
     head_count = half_width // HEAD_IMG
-    patch_count = image_ref.shape[1]
+    group, patch_count, _ = image_ref.shape
 
     @pl.when(step == 0)
     def _():
         unfold(slot_ref, 0, w_in, wide, 128)
         unfold(slot_ref, model_width * 12, w_out, wide, 128)
 
-    tokens = image_ref[0].astype(F32)
+    tokens = image_ref[...].reshape(group * patch_count, model_width).astype(F32)
     centred = tokens - jnp.mean(tokens, axis=1, keepdims=True)
     variance = jnp.mean(centred * centred, axis=1, keepdims=True)
     normed = (centred * lax.rsqrt(variance + norm_eps)).astype(BF16)
-    queries = (dot_nn(normed, w_in[:, :half_width]).astype(BF16) * (1.0 / math.sqrt(HEAD_IMG))).astype(BF16)
+    queries = (dot_nn(normed, w_in[:, :half_width]) * (LOG2_E / math.sqrt(HEAD_IMG))).astype(BF16)
     keys = dot_nn(normed, w_in[:, half_width : 2 * half_width]).astype(BF16)
     row_ids = lax.broadcasted_iota(jnp.int32, (head_count, patch_count), 0)
-    weights = jnp.zeros((head_count, patch_count), F32)
-    for head in range(head_count):
-        span = slice(head * HEAD_IMG, (head + 1) * HEAD_IMG)
-        scores = dot_nt(keys[:, span], queries[:, span])
-        exps = jnp.exp(scores - jnp.max(scores, axis=0, keepdims=True))
-        share = (1.0 / patch_count) / jnp.sum(exps, axis=0, keepdims=True)
-        share = jnp.where(row_ids == head, share, 0.0).astype(BF16)
-        weights = weights + dot_nt(share, exps.astype(BF16))
-    heads_mean[pl.ds(step * head_count, head_count), :] = dot_two(weights, normed)
-    residual = jnp.mean(tokens, axis=0, keepdims=True) * flag_ref[0].astype(F32)
-    pooled_ref[pl.ds(step, 1), :] = residual
-
-    @pl.when(step == item_count - 1)
+    flag = flag_ref[0].astype(F32)
+    for member in range(group):
+        rows = slice(member * patch_count, (member + 1) * patch_count)
+        weights = jnp.zeros((head_count, patch_count), F32)
+        for head in range(head_count):
+            span = slice(head * HEAD_IMG, (head + 1) * HEAD_IMG)
+            scores = dot_nt(queries[rows, span], keys[rows, span])
+            exps = jnp.exp2(scores - jnp.max(scores, axis=1, keepdims=True))
+            share = (1.0 / patch_count) / jnp.sum(exps, axis=1, keepdims=True)
+            mean_share = jnp.sum(exps * share, axis=0, keepdims=True)
+            weights = weights + jnp.where(row_ids == head, mean_share, 0.0)
+        item = step * group + member
+        heads_mean[pl.ds(item * head_count, head_count), :] = dot_two(weights, normed[rows])
+        pooled_ref[pl.ds(item, 1), :] = jnp.mean(tokens[rows], axis=0, keepdims=True) * flag
+
+    @pl.when(step == item_count // group - 1)
     def _():
         values = dot_two(heads_mean[...], w_in[:, 2 * half_width :])
         rows = lax.broadcasted_iota(jnp.int32, values.shape, 0)
@@ -110,10 +115,10 @@
     head_count = half_width // HEAD_IMG
     return pl.pallas_call(
         image_kernel,
-        grid=(item_count,),
+        grid=(item_count // IMAGE_GROUP,),
         in_specs=[
             pl.BlockSpec(memory_space=pltpu.SMEM),
-            pl.BlockSpec((1, patch_count, model_width), lambda i: (i, 0, 0)),
+            pl.BlockSpec((IMAGE_GROUP, patch_count, model_width), lambda i: (i, 0, 0)),
             pl.BlockSpec((1, 16 * model_width, 128), lambda i: (0, 0, 0), pipeline_mode=pl.Buffered(1)),
         ],
         out_specs=pl.BlockSpec((item_count, model_width), lambda i: (0, 0)),
@@ -297,27 +302,25 @@
     return max([shard_rows] + [inside + width // columns * max(shares) for _, inside, _, _, shares in groups])
 
 
-def message_kernel(groups, place_ref, rows_ref, message_ref):
-    shard, segment = place_ref[0], place_ref[1]
+def message_kernel(groups, rows_ref, message_ref):
+    shard, segment = lax.axis_index("dp"), lax.axis_index("segment")
     row_count, width = rows_ref.shape
     copies, _, columns = message_ref.shape
+    segment_count = width // (SIDES * columns)
     first_last = groups[0][0]
 
-    @pl.when(shard <= first_last)
-    def _():
-        wanted = lax.broadcasted_iota(jnp.int32, (width, SIDES * columns), 1)
-        unit = jnp.zeros_like(wanted)
-        offset = 0
-        for side in range(SIDES):
-            for _, _, base, starts, shares in groups:
-                inside = (wanted >= offset) & (wanted < offset + shares[side])
-                unit = jnp.where(inside, wanted - offset + base + starts[side] + shares[side] * segment, unit)
-                offset += shares[side]
-        chosen = (lax.broadcasted_iota(jnp.int32, (width, SIDES * columns), 0) == unit).astype(F32).astype(BF16)
-        message = dot_nn(rows_ref[...], chosen).astype(BF16)
-        for copy in range(copies):
-            side = copy % SIDES
-            message_ref[copy, :row_count, :] = message[:, side * columns : (side + 1) * columns]
+    for part in range(segment_count):
+
+        @pl.when((shard <= first_last) & (segment == part))
+        def _(part=part):
+            for side in range(SIDES):
+                picked = [
+                    rows_ref[:, base + starts[side] + shares[side] * part : base + starts[side] + shares[side] * (part + 1)]
+                    for _, _, base, starts, shares in groups
+                ]
+                message = jnp.concatenate(picked, axis=1)
+                for copy in range(side, copies, SIDES):
+                    message_ref[copy, :row_count, :] = message
 
     for group_shard, inside, _, starts, shares in groups:
 
@@ -332,21 +335,20 @@
                         message_ref[copy, inside + block * share : inside + (block + 1) * share, :] = piece
 
 
-def weight_message(uniting_weights, place, groups, copies, columns):
+def weight_message(uniting_weights, groups, copies, columns):
     shard_rows, width = uniting_weights.shape
     vm = pl.BlockSpec(memory_space=pltpu.VMEM)
     return pl.pallas_call(
         functools.partial(message_kernel, groups),
-        in_specs=[pl.BlockSpec(memory_space=pltpu.SMEM), vm],
+        in_specs=[vm],
         out_specs=vm,
         out_shape=jax.ShapeDtypeStruct((copies, piece_rows(groups, shard_rows, width, columns), columns), BF16),
-    )(place, uniting_weights)
+    )(uniting_weights)
 
 
 def forward_kernel(
     groups,
     first_rows,
-    place_ref,
     embedded_ref,
     own_ref,
     weights,
@@ -380,7 +382,7 @@
     active_ref[...] = active
     for side in range(SIDES):
 
-        @pl.when(lax.rem(place_ref[0], SIDES) == side)
+        @pl.when(lax.rem(lax.axis_index("dp"), SIDES) == side)
         def _(side=side):
             offset = 0
             for block, inside, _, _, shares in groups:
@@ -394,13 +396,13 @@
     partial_ref[...] = dot_nn(dot_nn(own_ref[...], active).astype(BF16), second_ref[...])
 
 
-def merge_part(embedded_all, pieces, own, place, groups, shard_rows, first_rows, width):
+def merge_part(embedded_all, pieces, own, groups, shard_rows, first_rows, width):
     shard_count, _, columns = pieces.shape
     items = embedded_all.shape[0] * embedded_all.shape[1]
     vm = pl.BlockSpec(memory_space=pltpu.VMEM)
     return pl.pallas_call(
         functools.partial(forward_kernel, groups, first_rows),
-        in_specs=[pl.BlockSpec(memory_space=pltpu.SMEM), vm, vm, vm],
+        in_specs=[vm] * 3,
         out_specs=[vm] * 5,
         out_shape=[
             jax.ShapeDtypeStruct((shard_count, items, shard_rows), BF16),
@@ -410,7 +412,7 @@
             jax.ShapeDtypeStruct((own.shape[0], width), F32),
         ],
         compiler_params=pltpu.CompilerParams(vmem_limit_bytes=32 * 1024 * 1024),
-    )(place, embedded_all, own, pieces)
+    )(embedded_all, own, pieces)
 
 
 def split(value):
@@ -450,7 +452,7 @@
     return (dot_nt(ones, high) + dot_nt(ones, low))[:1]
 
 
-def quantizer_kernel(loss_scale, merged_ref, book_ref, bank_ref, count_ref, book_grad_ref, merged_grad_ref, loss_ref, highs, lows):
+def quantizer_kernel(loss_scale, merged_ref, book_ref, bank_ref, count_ref, merged_grad_ref, loss_ref, left_ref, right_ref, highs, lows):
     width = merged_ref.shape[1]
     levels = book_ref.shape[0]
     inverse_tau = 2.0 / math.sqrt(width)
@@ -502,20 +504,14 @@
     unit_grad = own_weight * anchor
     quantized_grad = anchor_scale * (anchor_grad - anchor * jnp.mean(anchor * anchor_grad, axis=1, keepdims=True))
     residual_grad = last * (2.0 * loss_scale / width)
-    ones = jnp.ones((rows, 128), F32)
     for level in reversed(range(levels)):
         high, low = highs[level], lows[level]
         chosen_grad = quantized_grad - residual_grad
         share_grad = exact_nt(chosen_grad, high, low)
         share = shares[level]
         logit_grad = share * (share_grad - jnp.sum(share * share_grad, axis=1, keepdims=True)) * (2.0 * inverse_tau)
-        book_part = exact_tn(
-            jnp.concatenate([share, logit_grad], axis=0), jnp.concatenate([chosen_grad, residuals[level]], axis=0)
-        )
-        totals = exact_tn(logit_grad, ones)
-        for block in range(width // 128):
-            span = slice(block * 128, (block + 1) * 128)
-            book_grad_ref[level, :, span] = book_part[:, span] - totals * book_ref[level, :, span]
+        left_ref[level] = jnp.concatenate([share, logit_grad], axis=0)
+        right_ref[level] = jnp.concatenate([chosen_grad, residuals[level]], axis=0)
         residual_grad = residual_grad + exact_nn(logit_grad, high, low)
     unit_grad = unit_grad + residual_grad
     unit = residuals[0]
@@ -524,19 +520,46 @@
 
 
 def quantizer(merged, books, bank, counts, loss_scale):
+    levels, codes, width = books.shape
+    rows = merged.shape[0]
     vm = pl.BlockSpec(memory_space=pltpu.VMEM)
     return pl.pallas_call(
         functools.partial(quantizer_kernel, loss_scale),
         in_specs=[vm] * 4,
-        out_specs=[vm] * 3,
+        out_specs=[vm] * 4,
         out_shape=[
-            jax.ShapeDtypeStruct(books.shape, F32),
             jax.ShapeDtypeStruct(merged.shape, BF16),
             jax.ShapeDtypeStruct((8, 128), F32),
+            jax.ShapeDtypeStruct((levels, 2 * rows, codes), F32),
+            jax.ShapeDtypeStruct((levels, 2 * rows, width), F32),
         ],
         scratch_shapes=[pltpu.VMEM(books.shape, BF16), pltpu.VMEM(books.shape, BF16)],
         compiler_params=pltpu.CompilerParams(vmem_limit_bytes=32 * 1024 * 1024),
     )(merged, books, bank, counts)
+
+
+def codebook_kernel(left_ref, right_ref, book_ref, grad_ref):
+    levels, doubled, _ = left_ref.shape
+    width = right_ref.shape[2]
+    rows = doubled // 2
+    ones = jnp.ones((rows, 128), F32)
+    for level in range(levels):
+        outer = exact_tn(left_ref[level], right_ref[level])
+        totals = exact_tn(left_ref[level, rows:], ones)
+        for block in range(width // 128):
+            span = slice(block * 128, (block + 1) * 128)
+            grad_ref[level, :, span] = outer[:, span] - totals * book_ref[level, :, span]
+
+
+def codebook_grad(left, right, books):
+    vm = pl.BlockSpec(memory_space=pltpu.VMEM)
+    return pl.pallas_call(
+        codebook_kernel,
+        in_specs=[vm] * 3,
+        out_specs=vm,
+        out_shape=jax.ShapeDtypeStruct(books.shape, F32),
+        compiler_params=pltpu.CompilerParams(vmem_limit_bytes=32 * 1024 * 1024),
+    )(left, right, books)
 
 
 def backward_kernel(gathered_ref, order_ref, hidden_ref, active_ref, second_ref, out_grad_ref, sent_ref):
@@ -566,23 +589,26 @@
 
 
 def weight_grad_kernel(
-    groups, place_ref, block_ref, out_grad_ref, near_ref, across_ref, grad_ref, hidden_grad, active
+    groups, block_ref, out_grad_ref, here_ref, row_ref, side_ref, corner_ref, grad_ref, hidden_grad, active
 ):
-    shard = place_ref[0]
-    segment_count, items, doubled = near_ref.shape
+    shard, segment = lax.axis_index("dp"), lax.axis_index("segment")
+    cores, items, doubled = here_ref.shape
     columns = doubled // 2
     shard_rows = block_ref.shape[1]
-    here = lax.rem(shard, SIDES)
+    own_side, own_row = lax.rem(shard, SIDES), segment // cores
+    segment_count = hidden_grad.shape[1] // (SIDES * columns)
 
     def place_units(target, first):
         for side in range(SIDES):
-            for segment in range(segment_count):
-                near = near_ref[segment, :, first : first + columns]
-                across = across_ref[segment, :, first : first + columns]
-                part = jnp.where(here == side, near, across)
+            for other in range(segment_count):
+                parts = [ref[other % cores, :, first : first + columns] for ref in (here_ref, row_ref, side_ref, corner_ref)]
+                same_row = own_row == other // cores
+                near = jnp.where(same_row, parts[0], parts[1])
+                across = jnp.where(same_row, parts[2], parts[3])
+                part = jnp.where(own_side == side, near, across)
                 offset = 0
                 for _, _, base, starts, shares in groups:
-                    spot = base + starts[side] + shares[side] * segment
+                    spot = base + starts[side] + shares[side] * other
                     target[:, spot : spot + shares[side]] = part[:, offset : offset + shares[side]]
                     offset += shares[side]
 
@@ -597,18 +623,28 @@
             grad_ref[inside:, :] = dot_tn(wanted, out_grad_ref[...])
 
 
-def weight_grad(place, block, out_grad, near, across, groups):
+def weight_grad(block, out_grad, parts, groups):
     items, shard_rows = block.shape
     width = out_grad.shape[1]
     vm = pl.BlockSpec(memory_space=pltpu.VMEM)
     return pl.pallas_call(
         functools.partial(weight_grad_kernel, groups),
-        in_specs=[pl.BlockSpec(memory_space=pltpu.SMEM)] + [vm] * 4,
+        in_specs=[vm] * (2 + len(parts)),
         out_specs=vm,
         out_shape=jax.ShapeDtypeStruct((shard_rows, width), F32),
         scratch_shapes=[pltpu.VMEM((items, width), BF16), pltpu.VMEM((items, width), BF16)],
         compiler_params=pltpu.CompilerParams(vmem_limit_bytes=32 * 1024 * 1024),
-    )(place, block, out_grad, near, across)
+    )(block, out_grad, *parts)
+
+
+def around(near, across, segment_count, dp_count):
+    row = lax.ppermute(near, "segment", [(j, j ^ 2) for j in range(segment_count)])
+    side = lax.ppermute(across, "dp", [(i, i ^ 1) for i in range(dp_count)])
+    corners = [
+        (j * dp_count + i, (j ^ 2) * dp_count + (i ^ 1)) for j in range(segment_count) for i in range(dp_count)
+    ]
+    corner = lax.ppermute(across, ("segment", "dp"), corners)
+    return row, side, corner
 
 
 def spread(rows, axis_name, count):
@@ -630,10 +666,10 @@
     shard_rows, width = uniting_weights.shape
     columns = width // (SIDES * segment_count)
     groups = unit_groups(dp_count, shard_rows, first_rows, segment_count)
-    place = jnp.stack([dp_index, segment_index]).astype(jnp.int32)
-    message = weight_message(uniting_weights, place, groups, dp_count, columns)
+    message = weight_message(uniting_weights, groups, dp_count, columns)
+    flag = (1 - segment_index % 2).astype(jnp.int32).reshape(1)
+    flag, message = lax.optimization_barrier((flag, message))
     pieces = lax.all_to_all(message, "dp", 0, 0, tiled=True)
-    flag = (1 - segment_index % 2).astype(jnp.int32).reshape(1)
     pooled = pooled_features(images, texts, section_weights, segment_index, flag)
     pooled = pooled + lax.ppermute(pooled, "segment", [(i, i ^ 1) for i in range(segment_count)])
     mine = pooled.astype(BF16)
@@ -665,18 +701,21 @@
     counts = jnp.sum((own_negatives[:, :, None] == bank_ids[None, None, :]).astype(F32), axis=1)
 
     blocks, hidden, active, second, partial = merge_part(
-        embedded_all, pieces, both_own, place, groups, shard_rows, first_rows, width
+        embedded_all, pieces, both_own, groups, shard_rows, first_rows, width
     )
     partial = partial + lax.ppermute(partial, "segment", [(i, i ^ 1) for i in range(segment_count)])
-    partial = partial + lax.ppermute(partial, "segment", [(i, i ^ 2) for i in range(segment_count)])
-    merged = partial[:owned] + lax.ppermute(partial[owned:], "dp", [(i, i ^ 1) for i in range(dp_count)])
-    book_grad, merged_grad, loss = quantizer(merged, codebooks[0], bank, counts, 1.0 / math.sqrt(items))
+    row, side, corner = around(partial[:owned], partial[owned:], segment_count, dp_count)
+    merged = (partial[:owned] + row) + (side + corner)
+    merged_grad, loss, left, right = quantizer(merged, codebooks[0], bank, counts, 1.0 / math.sqrt(items))
     gathered = spread(merged_grad, "dp", dp_count)
+    book_grad = codebook_grad(left, right, codebooks[0])
     out_grad, sent = backward_part(gathered, order, hidden, active, second)
-    near = lax.all_gather(sent, "segment", axis=0)
-    across = lax.ppermute(near, "dp", [(i, i ^ 1) for i in range(dp_count)])
+    twin = lax.ppermute(sent, "segment", [(i, i ^ 1) for i in range(segment_count)])
+    first_core = segment_index % 2 == 0
+    here = jnp.stack([jnp.where(first_core, sent, twin), jnp.where(first_core, twin, sent)])
+    parts = (here,) + around(here, here, segment_count, dp_count)
     block = lax.dynamic_index_in_dim(blocks, dp_index, 0, keepdims=False)
-    uniting_grad = weight_grad(place, block, out_grad, near, across, groups)
+    uniting_grad = weight_grad(block, out_grad, parts, groups)
     return (uniting_grad, book_grad[None], loss[0, :1])
 
 

time: 96.5 us -> 86.6 us (0.90)
  blocking collectives: 16.2 us -> 10.8 us
  waiting for transfers between devices: 25.3 us -> 21.4 us
  Pallas kernels: 34.6 us -> 30.8 us
  starting transfers between devices: 15.3 us -> 18.7 us
    ppermute x3 -> x7, waiting for transfers between devices: 10.4 us -> 4.38 us  [the longest x2 3.18 us: around(): lax.ppermute(near, 'segment', [(j, j ^ 2) for j in range(segment_count)])]
    all_gather x1 -> x0, blocking collectives: 5.43 us -> none  [per_device_parts(): near = lax.all_gather(sent, 'segment', axis=0)]
    ppermute x3 -> x7, starting transfers between devices: 2.1 us -> 7.18 us  [the longest x2 2.71 us: around(): corner = lax.ppermute(across, ('segment', 'dp'), corners)]
    all_to_all x1, waiting for transfers between devices: 0.01 us -> 1.78 us  [per_device_parts(): pieces = lax.all_to_all(message, 'dp', 0, 0, tiled=True)]
    pallas_call x1, Pallas kernels: 6.7 us -> 4.92 us  [quantizer(): pl.pallas_call(functools.partial(quantizer_kernel, loss_scale), in_specs=...]
    all_to_all x1, starting transfers between devices: 5.98 us -> 4.21 us  [spread(): lax.all_to_all(jnp.broadcast_to(rows[None], (count,) + rows.shape), axis_...]
    pallas_call x3 -> x4, Pallas kernels: 26 us -> 24.8 us  [the longest x1 18.5 us: image_pooled(): pl.pallas_call(image_kernel, grid=(item_count // IMAGE_GROUP,), in_specs=...]
  transfers between devices with their start and end apart: 8 -> 12, of which waited for: 7 -> 7; matrix products, arithmetic and copies ran while one was open for 2% -> 3% of each run, Pallas kernels for 22% -> 24%
where the time goes in v3:
time: 86.6 us; the launch traced here: 86.1 us
  Pallas kernels  30.8 us (36%)
  waiting for transfers between devices  21.4 us (25%)
  starting transfers between devices  18.7 us (22%)
  blocking collectives  10.8 us (12%)
  local copies, waits for them, and re-layouts  2.53 us (3%)
  between operations  0.91 us (1%)
    pallas_call x1, Pallas kernels, image_pooled(): pl.pallas_call(image_kernel, grid=(item_count // IMAGE_GROUP,), in_specs=...  18.5 us
    all_to_all x1, blocking collectives, spread(): lax.all_to_all(jnp.broadcast_to(rows[None], (count,) + rows.shape), axis_...  10.8 us
    all_to_all x1, waiting for transfers between devices, spread(): lax.all_to_all(jnp.broadcast_to(rows[None], (count,) + rows.shape), axis_...  9.66 us
    all_to_all x1, starting transfers between devices, per_device_parts(): pieces = lax.all_to_all(message, 'dp', 0, 0, tiled=True)  7.21 us
    pallas_call x1, Pallas kernels, quantizer(): pl.pallas_call(functools.partial(quantizer_kernel, loss_scale), in_specs=...  4.92 us
    all_to_all x1, starting transfers between devices, spread(): lax.all_to_all(jnp.broadcast_to(rows[None], (count,) + rows.shape), axis_...  4.21 us
    ppermute x1, waiting for transfers between devices, per_device_parts(): lax.ppermute(mine, 'segment', [(i, i ^ 2) for i in range(segment_count)])  3.74 us
    ppermute x2, waiting for transfers between devices, around(): lax.ppermute(near, 'segment', [(j, j ^ 2) for j in range(segment_count)])  3.18 us
  transfers between devices with their start and end apart: 12, of which 7 were waited for; matrix products, arithmetic and copies ran while one was open for 3% of the time, Pallas kernels for 24%

profile of v3, /device:TPU:0, one launch (start us, length us, event | category | flops | bytes accessed | tf_op | source)
XLA Modules:
  0.0 86.1 jit_solution(5132041529380588969)
XLA Ops:
  0.7 2.6 %shard_map.137 = bf16[8,512,128]{2,1,0:T(8,128)(2,1)} custom-call(bf16[448,1024]{1,0:T(8,128)(2,1)} %rows_ref.1), custom_call_target="tpu_custom_call" | custom-call | tf_op jit(solution)/shard_map/pallas_call | solution.py:341
  3.2 7.2 %all-to-all-start = ((bf16[8,512,128]{2,1,0:T(8,128)(2,1)}), bf16[8,512,128]{2,1,0:T(8,128)(2,1)S(1)}, u32[]{:S(2)}, u32[]{:S(2)}) async-start(bf16[8,512,128]{2,1,0:T(8,128)(2,1)} %shard_map.137), calls=%async_computation | async-start | bytes 2097152 | tf_op jit(solution)/shard_map/all_to_all | solution.py:672
  10.5 18.7 %conditional.1 = (f32[8,1536]{1,0:T(8,128)S(1)}) conditional(s32[]{:T(128)} %convert_element_type.34, (s32[1]{0:T(128)}, bf16[8,64,1536]{2,1,0:T(8,128)(2,1)S(1)}, bf16[1,21504,128]{2,1,0:T(8,128)(2,1)}) %tuple.31, (s32[1]{0:T(128)}, bf16[8,256,1024]{2,1,0:T(8,128)(2,1)}, bf16[1,21504,128]{2,1,0:T(8,128)(2,1)}) %tuple.18), branch_computations={%region_0.1_spmd.clone, %region_1.2_spmd} | conditional | bytes 2097216 | solution.py:732
  10.7 18.5 %branch_1_fun.1 = f32[8,1024]{1,0:T(8,128)S(1)} custom-call(s32[1]{0:T(128)} %get-tuple-element.24.flag_ref, bf16[8,256,1024]{2,1,0:T(8,128)(2,1)} %get-tuple-element.67.image_ref, bf16[1,21504,128]{2,1,0:T(8,128)(2,1)} %get-tuple-element.26.slot_ref), custom_call_target="tpu_custom_call" | custom-call | tf_op jit(solution)/shard_map/cond/branch_1_fun/pallas_call | solution.py:116
  29.3 0.1 copy.27
  29.5 0.1 eq.63
  29.7 0.2 select_reduce_fusion
  29.9 0.6 collective-permute-done
  30.6 3.7 %collective-permute-done.1 = bf16[8,1536]{1,0:T(8,128)(2,1)S(1)} collective-permute-done((bf16[8,1536]{1,0:T(8,128)(2,1)S(1)}, bf16[8,1536]{1,0:T(8,128)(2,1)S(1)}, u32[]{:S(2)}, u32[]{:S(2)}) %collective-permute-start.1) | collective-permute-done | bytes 24608 | tf_op jit(solution)/shard_map/ppermute | solution.py:676
  34.4 1.8 %all-to-all-done.weights = bf16[8,512,128]{2,1,0:T(8,128)(2,1)S(1)} async-done(((bf16[8,512,128]{2,1,0:T(8,128)(2,1)}), bf16[8,512,128]{2,1,0:T(8,128)(2,1)S(1)}, u32[]{:S(2)}, u32[]{:S(2)}) %all-to-all-start) | async-done | bytes 1048608 | tf_op jit(solution)/shard_map/all_to_all | solution.py:672
  36.2 0.7 broadcast_in_dim.26
  36.9 4.2 %all-to-all-start.1 = ((bf16[8,8,2560]{2,1,0:T(8,128)(2,1)}), bf16[8,8,2560]{2,1,0:T(8,128)(2,1)S(1)}, u32[]{:S(2)}, u32[]{:S(2)}) async-start(bf16[8,8,2560]{2,1,0:T(8,128)(2,1)} %broadcast_in_dim.26), calls=%async_computation.1 | async-start | bytes 655360 | tf_op jit(solution)/shard_map/all_to_all | solution.py:651
  41.2 0.1 fusion.1
  41.3 9.7 %all-to-all-done.1.embedded_ref = bf16[8,8,2560]{2,1,0:T(8,128)(2,1)S(1)} async-done(((bf16[8,8,2560]{2,1,0:T(8,128)(2,1)}), bf16[8,8,2560]{2,1,0:T(8,128)(2,1)S(1)}, u32[]{:S(2)}, u32[]{:S(2)}) %all-to-all-start.1) | async-done | bytes 327712 | tf_op jit(solution)/shard_map/all_to_all | solution.py:651
  51.0 0.8 shard_map.138
  51.8 1.2 %collective-permute-done.2 = f32[16,1024]{1,0:T(8,128)S(1)} collective-permute-done((f32[16,1024]{1,0:T(8,128)S(1)}, f32[16,1024]{1,0:T(8,128)S(1)}, u32[]{:S(2)}, u32[]{:S(2)}) %collective-permute-start.2) | collective-permute-done | bytes 65568 | tf_op jit(solution)/shard_map/ppermute | solution.py:706
  53.0 2.5 %collective-permute-start.5 = (f32[8,1024]{1,0:T(8,128)S(1)}, f32[8,1024]{1,0:T(8,128)S(1)}, u32[]{:S(2)}, u32[]{:S(2)}) collective-permute-start(f32[8,1024]{1,0:T(8,128)S(1)} %get-tuple-element.77), channel_id=1, source_target_pairs={{0,17},{1,16},{2,19},{3,18},{4,21},{5,20},{6,23},{7,22},{8,25},{9,... | collective-permute-start | bytes 98312 | tf_op jit(solution)/shard_map/ppermute | solution.py:646
  55.5 0.6 collective-permute-start.4
  56.1 0.5 collective-permute-start.3
  56.6 0.2 convert_reduce_fusion.count_ref
  56.8 3.2 %collective-permute-done.3 = f32[8,1024]{1,0:T(8,128)S(1)} collective-permute-done((f32[8,1024]{1,0:T(8,128)S(1)}, f32[8,1024]{1,0:T(8,128)S(1)}, u32[]{:S(2)}, u32[]{:S(2)}) %collective-permute-start.3) | collective-permute-done | bytes 32800 | tf_op jit(solution)/shard_map/ppermute | solution.py:641
  60.0 4.9 %shard_map.139 = (bf16[8,1024]{1,0:T(8,128)(2,1)S(1)}, f32[8,128]{1,0:T(8,128)S(1)}, f32[2,16,256]{2,1,0:T(8,128)S(1)}, f32[2,16,1024]{2,1,0:T(8,128)S(1)}) custom-call(f32[8,1024]{1,0:T(8,128)S(1)} %add_add_fusion.merged_ref, f32[2,256,1024]{2,1,0:T(8,128)S(1)} %bitcast.19, bf16[256,1024]{1,0:T(8,128)(2,1)S(1)} %bitcast.21, ...), custom_call_target="tpu_custom_call" | custom-call | tf_op jit(solution)/shard_map/pallas_call | solution.py:526
  65.0 10.8 %all_to_all.15.gathered_ref = bf16[8,8,1024]{2,1,0:T(8,128)(2,1)S(1)} all-to-all(bf16[8,8,1024]{2,1,0:T(8,128)(2,1)S(1)} %broadcast_in_dim.50), channel_id=1, replica_groups=mesh['segment'=4,'dp'=8] {'dp'}, dimensions={0} | all-to-all | bytes 262144 | tf_op jit(solution)/shard_map/all_to_all | solution.py:651
  75.8 0.4 shard_map.140
  76.2 1.2 %collective-permute-done.6 = bf16[64,256]{1,0:T(8,128)(2,1)S(1)} collective-permute-done((bf16[64,256]{1,0:T(8,128)(2,1)S(1)}, bf16[64,256]{1,0:T(8,128)(2,1)S(1)}, u32[]{:S(2)}, u32[]{:S(2)}) %collective-permute-start.6) | collective-permute-done | bytes 32800 | tf_op jit(solution)/shard_map/ppermute | solution.py:713
  77.5 0.2 collective-permute-start.9
  77.7 1.8 %collective-permute-start.8 = (bf16[2,64,256]{2,1,0:T(8,128)(2,1)S(1)}, bf16[2,64,256]{2,1,0:T(8,128)(2,1)S(1)}, u32[]{:S(2)}, u32[]{:S(2)}) collective-permute-start(bf16[2,64,256]{2,1,0:T(8,128)(2,1)S(1)} %pad_maximum_fusion.here_ref), channel_id=1, source_target_pairs={{0,1},{1,0},{2,3},{3,2},{4,5},{5,4},{6,7},{7,6},{8,9},{9,8},{10,11... | collective-permute-start | bytes 196616 | tf_op jit(solution)/shard_map/ppermute | solution.py:642
  79.5 1.5 %collective-permute-start.7 = (bf16[2,64,256]{2,1,0:T(8,128)(2,1)S(1)}, bf16[2,64,256]{2,1,0:T(8,128)(2,1)S(1)}, u32[]{:S(2)}, u32[]{:S(2)}) collective-permute-start(bf16[2,64,256]{2,1,0:T(8,128)(2,1)S(1)} %pad_maximum_fusion.here_ref), channel_id=1, source_target_pairs={{0,16},{8,24},{16,0},{24,8},{1,17},{9,25},{17,1},{25,9},{2,18},{10... | collective-permute-start | bytes 196616 | tf_op jit(solution)/shard_map/ppermute | solution.py:641
  81.0 0.8 dynamic-slice_bitcast_fusion.block_ref
  81.9 0.5 slice.16
  82.4 1.9 %shard_map.142 = f32[2,256,1024]{2,1,0:T(8,128)} custom-call(f32[2,16,256]{2,1,0:T(8,128)S(1)} %get-tuple-element.57.left_ref, f32[2,16,1024]{2,1,0:T(8,128)S(1)} %get-tuple-element.58.right_ref, f32[2,256,1024]{2,1,0:T(8,128)S(1)} %bitcast.20), custom_call_target="tpu_custom_call" | custom-call | tf_op jit(solution)/shard_map/pallas_call | solution.py:556
  84.3 1.8 %shard_map.141 = f32[448,1024]{1,0:T(8,128)} custom-call(bf16[64,448]{1,0:T(8,128)(2,1)S(1)} %dynamic-slice_bitcast_fusion.block_ref, bf16[64,1024]{1,0:T(8,128)(2,1)S(1)} %get-tuple-element.55.out_grad_ref, bf16[2,64,256]{2,1,0:T(8,128)(2,1)S(1)} %pad_maximum_fusion.here_ref, bf16[2,64,256]{2,1,0:T(8,128)(2,1)S(1)} %collective-permute-done.7.row_ref, ...), custom_call_target="tpu_custom_call" | custom-call | tf_op jit(solution)/shard_map/pallas_call | solution.py:630
  (43 shorter events, 0.6 us)
Async XLA Ops:
  0.6 9.8 %copy-start.5 = (bf16[8,64,1536]{2,1,0:T(8,128)(2,1)S(1)}, bf16[8,64,1536]{2,1,0:T(8,128)(2,1)}, u32[]{:S(2)}) copy-start(bf16[8,64,1536]{2,1,0:T(8,128)(2,1)} %param.14) | copy-start | bytes 4718596
  3.2 27.4 %copy-start.6 = (s32[4,16,128]{2,1,0:T(8,128)S(1)}, s32[4,16,128]{2,1,0:T(8,128)}, u32[]{:S(2)}) copy-start(s32[4,16,128]{2,1,0:T(8,128)} %param.21) | copy-start | bytes 98308
  3.2 33.0 %all-to-all-start = ((bf16[8,512,128]{2,1,0:T(8,128)(2,1)}), bf16[8,512,128]{2,1,0:T(8,128)(2,1)S(1)}, u32[]{:S(2)}, u32[]{:S(2)}) async-start(bf16[8,512,128]{2,1,0:T(8,128)(2,1)} %shard_map.137), calls=%async_computation | async-start | bytes 2097152 | tf_op jit(solution)/shard_map/all_to_all | solution.py:672
  10.4 18.8 %copy-start.7 = (s32[4,16,1]{1,2,0:T(1,128)S(1)}, s32[4,16,1]{1,2,0:T(1,128)}, u32[]{:S(2)}) copy-start(s32[4,16,1]{1,2,0:T(1,128)} %param.19) | copy-start | bytes 772
  10.4 19.2 %copy-start.8 = (s32[8]{0:T(128)S(1)}, s32[8]{0:T(128)}, u32[]{:S(2)}) copy-start(s32[8]{0:T(128)} %param.20) | copy-start | bytes 100
  29.2 30.9 %copy-start = (f32[1,2,256,1024]{3,2,1,0:T(8,128)S(1)}, f32[1,2,256,1024]{3,2,1,0:T(8,128)}, u32[]{:S(2)}) copy-start(f32[1,2,256,1024]{3,2,1,0:T(8,128)} %param.17) | copy-start | bytes 6291460
  29.2 1.3 %collective-permute-start = (f32[8,1536]{1,0:T(8,128)S(1)}, f32[8,1536]{1,0:T(8,128)S(1)}, u32[]{:S(2)}, u32[]{:S(2)}) collective-permute-start(f32[8,1536]{1,0:T(8,128)S(1)} %get-tuple-element.82), channel_id=1, source_target_pairs={{0,8},{8,0},{16,24},{24,16},{1,9},{9,1},{17,25},{25,17},{2,10},{10... | collective-permute-start | bytes 147464 | tf_op jit(solution)/shard_map/ppermute | solution.py:674
  30.5 3.9 %collective-permute-start.1 = (bf16[8,1536]{1,0:T(8,128)(2,1)S(1)}, bf16[8,1536]{1,0:T(8,128)(2,1)S(1)}, u32[]{:S(2)}, u32[]{:S(2)}) collective-permute-start(bf16[8,1536]{1,0:T(8,128)(2,1)S(1)} %add_convert_fusion), channel_id=1, source_target_pairs={{0,16},{8,24},{16,0},{24,8},{1,17},{9,25},{17,1},{25,9},{2,18},{10... | collective-permute-start | bytes 73736 | tf_op jit(solution)/shard_map/ppermute | solution.py:676
  36.9 14.0 %all-to-all-start.1 = ((bf16[8,8,2560]{2,1,0:T(8,128)(2,1)}), bf16[8,8,2560]{2,1,0:T(8,128)(2,1)S(1)}, u32[]{:S(2)}, u32[]{:S(2)}) async-start(bf16[8,8,2560]{2,1,0:T(8,128)(2,1)} %broadcast_in_dim.26), calls=%async_computation.1 | async-start | bytes 655360 | tf_op jit(solution)/shard_map/all_to_all | solution.py:651
  51.0 9.1 %copy-start.1 = (bf16[1,256,1024]{2,1,0:T(8,128)(2,1)S(1)}, bf16[1,256,1024]{2,1,0:T(8,128)(2,1)}, u32[]{:S(2)}) copy-start(bf16[1,256,1024]{2,1,0:T(8,128)(2,1)} %param.18) | copy-start | bytes 1572868
  51.7 24.4 %copy-start.4 = (bf16[8,64,448]{2,1,0:T(8,128)(2,1)}, bf16[8,64,448]{2,1,0:T(8,128)(2,1)S(1)}, u32[]{:S(2)}) copy-start(bf16[8,64,448]{2,1,0:T(8,128)(2,1)S(1)} %get-tuple-element.49) | copy-start | bytes 1376260
  51.7 1.3 %collective-permute-start.2 = (f32[16,1024]{1,0:T(8,128)S(1)}, f32[16,1024]{1,0:T(8,128)S(1)}, u32[]{:S(2)}, u32[]{:S(2)}) collective-permute-start(f32[16,1024]{1,0:T(8,128)S(1)} %get-tuple-element.50), channel_id=1, source_target_pairs={{0,8},{8,0},{16,24},{24,16},{1,9},{9,1},{17,25},{25,17},{2,10},{10... | collective-permute-start | bytes 196616 | tf_op jit(solution)/shard_map/ppermute | solution.py:706
  53.0 7.0 %collective-permute-start.5 = (f32[8,1024]{1,0:T(8,128)S(1)}, f32[8,1024]{1,0:T(8,128)S(1)}, u32[]{:S(2)}, u32[]{:S(2)}) collective-permute-start(f32[8,1024]{1,0:T(8,128)S(1)} %get-tuple-element.77), channel_id=1, source_target_pairs={{0,17},{1,16},{2,19},{3,18},{4,21},{5,20},{6,23},{7,22},{8,25},{9,... | collective-permute-start | bytes 98312 | tf_op jit(solution)/shard_map/ppermute | solution.py:646
  55.5 4.5 %collective-permute-start.4 = (f32[8,1024]{1,0:T(8,128)S(1)}, f32[8,1024]{1,0:T(8,128)S(1)}, u32[]{:S(2)}, u32[]{:S(2)}) collective-permute-start(f32[8,1024]{1,0:T(8,128)S(1)} %get-tuple-element.77), channel_id=1, source_target_pairs={{0,1},{1,0},{2,3},{3,2},{4,5},{5,4},{6,7},{7,6},{8,9},{9,8},{10,11... | collective-permute-start | bytes 98312 | tf_op jit(solution)/shard_map/ppermute | solution.py:642
  56.1 3.9 %collective-permute-start.3 = (f32[8,1024]{1,0:T(8,128)S(1)}, f32[8,1024]{1,0:T(8,128)S(1)}, u32[]{:S(2)}, u32[]{:S(2)}) collective-permute-start(f32[8,1024]{1,0:T(8,128)S(1)} %get-tuple-element.76), channel_id=1, source_target_pairs={{0,16},{8,24},{16,0},{24,8},{1,17},{9,25},{17,1},{25,9},{2,18},{10... | collective-permute-start | bytes 98312 | tf_op jit(solution)/shard_map/ppermute | solution.py:641
  76.2 1.3 %collective-permute-start.6 = (bf16[64,256]{1,0:T(8,128)(2,1)S(1)}, bf16[64,256]{1,0:T(8,128)(2,1)S(1)}, u32[]{:S(2)}, u32[]{:S(2)}) collective-permute-start(bf16[64,256]{1,0:T(8,128)(2,1)S(1)} %get-tuple-element.56), channel_id=1, source_target_pairs={{0,8},{8,0},{16,24},{24,16},{1,9},{9,1},{17,25},{25,17},{2,10},{10... | collective-permute-start | bytes 98312 | tf_op jit(solution)/shard_map/ppermute | solution.py:713
  77.5 6.8 %collective-permute-start.9 = (bf16[2,64,256]{2,1,0:T(8,128)(2,1)S(1)}, bf16[2,64,256]{2,1,0:T(8,128)(2,1)S(1)}, u32[]{:S(2)}, u32[]{:S(2)}) collective-permute-start(bf16[2,64,256]{2,1,0:T(8,128)(2,1)S(1)} %pad_maximum_fusion.here_ref), channel_id=1, source_target_pairs={{0,17},{1,16},{2,19},{3,18},{4,21},{5,20},{6,23},{7,22},{8,25},{9,... | collective-permute-start | bytes 196616 | tf_op jit(solution)/shard_map/ppermute | solution.py:646
  77.7 6.6 %collective-permute-start.8 = (bf16[2,64,256]{2,1,0:T(8,128)(2,1)S(1)}, bf16[2,64,256]{2,1,0:T(8,128)(2,1)S(1)}, u32[]{:S(2)}, u32[]{:S(2)}) collective-permute-start(bf16[2,64,256]{2,1,0:T(8,128)(2,1)S(1)} %pad_maximum_fusion.here_ref), channel_id=1, source_target_pairs={{0,1},{1,0},{2,3},{3,2},{4,5},{5,4},{6,7},{7,6},{8,9},{9,8},{10,11... | collective-permute-start | bytes 196616 | tf_op jit(solution)/shard_map/ppermute | solution.py:642
  79.5 4.8 %collective-permute-start.7 = (bf16[2,64,256]{2,1,0:T(8,128)(2,1)S(1)}, bf16[2,64,256]{2,1,0:T(8,128)(2,1)S(1)}, u32[]{:S(2)}, u32[]{:S(2)}) collective-permute-start(bf16[2,64,256]{2,1,0:T(8,128)(2,1)S(1)} %pad_maximum_fusion.here_ref), channel_id=1, source_target_pairs={{0,16},{8,24},{16,0},{24,8},{1,17},{9,25},{17,1},{25,9},{2,18},{10... | collective-permute-start | bytes 196616 | tf_op jit(solution)/shard_map/ppermute | solution.py:641

commit v4 on v3

--- a/solution.py
+++ b/solution.py
@@ -15,10 +15,12 @@
 HEAD_IMG = 64
 HEAD_TXT = 128
 CAP = 2
+OWNED = 4 * CAP
+MIB = 1024 * 1024
 IMAGE_GROUP = 4
 LOG2_E = 1.4426950408889634
 SIDES = 2
-TILE = 16
+TILE = 8
 
 
 norm_eps = 1e-06
@@ -262,87 +264,78 @@
     return jnp.where(in_first[:, None], first_term, second_term)
 
 
+def cost(flops, moved):
+    return pl.CostEstimate(flops=flops, bytes_accessed=moved, transcendentals=0)
+
+
 def first_rows_in(shard, shard_rows, first_rows):
     return min(max(first_rows - shard * shard_rows, 0), shard_rows)
 
 
-def unit_groups(shard_count, shard_rows, first_rows, segment_count):
-    shards = []
+def unit_groups(shard_count, shard_rows, first_rows, part_count):
+    groups = []
     for shard in range(shard_count):
         inside = first_rows_in(shard, shard_rows, first_rows)
         if inside < shard_rows:
-            shards.append((shard, inside, shard * shard_rows + inside - first_rows, shard_rows - inside))
-    tiles = [rows // (TILE * segment_count) for _, _, _, rows in shards]
-    room = sum(tiles) // SIDES
-    taken = [count // SIDES for count in tiles]
-    for index, count in enumerate(tiles):
-        if count % SIDES and sum(taken) < room:
-            taken[index] += 1
-    sides = [taken, [count - mine for count, mine in zip(tiles, taken)]]
-    groups = []
-    for index, (shard, inside, base, _) in enumerate(shards):
-        starts, shares, start = [], [], 0
-        for side in range(SIDES):
-            share = sides[side][index] * TILE
-            starts.append(start)
-            shares.append(share)
-            start += share * segment_count
-        groups.append((shard, inside, base, tuple(starts), tuple(shares)))
+            groups.append((shard, inside, shard * shard_rows + inside - first_rows, (shard_rows - inside) // part_count))
     return groups
 
 
-def even_units(groups, shard_rows, segment_count, width):
+def even_units(groups, shard_rows, part_count):
     return all(
-        inside % TILE == 0 and sum(shares) * segment_count == shard_rows - inside and min(shares) > 0
-        for _, inside, _, _, shares in groups
-    ) and all(sum(group[4][side] for group in groups) * segment_count * SIDES == width for side in range(SIDES))
-
-
-def piece_rows(groups, shard_rows, width, columns):
-    return max([shard_rows] + [inside + width // columns * max(shares) for _, inside, _, _, shares in groups])
-
-
-def message_kernel(groups, rows_ref, message_ref):
+        inside % TILE == 0 and share % TILE == 0 and inside + share * part_count == shard_rows
+        for _, inside, _, share in groups
+    )
+
+
+def message_kernel(groups, rows_ref, message_ref, built, semaphores):
     shard, segment = lax.axis_index("dp"), lax.axis_index("segment")
-    row_count, width = rows_ref.shape
     copies, _, columns = message_ref.shape
+    shard_rows, width = rows_ref.shape
     segment_count = width // (SIDES * columns)
     first_last = groups[0][0]
 
     for part in range(segment_count):
-
-        @pl.when((shard <= first_last) & (segment == part))
+        here = segment == part
+
+        @pl.when((shard <= first_last) & here)
         def _(part=part):
             for side in range(SIDES):
-                picked = [
-                    rows_ref[:, base + starts[side] + shares[side] * part : base + starts[side] + shares[side] * (part + 1)]
-                    for _, _, base, starts, shares in groups
-                ]
-                message = jnp.concatenate(picked, axis=1)
-                for copy in range(side, copies, SIDES):
-                    message_ref[copy, :row_count, :] = message
-
-    for group_shard, inside, _, starts, shares in groups:
-
-        @pl.when(shard == group_shard)
-        def _(inside=inside, starts=starts, shares=shares):
-            for side in range(SIDES):
-                share = shares[side]
-                start = pl.multiple_of(inside + starts[side] + share * segment, TILE)
-                for block in range(width // columns):
-                    piece = rows_ref[pl.ds(start, share), block * columns : (block + 1) * columns]
-                    for copy in range(side, copies, SIDES):
-                        message_ref[copy, inside + block * share : inside + (block + 1) * share, :] = piece
+                picked = []
+                for _, _, base, share in groups:
+                    start = base + share * (side * segment_count + part)
+                    picked.append(rows_ref[:, start : start + share])
+                built[side] = jnp.concatenate(picked, axis=1)
+
+        for group_shard, inside, _, share in groups:
+
+            @pl.when((shard == group_shard) & here)
+            def _(part=part, inside=inside, share=share):
+                for side in range(SIDES):
+                    start = inside + share * (side * segment_count + part)
+                    for block in range(width // columns):
+                        lanes = slice(block * columns, (block + 1) * columns)
+                        spot = inside + block * share
+                        built[side, spot : spot + share, :] = rows_ref[start : start + share, lanes]
+
+    sends = [
+        pltpu.make_async_copy(built.at[copy % SIDES], message_ref.at[copy, :shard_rows], semaphores.at[copy]) for copy in range(copies)
+    ]
+    for send in sends:
+        send.start()
+    for send in sends:
+        send.wait()
 
 
 def weight_message(uniting_weights, groups, copies, columns):
-    shard_rows, width = uniting_weights.shape
-    vm = pl.BlockSpec(memory_space=pltpu.VMEM)
+    shard_rows = uniting_weights.shape[0]
     return pl.pallas_call(
         functools.partial(message_kernel, groups),
-        in_specs=[vm],
-        out_specs=vm,
-        out_shape=jax.ShapeDtypeStruct((copies, piece_rows(groups, shard_rows, width, columns), columns), BF16),
+        in_specs=[pl.BlockSpec(memory_space=pltpu.VMEM)],
+        out_specs=pl.BlockSpec(memory_space=pl.ANY),
+        out_shape=jax.ShapeDtypeStruct((copies, shard_rows + 16, columns), BF16),
+        scratch_shapes=[pltpu.VMEM((SIDES, shard_rows, columns), BF16), pltpu.SemaphoreType.DMA((copies,))],
+        cost_estimate=cost(0, 4 * uniting_weights.size),
     )(uniting_weights)
 
 
@@ -352,20 +345,22 @@
     embedded_ref,
     own_ref,
     weights,
-    blocks_ref,
+    block_ref,
     hidden_ref,
     active_ref,
     second_ref,
     partial_ref,
 ):
     shard_count, _, columns = weights.shape
-    shard_rows = blocks_ref.shape[2]
+    shard_rows = block_ref.shape[1]
+    shard = lax.axis_index("dp")
     source_count, source_items, width = embedded_ref.shape
     items = source_count * source_items
     embedded = embedded_ref[...].astype(F32).reshape(items, width)
     normed = embedded * lax.rsqrt(jnp.mean(embedded * embedded, axis=1, keepdims=True) + norm_eps)
     normed = normed.astype(BF16)
     hidden = jnp.zeros((items, columns), F32)
+    own_block = jnp.zeros((items, shard_rows), BF16)
     for block in range(shard_count):
         inside = first_rows_in(block, shard_rows, first_rows)
         start = block * shard_rows
@@ -374,25 +369,18 @@
             hidden = hidden + dot_nn(rows, weights[block, :inside])
             if inside < shard_rows:
                 rows = jnp.concatenate([rows, jnp.zeros((items, shard_rows - inside), BF16)], axis=1)
-            blocks_ref[block] = rows
-        else:
-            blocks_ref[block] = jnp.zeros((items, shard_rows), BF16)
+            own_block = jnp.where(shard == block, rows, own_block)
+    block_ref[...] = own_block
     hidden_ref[...] = hidden
     active = gelu_value(hidden).astype(BF16)
     active_ref[...] = active
-    for side in range(SIDES):
-
-        @pl.when(lax.rem(lax.axis_index("dp"), SIDES) == side)
-        def _(side=side):
-            offset = 0
-            for block, inside, _, _, shares in groups:
-                share = shares[side]
-                for part in range(partial_ref.shape[1] // columns):
-                    second_ref[offset : offset + share, part * columns : (part + 1) * columns] = weights[
-                        block, inside + part * share : inside + (part + 1) * share, :
-                    ]
-                offset += share
-
+    offset = 0
+    for block, inside, _, share in groups:
+        for part in range(partial_ref.shape[1] // columns):
+            second_ref[offset : offset + share, part * columns : (part + 1) * columns] = weights[
+                block, inside + part * share : inside + (part + 1) * share, :
+            ]
+        offset += share
     partial_ref[...] = dot_nn(dot_nn(own_ref[...], active).astype(BF16), second_ref[...])
 
 
@@ -405,13 +393,14 @@
         in_specs=[vm] * 3,
         out_specs=[vm] * 5,
         out_shape=[
-            jax.ShapeDtypeStruct((shard_count, items, shard_rows), BF16),
+            jax.ShapeDtypeStruct((items, shard_rows), BF16),
             jax.ShapeDtypeStruct((items, columns), F32),
             jax.ShapeDtypeStruct((items, columns), BF16),
             jax.ShapeDtypeStruct((columns, width), BF16),
             jax.ShapeDtypeStruct((own.shape[0], width), F32),
         ],
-        compiler_params=pltpu.CompilerParams(vmem_limit_bytes=32 * 1024 * 1024),
+        cost_estimate=cost(2 * items * first_rows * columns, 2 * pieces.size),
+        compiler_params=pltpu.CompilerParams(vmem_limit_bytes=8 * MIB),
     )(embedded_all, own, pieces)
 
 
@@ -449,12 +438,54 @@
 def square_sums(value):
     high, low = split(value * value)
     ones = jnp.ones((8, value.shape[1]), BF16)
-    return (dot_nt(ones, high) + dot_nt(ones, low))[:1]
-
-
-def quantizer_kernel(loss_scale, merged_ref, book_ref, bank_ref, count_ref, merged_grad_ref, loss_ref, left_ref, right_ref, highs, lows):
+    return dot_nt(ones, high) + dot_nt(ones, low)
+
+
+def prepare_kernel(book_ref, bank_ref, high_ref, low_ref, norm_ref, scale_ref):
+    width = bank_ref.shape[1]
+    for level in range(book_ref.shape[0]):
+        codes = book_ref[level]
+        high, low = split(codes)
+        high_ref[level] = high
+        low_ref[level] = low
+        norm_ref[level] = square_sums(codes)
+    scale_ref[...] = lax.rsqrt(square_sums(bank_ref[...].astype(F32)) * (1.0 / width) + norm_eps)
+
+
+def prepared(books, bank):
+    levels, codes, _ = books.shape
+    vm = pl.BlockSpec(memory_space=pltpu.VMEM)
+    return pl.pallas_call(
+        prepare_kernel,
+        in_specs=[vm] * 2,
+        out_specs=[vm] * 4,
+        out_shape=[
+            jax.ShapeDtypeStruct(books.shape, BF16),
+            jax.ShapeDtypeStruct(books.shape, BF16),
+            jax.ShapeDtypeStruct((levels, 8, codes), F32),
+            jax.ShapeDtypeStruct((8, bank.shape[0]), F32),
+        ],
+        cost_estimate=cost(0, 12 * books.size),
+        compiler_params=pltpu.CompilerParams(vmem_limit_bytes=10 * MIB),
+    )(books, bank)
+
+
+def quantizer_kernel(
+    loss_scale,
+    merged_ref,
+    highs,
+    lows,
+    norm_ref,
+    bank_ref,
+    bank_scale_ref,
+    count_ref,
+    merged_grad_ref,
+    loss_ref,
+    left_ref,
+    right_ref,
+):
     width = merged_ref.shape[1]
-    levels = book_ref.shape[0]
+    levels = highs.shape[0]
     inverse_tau = 2.0 / math.sqrt(width)
     inverse_temp = 1.0 / (width * contrast_temp)
     merged = merged_ref[...].astype(BF16).astype(F32)
@@ -462,11 +493,8 @@
     residuals = [merged * merged_scale]
     shares, chosen_rows = [], []
     for level in range(levels):
-        codes = book_ref[level]
-        high, low = split(codes)
-        highs[level] = high
-        lows[level] = low
-        logits = (2.0 * exact_nt(residuals[level], high, low) - square_sums(codes)) * inverse_tau
+        high, low = highs[level], lows[level]
+        logits = (2.0 * exact_nt(residuals[level], high, low) - norm_ref[level]) * inverse_tau
         exps = jnp.exp(logits - jnp.max(logits, axis=1, keepdims=True))
         share = exps / jnp.sum(exps, axis=1, keepdims=True)
         chosen = exact_nn(share, high, low)
@@ -481,8 +509,7 @@
     anchor = quantized * anchor_scale
     own = jnp.sum(anchor * residuals[0], axis=1, keepdims=True) * inverse_temp
     bank = bank_ref[...]
-    bank_wide = bank.astype(F32)
-    bank_scale = lax.rsqrt(square_sums(bank_wide) * (1.0 / width) + norm_eps)
+    bank_scale = bank_scale_ref[...]
     anchor_parts = jnp.concatenate(split(anchor), axis=0)
     rows = anchor.shape[0]
     both = dot_nt(anchor_parts, bank)
@@ -494,7 +521,7 @@
     own_exp = jnp.exp(own - top)
     total = jnp.sum(bank_exps, axis=1, keepdims=True) + own_exp
     item_losses = top + jnp.log(total) - own + jnp.mean(last * last, axis=1, keepdims=True)
-    loss_ref[...] = jnp.broadcast_to(jnp.sum(item_losses, axis=0, keepdims=True) * loss_scale, loss_ref.shape)
+    loss_ref[0] = jnp.sum(item_losses) * loss_scale
 
     bank_weight = bank_exps / total * (loss_scale * inverse_temp)
     own_weight = (own_exp / total - 1.0) * (loss_scale * inverse_temp)
@@ -519,23 +546,24 @@
     merged_grad_ref[...] = merged_grad.astype(BF16)
 
 
-def quantizer(merged, books, bank, counts, loss_scale):
-    levels, codes, width = books.shape
+def quantizer(merged, ready, bank, counts, loss_scale):
+    highs, lows, norms, bank_scale = ready
+    levels, codes, width = highs.shape
     rows = merged.shape[0]
     vm = pl.BlockSpec(memory_space=pltpu.VMEM)
     return pl.pallas_call(
         functools.partial(quantizer_kernel, loss_scale),
-        in_specs=[vm] * 4,
-        out_specs=[vm] * 4,
+        in_specs=[vm] * 7,
+        out_specs=[vm, pl.BlockSpec(memory_space=pltpu.SMEM), vm, vm],
         out_shape=[
             jax.ShapeDtypeStruct(merged.shape, BF16),
-            jax.ShapeDtypeStruct((8, 128), F32),
+            jax.ShapeDtypeStruct((1,), F32),
             jax.ShapeDtypeStruct((levels, 2 * rows, codes), F32),
             jax.ShapeDtypeStruct((levels, 2 * rows, width), F32),
         ],
-        scratch_shapes=[pltpu.VMEM(books.shape, BF16), pltpu.VMEM(books.shape, BF16)],
-        compiler_params=pltpu.CompilerParams(vmem_limit_bytes=32 * 1024 * 1024),
-    )(merged, books, bank, counts)
+        cost_estimate=cost(64 * highs.size, 4 * highs.size),
+        compiler_params=pltpu.CompilerParams(vmem_limit_bytes=12 * MIB),
+    )(merged, highs, lows, norms, bank, bank_scale, counts)
 
 
 def codebook_kernel(left_ref, right_ref, book_ref, grad_ref):
@@ -558,7 +586,8 @@
         in_specs=[vm] * 3,
         out_specs=vm,
         out_shape=jax.ShapeDtypeStruct(books.shape, F32),
-        compiler_params=pltpu.CompilerParams(vmem_limit_bytes=32 * 1024 * 1024),
+        cost_estimate=cost(96 * books.size, 8 * books.size),
+        compiler_params=pltpu.CompilerParams(vmem_limit_bytes=10 * MIB),
     )(left, right, books)
 
 
@@ -584,7 +613,8 @@
             jax.ShapeDtypeStruct((items, gathered.shape[2]), BF16),
             jax.ShapeDtypeStruct((items, 2 * columns), BF16),
         ],
-        compiler_params=pltpu.CompilerParams(vmem_limit_bytes=32 * 1024 * 1024),
+        cost_estimate=cost(2 * items * second.size, 2 * second.size),
+        compiler_params=pltpu.CompilerParams(vmem_limit_bytes=8 * MIB),
     )(gathered, order, hidden, active, second)
 
 
@@ -607,14 +637,14 @@
                 across = jnp.where(same_row, parts[2], parts[3])
                 part = jnp.where(own_side == side, near, across)
                 offset = 0
-                for _, _, base, starts, shares in groups:
-                    spot = base + starts[side] + shares[side] * other
-                    target[:, spot : spot + shares[side]] = part[:, offset : offset + shares[side]]
-                    offset += shares[side]
+                for _, _, base, share in groups:
+                    spot = base + share * (side * segment_count + other)
+                    target[:, spot : spot + share] = part[:, offset : offset + share]
+                    offset += share
 
     place_units(hidden_grad, 0)
     grad_ref[...] = dot_tn(block_ref[...], hidden_grad[...])
-    for group_shard, inside, base, _, _ in groups:
+    for group_shard, inside, base, _ in groups:
 
         @pl.when(shard == group_shard)
         def _(inside=inside, base=base):
@@ -633,7 +663,8 @@
         out_specs=vm,
         out_shape=jax.ShapeDtypeStruct((shard_rows, width), F32),
         scratch_shapes=[pltpu.VMEM((items, width), BF16), pltpu.VMEM((items, width), BF16)],
-        compiler_params=pltpu.CompilerParams(vmem_limit_bytes=32 * 1024 * 1024),
+        cost_estimate=cost(2 * items * shard_rows * width, 4 * shard_rows * width),
+        compiler_params=pltpu.CompilerParams(vmem_limit_bytes=8 * MIB),
     )(block, out_grad, *parts)
 
 
@@ -665,7 +696,7 @@
     first_rows = image_width + text_width
     shard_rows, width = uniting_weights.shape
     columns = width // (SIDES * segment_count)
-    groups = unit_groups(dp_count, shard_rows, first_rows, segment_count)
+    groups = unit_groups(dp_count, shard_rows, first_rows, SIDES * segment_count)
     message = weight_message(uniting_weights, groups, dp_count, columns)
     flag = (1 - segment_index % 2).astype(jnp.int32).reshape(1)
     flag, message = lax.optimization_barrier((flag, message))
@@ -678,7 +709,7 @@
     embedded = jnp.concatenate(
         [jnp.where(is_image, mine, other)[:, :image_width], jnp.where(is_image, other, mine)], axis=1
     )
-    embedded, pieces = lax.optimization_barrier((embedded, pieces))
+    embedded, pieces, books = lax.optimization_barrier((embedded, pieces, codebooks[0]))
     embedded_all = spread(embedded, "dp", dp_count)
 
     pair = item_cats.shape[1] // dp_count
@@ -697,26 +728,26 @@
     negatives = neg_index.reshape(segment_count, dp_count, pair, -1).transpose(1, 0, 2, 3).reshape(items, -1)
     own_negatives = jnp.dot(own.astype(F32), negatives.astype(F32), precision=highest)
     bank = neg_bank[0]
+    ready = prepared(books, bank)
     bank_ids = jnp.arange(bank.shape[0]).astype(F32)
     counts = jnp.sum((own_negatives[:, :, None] == bank_ids[None, None, :]).astype(F32), axis=1)
 
-    blocks, hidden, active, second, partial = merge_part(
+    block, hidden, active, second, partial = merge_part(
         embedded_all, pieces, both_own, groups, shard_rows, first_rows, width
     )
     partial = partial + lax.ppermute(partial, "segment", [(i, i ^ 1) for i in range(segment_count)])
     row, side, corner = around(partial[:owned], partial[owned:], segment_count, dp_count)
     merged = (partial[:owned] + row) + (side + corner)
-    merged_grad, loss, left, right = quantizer(merged, codebooks[0], bank, counts, 1.0 / math.sqrt(items))
+    merged_grad, loss, left, right = quantizer(merged, ready, bank, counts, 1.0 / math.sqrt(items))
     gathered = spread(merged_grad, "dp", dp_count)
-    book_grad = codebook_grad(left, right, codebooks[0])
+    book_grad = codebook_grad(left, right, books)
     out_grad, sent = backward_part(gathered, order, hidden, active, second)
     twin = lax.ppermute(sent, "segment", [(i, i ^ 1) for i in range(segment_count)])
     first_core = segment_index % 2 == 0
     here = jnp.stack([jnp.where(first_core, sent, twin), jnp.where(first_core, twin, sent)])
     parts = (here,) + around(here, here, segment_count, dp_count)
-    block = lax.dynamic_index_in_dim(blocks, dp_index, 0, keepdims=False)
     uniting_grad = weight_grad(block, out_grad, parts, groups)
-    return (uniting_grad, book_grad[None], loss[0, :1])
+    return (uniting_grad, book_grad[None], loss)
 
 
 def pooled_features(images, texts, section_weights, segment_index, flag):
@@ -833,8 +864,8 @@
     segment_count, dp_count = lax.axis_size("segment"), lax.axis_size("dp")
     shard_rows = uniting_weights.shape[0]
     first_rows = images.shape[2] + texts.shape[2]
-    groups = unit_groups(dp_count, shard_rows, first_rows, segment_count)
-    if dp_count % SIDES == 0 and even_units(groups, shard_rows, segment_count, uniting_weights.shape[1]):
+    groups = unit_groups(dp_count, shard_rows, first_rows, SIDES * segment_count)
+    if dp_count % SIDES == 0 and even_units(groups, shard_rows, SIDES * segment_count):
         return per_device_parts(*operands)
     return per_device_gathered(*operands)
 

time: 86.6 us -> 84.6 us (0.977)
  waiting for transfers between devices: 21.4 us -> 18 us
  starting transfers between devices: 18.7 us -> 20.3 us
    ppermute x2, waiting for transfers between devices: 3.18 us -> 0.75 us  [around(): lax.ppermute(near, 'segment', [(j, j ^ 2) for j in range(segment_count)])]
    all_to_all x1, waiting for transfers between devices: 1.78 us -> 0.01 us  [per_device_parts(): pieces = lax.all_to_all(message, 'dp', 0, 0, tiled=True)]
    all_to_all x1, starting transfers between devices: 4.21 us -> 5.97 us  [spread(): lax.all_to_all(jnp.broadcast_to(rows[None], (count,) + rows.shape), axis_...]
    pallas_call x1 -> x2, Pallas kernels: 2.56 us -> 3.65 us  [the longest x1 2.59 us: weight_message(): pl.pallas_call(functools.partial(message_kernel, groups), in_specs=[pl.Bl...]
    unnamed x15, local copies, waits for them, and re-layouts: 0.12 us -> 1.15 us
    pallas_call x1, Pallas kernels: 4.92 us -> 4.03 us  [quantizer(): pl.pallas_call(functools.partial(quantizer_kernel, loss_scale), in_specs=...]
  transfers between devices with their start and end apart: 12 -> 12, of which waited for: 7 -> 8; matrix products, arithmetic and copies ran while one was open for 3% -> 1% of each run, Pallas kernels for 24% -> 25%
where the time goes in v4:
time: 84.6 us; the launch traced here: 84.1 us
  Pallas kernels  31 us (37%)
  starting transfers between devices  20.3 us (24%)
  waiting for transfers between devices  18 us (21%)
  blocking collectives  10.8 us (13%)
  local copies, waits for them, and re-layouts  2.2 us (3%)
  between operations  0.96 us (1%)
    pallas_call x1, Pallas kernels, image_pooled(): pl.pallas_call(image_kernel, grid=(item_count // IMAGE_GROUP,), in_specs=...  18.5 us
    all_to_all x1, blocking collectives, spread(): lax.all_to_all(jnp.broadcast_to(rows[None], (count,) + rows.shape), axis_...  10.8 us
    all_to_all x1, waiting for transfers between devices, spread(): lax.all_to_all(jnp.broadcast_to(rows[None], (count,) + rows.shape), axis_...  9.29 us
    all_to_all x1, starting transfers between devices, per_device_parts(): pieces = lax.all_to_all(message, 'dp', 0, 0, tiled=True)  7.04 us
    all_to_all x1, starting transfers between devices, spread(): lax.all_to_all(jnp.broadcast_to(rows[None], (count,) + rows.shape), axis_...  5.97 us
    pallas_call x1, Pallas kernels, quantizer(): pl.pallas_call(functools.partial(quantizer_kernel, loss_scale), in_specs=...  4.03 us
    ppermute x1, waiting for transfers between devices, per_device_parts(): lax.ppermute(mine, 'segment', [(i, i ^ 2) for i in range(segment_count)])  3.74 us
    pallas_call x1, Pallas kernels, weight_message(): pl.pallas_call(functools.partial(message_kernel, groups), in_specs=[pl.Bl...  2.59 us
  transfers between devices with their start and end apart: 12, of which 8 were waited for; matrix products, arithmetic and copies ran while one was open for 1% of the time, Pallas kernels for 25%

profile of v4, /device:TPU:0, one launch (start us, length us, event | category | flops | bytes accessed | tf_op | source)
XLA Modules:
  0.0 84.1 jit_solution(8637257004699903360)
XLA Ops:
  0.7 2.6 %shard_map.137 = bf16[8,464,128]{2,1,0:T(8,128)(2,1)} custom-call(bf16[448,1024]{1,0:T(8,128)(2,1)} %rows_ref.1), custom_call_target="tpu_custom_call" | custom-call | bytes 1835008 | tf_op jit(solution)/shard_map/pallas_call | solution.py:332
  3.3 7.0 %all-to-all-start = ((bf16[8,464,128]{2,1,0:T(8,128)(2,1)}), bf16[8,464,128]{2,1,0:T(8,128)(2,1)S(1)}, u32[]{:S(2)}, u32[]{:S(2)}) async-start(bf16[8,464,128]{2,1,0:T(8,128)(2,1)} %shard_map.137), calls=%async_computation | async-start | bytes 1900544 | tf_op jit(solution)/shard_map/all_to_all | solution.py:703
  10.3 18.7 %conditional.1 = (f32[8,1536]{1,0:T(8,128)S(1)}) conditional(s32[]{:T(128)} %convert_element_type.34, (s32[1]{0:T(128)}, bf16[8,64,1536]{2,1,0:T(8,128)(2,1)S(1)}, bf16[1,21504,128]{2,1,0:T(8,128)(2,1)}) %tuple.31, (s32[1]{0:T(128)}, bf16[8,256,1024]{2,1,0:T(8,128)(2,1)}, bf16[1,21504,128]{2,1,0:T(8,128)(2,1)}) %tuple.18), branch_computations={%region_0.1_spmd.clone, %region_1.2_spmd} | conditional | bytes 2097216 | solution.py:763
  10.5 18.5 %branch_1_fun.1 = f32[8,1024]{1,0:T(8,128)S(1)} custom-call(s32[1]{0:T(128)} %get-tuple-element.24.flag_ref, bf16[8,256,1024]{2,1,0:T(8,128)(2,1)} %get-tuple-element.77.image_ref, bf16[1,21504,128]{2,1,0:T(8,128)(2,1)} %get-tuple-element.26.slot_ref), custom_call_target="tpu_custom_call" | custom-call | tf_op jit(solution)/shard_map/cond/branch_1_fun/pallas_call | solution.py:118
  29.2 0.1 copy.27
  29.6 0.2 select_reduce_fusion
  29.8 0.6 collective-permute-done
  30.5 3.7 %collective-permute-done.1 = bf16[8,1536]{1,0:T(8,128)(2,1)S(1)} collective-permute-done((bf16[8,1536]{1,0:T(8,128)(2,1)S(1)}, bf16[8,1536]{1,0:T(8,128)(2,1)S(1)}, u32[]{:S(2)}, u32[]{:S(2)}) %collective-permute-start.1) | collective-permute-done | bytes 24608 | tf_op jit(solution)/shard_map/ppermute | solution.py:707
  34.3 0.7 broadcast_in_dim.26
  35.1 6.0 %all-to-all-start.1 = ((bf16[8,8,2560]{2,1,0:T(8,128)(2,1)}), bf16[8,8,2560]{2,1,0:T(8,128)(2,1)S(1)}, u32[]{:S(2)}, u32[]{:S(2)}) async-start(bf16[8,8,2560]{2,1,0:T(8,128)(2,1)} %broadcast_in_dim.26), calls=%async_computation.1 | async-start | bytes 655360 | tf_op jit(solution)/shard_map/all_to_all | solution.py:682
  41.1 0.1 fusion.1
  41.2 9.3 %all-to-all-done.1.embedded_ref = bf16[8,8,2560]{2,1,0:T(8,128)(2,1)S(1)} async-done(((bf16[8,8,2560]{2,1,0:T(8,128)(2,1)}), bf16[8,8,2560]{2,1,0:T(8,128)(2,1)S(1)}, u32[]{:S(2)}, u32[]{:S(2)}) %all-to-all-start.1) | async-done | bytes 327712 | tf_op jit(solution)/shard_map/all_to_all | solution.py:682
  50.5 0.7 shard_map.138
  51.2 1.3 %collective-permute-done.2 = f32[16,1024]{1,0:T(8,128)S(1)} collective-permute-done((f32[16,1024]{1,0:T(8,128)S(1)}, f32[16,1024]{1,0:T(8,128)S(1)}, u32[]{:S(2)}, u32[]{:S(2)}) %collective-permute-start.2) | collective-permute-done | bytes 65568 | tf_op jit(solution)/shard_map/ppermute | solution.py:738
  52.5 1.3 %collective-permute-start.5 = (f32[8,1024]{1,0:T(8,128)S(1)}, f32[8,1024]{1,0:T(8,128)S(1)}, u32[]{:S(2)}, u32[]{:S(2)}) collective-permute-start(f32[8,1024]{1,0:T(8,128)S(1)} %get-tuple-element.87), channel_id=1, source_target_pairs={{0,17},{1,16},{2,19},{3,18},{4,21},{5,20},{6,23},{7,22},{8,25},{9,... | collective-permute-start | bytes 98312 | tf_op jit(solution)/shard_map/ppermute | solution.py:677
  53.8 0.5 collective-permute-start.4
  54.3 1.8 %collective-permute-start.3 = (f32[8,1024]{1,0:T(8,128)S(1)}, f32[8,1024]{1,0:T(8,128)S(1)}, u32[]{:S(2)}, u32[]{:S(2)}) collective-permute-start(f32[8,1024]{1,0:T(8,128)S(1)} %get-tuple-element.86), channel_id=1, source_target_pairs={{0,16},{8,24},{16,0},{24,8},{1,17},{9,25},{17,1},{25,9},{2,18},{10... | collective-permute-start | bytes 98312 | tf_op jit(solution)/shard_map/ppermute | solution.py:672
  56.0 0.2 convert_reduce_fusion.count_ref
  56.3 1.0 %copy-done.1 = bf16[1,256,1024]{2,1,0:T(8,128)(2,1)S(1)} copy-done((bf16[1,256,1024]{2,1,0:T(8,128)(2,1)S(1)}, bf16[1,256,1024]{2,1,0:T(8,128)(2,1)}, u32[]{:S(2)}) %copy-start.1) | copy-done | bytes 524312
  57.3 1.1 %shard_map.139 = (bf16[2,256,1024]{2,1,0:T(8,128)(2,1)S(1)}, bf16[2,256,1024]{2,1,0:T(8,128)(2,1)S(1)}, f32[2,8,256]{2,1,0:T(8,128)S(1)}, f32[8,256]{1,0:T(8,128)S(1)}) custom-call(f32[2,256,1024]{2,1,0:T(8,128)S(1)} %bitcast.16, bf16[256,1024]{1,0:T(8,128)(2,1)S(1)} %bitcast.18), custom_call_target="tpu_custom_call" | custom-call | bytes 6291456 | tf_op jit(solution)/shard_map/pallas_call | solution.py:458
  58.5 4.0 %shard_map.140 = (bf16[8,1024]{1,0:T(8,128)(2,1)S(1)}, f32[1]{0:T(128)}, f32[2,16,256]{2,1,0:T(8,128)S(1)}, f32[2,16,1024]{2,1,0:T(8,128)S(1)}) custom-call(f32[8,1024]{1,0:T(8,128)S(1)} %add_add_fusion.merged_ref, bf16[2,256,1024]{2,1,0:T(8,128)(2,1)S(1)} %get-tuple-element.57.highs, bf16[2,256,1024]{2,1,0:T(8,128)(2,1)S(1)} %get-tuple-element.58.lows, ...), custom_call_target="tpu_custom_call" | custom-call | flops 33554432 | bytes 2097152 | tf_op jit(solution)/shard_map/pallas_call | solution.py:554
  62.5 10.8 %all_to_all.15.gathered_ref = bf16[8,8,1024]{2,1,0:T(8,128)(2,1)S(1)} all-to-all(bf16[8,8,1024]{2,1,0:T(8,128)(2,1)S(1)} %broadcast_in_dim.50), channel_id=1, replica_groups=mesh['segment'=4,'dp'=8] {'dp'}, dimensions={0} | all-to-all | bytes 262144 | tf_op jit(solution)/shard_map/all_to_all | solution.py:682
  73.3 0.4 shard_map.141
  73.7 1.2 %collective-permute-done.6 = bf16[64,256]{1,0:T(8,128)(2,1)S(1)} collective-permute-done((bf16[64,256]{1,0:T(8,128)(2,1)S(1)}, bf16[64,256]{1,0:T(8,128)(2,1)S(1)}, u32[]{:S(2)}, u32[]{:S(2)}) %collective-permute-start.6) | collective-permute-done | bytes 32800 | tf_op jit(solution)/shard_map/ppermute | solution.py:745
  75.0 1.2 %collective-permute-start.9 = (bf16[2,64,256]{2,1,0:T(8,128)(2,1)S(1)}, bf16[2,64,256]{2,1,0:T(8,128)(2,1)S(1)}, u32[]{:S(2)}, u32[]{:S(2)}) collective-permute-start(bf16[2,64,256]{2,1,0:T(8,128)(2,1)S(1)} %pad_maximum_fusion.here_ref), channel_id=1, source_target_pairs={{0,17},{1,16},{2,19},{3,18},{4,21},{5,20},{6,23},{7,22},{8,25},{9,... | collective-permute-start | bytes 196616 | tf_op jit(solution)/shard_map/ppermute | solution.py:677
  76.2 1.8 %collective-permute-start.8 = (bf16[2,64,256]{2,1,0:T(8,128)(2,1)S(1)}, bf16[2,64,256]{2,1,0:T(8,128)(2,1)S(1)}, u32[]{:S(2)}, u32[]{:S(2)}) collective-permute-start(bf16[2,64,256]{2,1,0:T(8,128)(2,1)S(1)} %pad_maximum_fusion.here_ref), channel_id=1, source_target_pairs={{0,1},{1,0},{2,3},{3,2},{4,5},{5,4},{6,7},{7,6},{8,9},{9,8},{10,11... | collective-permute-start | bytes 196616 | tf_op jit(solution)/shard_map/ppermute | solution.py:673
  78.0 0.5 collective-permute-start.7
  78.5 1.9 %shard_map.143 = f32[2,256,1024]{2,1,0:T(8,128)} custom-call(f32[2,16,256]{2,1,0:T(8,128)S(1)} %get-tuple-element.67.left_ref, f32[2,16,1024]{2,1,0:T(8,128)S(1)} %get-tuple-element.68.right_ref, f32[2,256,1024]{2,1,0:T(8,128)S(1)} %bitcast.17), custom_call_target="tpu_custom_call" | custom-call | flops 50331648 | bytes 4194304 | tf_op jit(solution)/shard_map/pallas_call | solution.py:584
  80.4 0.5 collective-permute-done.9.corner_ref
  80.9 0.7 collective-permute-done.8.side_ref
  81.5 0.7 collective-permute-done.7.row_ref
  82.3 1.8 %shard_map.142 = f32[448,1024]{1,0:T(8,128)} custom-call(bf16[64,448]{1,0:T(8,128)(2,1)S(1)} %get-tuple-element.54.block_ref, bf16[64,1024]{1,0:T(8,128)(2,1)S(1)} %get-tuple-element.65.out_grad_ref, bf16[2,64,256]{2,1,0:T(8,128)(2,1)S(1)} %pad_maximum_fusion.here_ref, bf16[2,64,256]{2,1,0:T(8,128)(2,1)S(1)} %collective-permute-done.7.row_ref, ...), custom_call_target="tpu_custom_call" | custom-call | flops 58720256 | bytes 1835008 | tf_op jit(solution)/shard_map/pallas_call | solution.py:660
  (42 shorter events, 0.7 us)
Async XLA Ops:
  0.6 9.7 %copy-start.5 = (bf16[8,64,1536]{2,1,0:T(8,128)(2,1)S(1)}, bf16[8,64,1536]{2,1,0:T(8,128)(2,1)}, u32[]{:S(2)}) copy-start(bf16[8,64,1536]{2,1,0:T(8,128)(2,1)} %param.14) | copy-start | bytes 4718596
  3.3 27.2 %copy-start.6 = (s32[4,16,128]{2,1,0:T(8,128)S(1)}, s32[4,16,128]{2,1,0:T(8,128)}, u32[]{:S(2)}) copy-start(s32[4,16,128]{2,1,0:T(8,128)} %param.21) | copy-start | bytes 98308
  3.3 31.0 %all-to-all-start = ((bf16[8,464,128]{2,1,0:T(8,128)(2,1)}), bf16[8,464,128]{2,1,0:T(8,128)(2,1)S(1)}, u32[]{:S(2)}, u32[]{:S(2)}) async-start(bf16[8,464,128]{2,1,0:T(8,128)(2,1)} %shard_map.137), calls=%async_computation | async-start | bytes 1900544 | tf_op jit(solution)/shard_map/all_to_all | solution.py:703
  10.3 18.8 %copy-start.7 = (s32[4,16,1]{1,2,0:T(1,128)S(1)}, s32[4,16,1]{1,2,0:T(1,128)}, u32[]{:S(2)}) copy-start(s32[4,16,1]{1,2,0:T(1,128)} %param.19) | copy-start | bytes 772
  10.3 19.2 %copy-start.8 = (s32[8]{0:T(128)S(1)}, s32[8]{0:T(128)}, u32[]{:S(2)}) copy-start(s32[8]{0:T(128)} %param.20) | copy-start | bytes 100
  29.1 27.2 %copy-start = (f32[1,2,256,1024]{3,2,1,0:T(8,128)S(1)}, f32[1,2,256,1024]{3,2,1,0:T(8,128)}, u32[]{:S(2)}) copy-start(f32[1,2,256,1024]{3,2,1,0:T(8,128)} %param.17) | copy-start | bytes 6291460
  29.1 1.3 %collective-permute-start = (f32[8,1536]{1,0:T(8,128)S(1)}, f32[8,1536]{1,0:T(8,128)S(1)}, u32[]{:S(2)}, u32[]{:S(2)}) collective-permute-start(f32[8,1536]{1,0:T(8,128)S(1)} %get-tuple-element.92), channel_id=1, source_target_pairs={{0,8},{8,0},{16,24},{24,16},{1,9},{9,1},{17,25},{25,17},{2,10},{10... | collective-permute-start | bytes 147464 | tf_op jit(solution)/shard_map/ppermute | solution.py:705
  30.4 3.9 %collective-permute-start.1 = (bf16[8,1536]{1,0:T(8,128)(2,1)S(1)}, bf16[8,1536]{1,0:T(8,128)(2,1)S(1)}, u32[]{:S(2)}, u32[]{:S(2)}) collective-permute-start(bf16[8,1536]{1,0:T(8,128)(2,1)S(1)} %add_convert_fusion), channel_id=1, source_target_pairs={{0,16},{8,24},{16,0},{24,8},{1,17},{9,25},{17,1},{25,9},{2,18},{10... | collective-permute-start | bytes 73736 | tf_op jit(solution)/shard_map/ppermute | solution.py:707
  35.1 15.4 %all-to-all-start.1 = ((bf16[8,8,2560]{2,1,0:T(8,128)(2,1)}), bf16[8,8,2560]{2,1,0:T(8,128)(2,1)S(1)}, u32[]{:S(2)}, u32[]{:S(2)}) async-start(bf16[8,8,2560]{2,1,0:T(8,128)(2,1)} %broadcast_in_dim.26), calls=%async_computation.1 | async-start | bytes 655360 | tf_op jit(solution)/shard_map/all_to_all | solution.py:682
  50.5 8.0 %copy-start.2 = (bf16[1,256,1024]{2,1,0:T(8,128)(2,1)S(1)}, bf16[1,256,1024]{2,1,0:T(8,128)(2,1)}, u32[]{:S(2)}) copy-start(bf16[1,256,1024]{2,1,0:T(8,128)(2,1)} %param.18) | copy-start | bytes 1572868
  51.2 1.3 %collective-permute-start.2 = (f32[16,1024]{1,0:T(8,128)S(1)}, f32[16,1024]{1,0:T(8,128)S(1)}, u32[]{:S(2)}, u32[]{:S(2)}) collective-permute-start(f32[16,1024]{1,0:T(8,128)S(1)} %get-tuple-element.55), channel_id=1, source_target_pairs={{0,8},{8,0},{16,24},{24,16},{1,9},{9,1},{17,25},{25,17},{2,10},{10... | collective-permute-start | bytes 196616 | tf_op jit(solution)/shard_map/ppermute | solution.py:738
  52.5 5.9 %collective-permute-start.5 = (f32[8,1024]{1,0:T(8,128)S(1)}, f32[8,1024]{1,0:T(8,128)S(1)}, u32[]{:S(2)}, u32[]{:S(2)}) collective-permute-start(f32[8,1024]{1,0:T(8,128)S(1)} %get-tuple-element.87), channel_id=1, source_target_pairs={{0,17},{1,16},{2,19},{3,18},{4,21},{5,20},{6,23},{7,22},{8,25},{9,... | collective-permute-start | bytes 98312 | tf_op jit(solution)/shard_map/ppermute | solution.py:677
  53.8 4.7 %collective-permute-start.4 = (f32[8,1024]{1,0:T(8,128)S(1)}, f32[8,1024]{1,0:T(8,128)S(1)}, u32[]{:S(2)}, u32[]{:S(2)}) collective-permute-start(f32[8,1024]{1,0:T(8,128)S(1)} %get-tuple-element.87), channel_id=1, source_target_pairs={{0,1},{1,0},{2,3},{3,2},{4,5},{5,4},{6,7},{7,6},{8,9},{9,8},{10,11... | collective-permute-start | bytes 98312 | tf_op jit(solution)/shard_map/ppermute | solution.py:673
  54.3 4.1 %collective-permute-start.3 = (f32[8,1024]{1,0:T(8,128)S(1)}, f32[8,1024]{1,0:T(8,128)S(1)}, u32[]{:S(2)}, u32[]{:S(2)}) collective-permute-start(f32[8,1024]{1,0:T(8,128)S(1)} %get-tuple-element.86), channel_id=1, source_target_pairs={{0,16},{8,24},{16,0},{24,8},{1,17},{9,25},{17,1},{25,9},{2,18},{10... | collective-permute-start | bytes 98312 | tf_op jit(solution)/shard_map/ppermute | solution.py:672
  56.3 1.0 %copy-start.1 = (bf16[1,256,1024]{2,1,0:T(8,128)(2,1)S(1)}, bf16[1,256,1024]{2,1,0:T(8,128)(2,1)}, u32[]{:S(2)}) copy-start(bf16[1,256,1024]{2,1,0:T(8,128)(2,1)} %param.18) | copy-start | bytes 1572868
  73.7 1.3 %collective-permute-start.6 = (bf16[64,256]{1,0:T(8,128)(2,1)S(1)}, bf16[64,256]{1,0:T(8,128)(2,1)S(1)}, u32[]{:S(2)}, u32[]{:S(2)}) collective-permute-start(bf16[64,256]{1,0:T(8,128)(2,1)S(1)} %get-tuple-element.66), channel_id=1, source_target_pairs={{0,8},{8,0},{16,24},{24,16},{1,9},{9,1},{17,25},{25,17},{2,10},{10... | collective-permute-start | bytes 98312 | tf_op jit(solution)/shard_map/ppermute | solution.py:745
  75.0 5.9 %collective-permute-start.9 = (bf16[2,64,256]{2,1,0:T(8,128)(2,1)S(1)}, bf16[2,64,256]{2,1,0:T(8,128)(2,1)S(1)}, u32[]{:S(2)}, u32[]{:S(2)}) collective-permute-start(bf16[2,64,256]{2,1,0:T(8,128)(2,1)S(1)} %pad_maximum_fusion.here_ref), channel_id=1, source_target_pairs={{0,17},{1,16},{2,19},{3,18},{4,21},{5,20},{6,23},{7,22},{8,25},{9,... | collective-permute-start | bytes 196616 | tf_op jit(solution)/shard_map/ppermute | solution.py:677
  76.2 5.4 %collective-permute-start.8 = (bf16[2,64,256]{2,1,0:T(8,128)(2,1)S(1)}, bf16[2,64,256]{2,1,0:T(8,128)(2,1)S(1)}, u32[]{:S(2)}, u32[]{:S(2)}) collective-permute-start(bf16[2,64,256]{2,1,0:T(8,128)(2,1)S(1)} %pad_maximum_fusion.here_ref), channel_id=1, source_target_pairs={{0,1},{1,0},{2,3},{3,2},{4,5},{5,4},{6,7},{7,6},{8,9},{9,8},{10,11... | collective-permute-start | bytes 196616 | tf_op jit(solution)/shard_map/ppermute | solution.py:673
  78.0 4.3 %collective-permute-start.7 = (bf16[2,64,256]{2,1,0:T(8,128)(2,1)S(1)}, bf16[2,64,256]{2,1,0:T(8,128)(2,1)S(1)}, u32[]{:S(2)}, u32[]{:S(2)}) collective-permute-start(bf16[2,64,256]{2,1,0:T(8,128)(2,1)S(1)} %pad_maximum_fusion.here_ref), channel_id=1, source_target_pairs={{0,16},{8,24},{16,0},{24,8},{1,17},{9,25},{17,1},{25,9},{2,18},{10... | collective-permute-start | bytes 196616 | tf_op jit(solution)/shard_map/ppermute | solution.py:672

commit v5 on v4

--- a/solution.py
+++ b/solution.py
@@ -342,7 +342,8 @@
 def forward_kernel(
     groups,
     first_rows,
-    embedded_ref,
+    mine_ref,
+    twin_ref,
     own_ref,
     weights,
     block_ref,
@@ -354,9 +355,12 @@
     shard_count, _, columns = weights.shape
     shard_rows = block_ref.shape[1]
     shard = lax.axis_index("dp")
-    source_count, source_items, width = embedded_ref.shape
-    items = source_count * source_items
-    embedded = embedded_ref[...].astype(F32).reshape(items, width)
+    source_count, source_items, half = mine_ref.shape
+    items, width = source_count * source_items, 2 * half
+    mine = mine_ref[...].astype(F32).reshape(items, half)
+    twin = twin_ref[...].astype(F32).reshape(items, half)
+    first_core = lax.rem(lax.axis_index("segment"), 2) == 0
+    embedded = jnp.concatenate([jnp.where(first_core, mine, twin), jnp.where(first_core, twin, mine)], axis=1)
     normed = embedded * lax.rsqrt(jnp.mean(embedded * embedded, axis=1, keepdims=True) + norm_eps)
     normed = normed.astype(BF16)
     hidden = jnp.zeros((items, columns), F32)
@@ -384,13 +388,13 @@
     partial_ref[...] = dot_nn(dot_nn(own_ref[...], active).astype(BF16), second_ref[...])
 
 
-def merge_part(embedded_all, pieces, own, groups, shard_rows, first_rows, width):
+def merge_part(mine_half, twin_half, pieces, own, groups, shard_rows, first_rows, width):
     shard_count, _, columns = pieces.shape
-    items = embedded_all.shape[0] * embedded_all.shape[1]
+    items = mine_half.shape[0] * mine_half.shape[1]
     vm = pl.BlockSpec(memory_space=pltpu.VMEM)
     return pl.pallas_call(
         functools.partial(forward_kernel, groups, first_rows),
-        in_specs=[vm] * 3,
+        in_specs=[vm] * 4,
         out_specs=[vm] * 5,
         out_shape=[
             jax.ShapeDtypeStruct((items, shard_rows), BF16),
@@ -401,7 +405,7 @@
         ],
         cost_estimate=cost(2 * items * first_rows * columns, 2 * pieces.size),
         compiler_params=pltpu.CompilerParams(vmem_limit_bytes=8 * MIB),
-    )(embedded_all, own, pieces)
+    )(mine_half, twin_half, own, pieces)
 
 
 def split(value):
@@ -619,10 +623,12 @@
 
 
 def weight_grad_kernel(
-    groups, block_ref, out_grad_ref, here_ref, row_ref, side_ref, corner_ref, grad_ref, hidden_grad, active
+    groups, block_ref, out_grad_ref, mine_ref, twin_ref, grad_ref, hidden_grad, active
 ):
     shard, segment = lax.axis_index("dp"), lax.axis_index("segment")
-    cores, items, doubled = here_ref.shape
+    _, items, doubled = mine_ref.shape
+    cores = 2
+    own_core = lax.rem(segment, cores)
     columns = doubled // 2
     shard_rows = block_ref.shape[1]
     own_side, own_row = lax.rem(shard, SIDES), segment // cores
@@ -631,7 +637,14 @@
     def place_units(target, first):
         for side in range(SIDES):
             for other in range(segment_count):
-                parts = [ref[other % cores, :, first : first + columns] for ref in (here_ref, row_ref, side_ref, corner_ref)]
+                parts = [
+                    jnp.where(
+                        own_core == other % cores,
+                        mine_ref[index, :, first : first + columns],
+                        twin_ref[index, :, first : first + columns],
+                    )
+                    for index in range(4)
+                ]
                 same_row = own_row == other // cores
                 near = jnp.where(same_row, parts[0], parts[1])
                 across = jnp.where(same_row, parts[2], parts[3])
@@ -653,19 +666,19 @@
             grad_ref[inside:, :] = dot_tn(wanted, out_grad_ref[...])
 
 
-def weight_grad(block, out_grad, parts, groups):
+def weight_grad(block, out_grad, mine, twin, groups):
     items, shard_rows = block.shape
     width = out_grad.shape[1]
     vm = pl.BlockSpec(memory_space=pltpu.VMEM)
     return pl.pallas_call(
         functools.partial(weight_grad_kernel, groups),
-        in_specs=[vm] * (2 + len(parts)),
+        in_specs=[vm] * 4,
         out_specs=vm,
         out_shape=jax.ShapeDtypeStruct((shard_rows, width), F32),
         scratch_shapes=[pltpu.VMEM((items, width), BF16), pltpu.VMEM((items, width), BF16)],
         cost_estimate=cost(2 * items * shard_rows * width, 4 * shard_rows * width),
         compiler_params=pltpu.CompilerParams(vmem_limit_bytes=8 * MIB),
-    )(block, out_grad, *parts)
+    )(block, out_grad, mine, twin)
 
 
 def around(near, across, segment_count, dp_count):
@@ -710,7 +723,10 @@
         [jnp.where(is_image, mine, other)[:, :image_width], jnp.where(is_image, other, mine)], axis=1
     )
     embedded, pieces, books = lax.optimization_barrier((embedded, pieces, codebooks[0]))
-    embedded_all = spread(embedded, "dp", dp_count)
+    half = first_rows // 2
+    embedded_half = jnp.where(segment_index % 2 == 0, embedded[:, :half], embedded[:, half:])
+    mine_half = spread(embedded_half, "dp", dp_count)
+    twin_half = lax.ppermute(mine_half, "segment", [(i, i ^ 1) for i in range(segment_count)])
 
     pair = item_cats.shape[1] // dp_count
     cats = item_cats.reshape(segment_count, dp_count, pair).transpose(1, 0, 2).reshape(-1)
@@ -733,7 +749,7 @@
     counts = jnp.sum((own_negatives[:, :, None] == bank_ids[None, None, :]).astype(F32), axis=1)
 
     block, hidden, active, second, partial = merge_part(
-        embedded_all, pieces, both_own, groups, shard_rows, first_rows, width
+        mine_half, twin_half, pieces, both_own, groups, shard_rows, first_rows, width
     )
     partial = partial + lax.ppermute(partial, "segment", [(i, i ^ 1) for i in range(segment_count)])
     row, side, corner = around(partial[:owned], partial[owned:], segment_count, dp_count)
@@ -742,11 +758,10 @@
     gathered = spread(merged_grad, "dp", dp_count)
     book_grad = codebook_grad(left, right, books)
     out_grad, sent = backward_part(gathered, order, hidden, active, second)
-    twin = lax.ppermute(sent, "segment", [(i, i ^ 1) for i in range(segment_count)])
-    first_core = segment_index % 2 == 0
-    here = jnp.stack([jnp.where(first_core, sent, twin), jnp.where(first_core, twin, sent)])
-    parts = (here,) + around(here, here, segment_count, dp_count)
-    uniting_grad = weight_grad(block, out_grad, parts, groups)
+    mine = jnp.stack((sent,) + around(sent, sent, segment_count, dp_count))
+    mine, book_grad = lax.optimization_barrier((mine, book_grad))
+    twin = lax.ppermute(mine, "segment", [(i, i ^ 1) for i in range(segment_count)])
+    uniting_grad = weight_grad(block, out_grad, mine, twin, groups)
     return (uniting_grad, book_grad[None], loss)
 
 

time: 84.6 us -> 82.9 us (0.980)
  blocking collectives: 10.8 us -> 9.74 us
  waiting for transfers between devices: 18 us -> 17.1 us
    all_to_all x1, waiting for transfers between devices: 9.29 us -> 7.36 us  [spread(): lax.all_to_all(jnp.broadcast_to(rows[None], (count,) + rows.shape), axis_...]
    ppermute x1 -> x2, waiting for transfers between devices: 1.19 us -> 2.7 us  [the longest x1 1.37 us: per_device_parts(): lax.ppermute(mine_half, 'segment', [(i, i ^ 1) for i in range(segment_cou...]
    ppermute x2, starting transfers between devices: 2.51 us -> 1.31 us  [around(): corner = lax.ppermute(across, ('segment', 'dp'), corners)]
    all_to_all x1, blocking collectives: 10.8 us -> 9.74 us  [spread(): lax.all_to_all(jnp.broadcast_to(rows[None], (count,) + rows.shape), axis_...]
    ppermute x2, starting transfers between devices: 2.33 us -> 3.27 us  [around(): side = lax.ppermute(across, 'dp', [(i, i ^ 1) for i in range(dp_count)])]
  transfers between devices with their start and end apart: 12 -> 13, of which waited for: 8 -> 7; matrix products, arithmetic and copies ran while one was open for 1% -> 1% of each run, Pallas kernels for 25% -> 26%
where the time goes in v5:
time: 82.9 us; the launch traced here: 82.4 us
  Pallas kernels  31 us (37%)
  starting transfers between devices  20.5 us (25%)
  waiting for transfers between devices  17.1 us (21%)
  blocking collectives  9.74 us (12%)
  local copies, waits for them, and re-layouts  2.13 us (3%)
  between operations  0.96 us (1%)
    pallas_call x1, Pallas kernels, image_pooled(): pl.pallas_call(image_kernel, grid=(item_count // IMAGE_GROUP,), in_specs=...  18.5 us
    all_to_all x1, blocking collectives, spread(): lax.all_to_all(jnp.broadcast_to(rows[None], (count,) + rows.shape), axis_...  9.74 us
    all_to_all x1, waiting for transfers between devices, spread(): lax.all_to_all(jnp.broadcast_to(rows[None], (count,) + rows.shape), axis_...  7.36 us
    all_to_all x1, starting transfers between devices, per_device_parts(): pieces = lax.all_to_all(message, 'dp', 0, 0, tiled=True)  7.04 us
    all_to_all x1, starting transfers between devices, spread(): lax.all_to_all(jnp.broadcast_to(rows[None], (count,) + rows.shape), axis_...  5.97 us
    pallas_call x1, Pallas kernels, quantizer(): pl.pallas_call(functools.partial(quantizer_kernel, loss_scale), in_specs=...  4.03 us
    ppermute x1, waiting for transfers between devices, per_device_parts(): lax.ppermute(mine, 'segment', [(i, i ^ 2) for i in range(segment_count)])  3.8 us
    ppermute x2, starting transfers between devices, around(): side = lax.ppermute(across, 'dp', [(i, i ^ 1) for i in range(dp_count)])  3.27 us
  transfers between devices with their start and end apart: 13, of which 7 were waited for; matrix products, arithmetic and copies ran while one was open for 1% of the time, Pallas kernels for 26%

profile of v5, /device:TPU:0, one launch (start us, length us, event | category | flops | bytes accessed | tf_op | source)
XLA Modules:
  0.0 82.4 jit_solution(18407254511697571153)
XLA Ops:
  0.7 2.6 %shard_map.137 = bf16[8,464,128]{2,1,0:T(8,128)(2,1)} custom-call(bf16[448,1024]{1,0:T(8,128)(2,1)} %rows_ref.1), custom_call_target="tpu_custom_call" | custom-call | bytes 1835008 | tf_op jit(solution)/shard_map/pallas_call | solution.py:332
  3.3 7.0 %all-to-all-start = ((bf16[8,464,128]{2,1,0:T(8,128)(2,1)}), bf16[8,464,128]{2,1,0:T(8,128)(2,1)S(1)}, u32[]{:S(2)}, u32[]{:S(2)}) async-start(bf16[8,464,128]{2,1,0:T(8,128)(2,1)} %shard_map.137), calls=%async_computation | async-start | bytes 1900544 | tf_op jit(solution)/shard_map/all_to_all | solution.py:716
  10.3 18.7 %conditional.1 = (f32[8,1536]{1,0:T(8,128)S(1)}) conditional(s32[]{:T(128)} %convert_element_type.34, (s32[1]{0:T(128)}, bf16[8,64,1536]{2,1,0:T(8,128)(2,1)S(1)}, bf16[1,21504,128]{2,1,0:T(8,128)(2,1)}) %tuple.32, (s32[1]{0:T(128)}, bf16[8,256,1024]{2,1,0:T(8,128)(2,1)}, bf16[1,21504,128]{2,1,0:T(8,128)(2,1)}) %tuple.19), branch_computations={%region_0.1_spmd.clone, %region_1.2_spmd} | conditional | bytes 2097216 | solution.py:778
  10.5 18.5 %branch_1_fun.1 = f32[8,1024]{1,0:T(8,128)S(1)} custom-call(s32[1]{0:T(128)} %get-tuple-element.24.flag_ref, bf16[8,256,1024]{2,1,0:T(8,128)(2,1)} %get-tuple-element.81.image_ref, bf16[1,21504,128]{2,1,0:T(8,128)(2,1)} %get-tuple-element.26.slot_ref), custom_call_target="tpu_custom_call" | custom-call | tf_op jit(solution)/shard_map/cond/branch_1_fun/pallas_call | solution.py:118
  29.2 0.1 copy.27
  29.4 0.1 eq.64
  29.6 0.2 select_reduce_fusion
  29.8 0.6 collective-permute-done
  30.5 3.8 %collective-permute-done.1 = bf16[8,1536]{1,0:T(8,128)(2,1)S(1)} collective-permute-done((bf16[8,1536]{1,0:T(8,128)(2,1)S(1)}, bf16[8,1536]{1,0:T(8,128)(2,1)S(1)}, u32[]{:S(2)}, u32[]{:S(2)}) %collective-permute-start.1) | collective-permute-done | bytes 24608 | tf_op jit(solution)/shard_map/ppermute | solution.py:720
  34.3 0.7 broadcast_in_dim.26
  35.0 6.0 %all-to-all-start.1 = ((bf16[8,8,1280]{2,1,0:T(8,128)(2,1)}), bf16[8,8,1280]{2,1,0:T(8,128)(2,1)S(1)}, u32[]{:S(2)}, u32[]{:S(2)}) async-start(bf16[8,8,1280]{2,1,0:T(8,128)(2,1)} %broadcast_in_dim.26), calls=%async_computation.1 | async-start | bytes 327680 | tf_op jit(solution)/shard_map/all_to_all | solution.py:695
  41.0 0.1 fusion.1
  41.2 7.4 %all-to-all-done.1.mine_ref = bf16[8,8,1280]{2,1,0:T(8,128)(2,1)S(1)} async-done(((bf16[8,8,1280]{2,1,0:T(8,128)(2,1)}), bf16[8,8,1280]{2,1,0:T(8,128)(2,1)S(1)}, u32[]{:S(2)}, u32[]{:S(2)}) %all-to-all-start.1) | async-done | bytes 163872 | tf_op jit(solution)/shard_map/all_to_all | solution.py:695
  48.6 1.4 %collective-permute-done.2.twin_ref = bf16[8,8,1280]{2,1,0:T(8,128)(2,1)S(1)} collective-permute-done((bf16[8,8,1280]{2,1,0:T(8,128)(2,1)S(1)}, bf16[8,8,1280]{2,1,0:T(8,128)(2,1)S(1)}, u32[]{:S(2)}, u32[]{:S(2)}) %collective-permute-start.2) | collective-permute-done | bytes 163872 | tf_op jit(solution)/shard_map/ppermute | solution.py:729
  49.9 0.8 shard_map.138
  50.7 0.2 collective-permute-start.3
  50.9 1.1 %collective-permute-done.3 = f32[16,1024]{1,0:T(8,128)S(1)} collective-permute-done((f32[16,1024]{1,0:T(8,128)S(1)}, f32[16,1024]{1,0:T(8,128)S(1)}, u32[]{:S(2)}, u32[]{:S(2)}) %collective-permute-start.3) | collective-permute-done | bytes 65568 | tf_op jit(solution)/shard_map/ppermute | solution.py:754
  52.1 1.5 %collective-permute-start.5 = (f32[8,1024]{1,0:T(8,128)S(1)}, f32[8,1024]{1,0:T(8,128)S(1)}, u32[]{:S(2)}, u32[]{:S(2)}) collective-permute-start(f32[8,1024]{1,0:T(8,128)S(1)} %get-tuple-element.89), channel_id=1, source_target_pairs={{0,1},{1,0},{2,3},{3,2},{4,5},{5,4},{6,7},{7,6},{8,9},{9,8},{10,11... | collective-permute-start | bytes 98312 | tf_op jit(solution)/shard_map/ppermute | solution.py:686
  53.5 2.0 %collective-permute-start.4 = (f32[8,1024]{1,0:T(8,128)S(1)}, f32[8,1024]{1,0:T(8,128)S(1)}, u32[]{:S(2)}, u32[]{:S(2)}) collective-permute-start(f32[8,1024]{1,0:T(8,128)S(1)} %get-tuple-element.88), channel_id=1, source_target_pairs={{0,16},{8,24},{16,0},{24,8},{1,17},{9,25},{17,1},{25,9},{2,18},{10... | collective-permute-start | bytes 98312 | tf_op jit(solution)/shard_map/ppermute | solution.py:685
  55.5 0.2 convert_reduce_fusion.count_ref
  55.8 1.0 %copy-done.1 = bf16[1,256,1024]{2,1,0:T(8,128)(2,1)S(1)} copy-done((bf16[1,256,1024]{2,1,0:T(8,128)(2,1)S(1)}, bf16[1,256,1024]{2,1,0:T(8,128)(2,1)}, u32[]{:S(2)}) %copy-start.1) | copy-done | bytes 524312
  56.8 1.1 %shard_map.139 = (bf16[2,256,1024]{2,1,0:T(8,128)(2,1)S(1)}, bf16[2,256,1024]{2,1,0:T(8,128)(2,1)S(1)}, f32[2,8,256]{2,1,0:T(8,128)S(1)}, f32[8,256]{1,0:T(8,128)S(1)}) custom-call(f32[2,256,1024]{2,1,0:T(8,128)S(1)} %bitcast.16, bf16[256,1024]{1,0:T(8,128)(2,1)S(1)} %bitcast.18), custom_call_target="tpu_custom_call" | custom-call | bytes 6291456 | tf_op jit(solution)/shard_map/pallas_call | solution.py:462
  58.0 4.0 %shard_map.140 = (bf16[8,1024]{1,0:T(8,128)(2,1)S(1)}, f32[1]{0:T(128)}, f32[2,16,256]{2,1,0:T(8,128)S(1)}, f32[2,16,1024]{2,1,0:T(8,128)S(1)}) custom-call(f32[8,1024]{1,0:T(8,128)S(1)} %add_add_fusion.merged_ref, bf16[2,256,1024]{2,1,0:T(8,128)(2,1)S(1)} %get-tuple-element.59.highs, bf16[2,256,1024]{2,1,0:T(8,128)(2,1)S(1)} %get-tuple-element.60.lows, ...), custom_call_target="tpu_custom_call" | custom-call | flops 33554432 | bytes 2097152 | tf_op jit(solution)/shard_map/pallas_call | solution.py:558
  62.0 9.7 %all_to_all.15.gathered_ref = bf16[8,8,1024]{2,1,0:T(8,128)(2,1)S(1)} all-to-all(bf16[8,8,1024]{2,1,0:T(8,128)(2,1)S(1)} %broadcast_in_dim.50), channel_id=1, replica_groups=mesh['segment'=4,'dp'=8] {'dp'}, dimensions={0} | all-to-all | bytes 262144 | tf_op jit(solution)/shard_map/all_to_all | solution.py:695
  71.8 0.4 shard_map.141
  72.1 1.2 %collective-permute-start.9 = (bf16[64,256]{1,0:T(8,128)(2,1)S(1)}, bf16[64,256]{1,0:T(8,128)(2,1)S(1)}, u32[]{:S(2)}, u32[]{:S(2)}) collective-permute-start(bf16[64,256]{1,0:T(8,128)(2,1)S(1)} %get-tuple-element.68), channel_id=1, source_target_pairs={{0,17},{1,16},{2,19},{3,18},{4,21},{5,20},{6,23},{7,22},{8,25},{9,... | collective-permute-start | bytes 98312 | tf_op jit(solution)/shard_map/ppermute | solution.py:690
  73.4 1.8 %collective-permute-start.8 = (bf16[64,256]{1,0:T(8,128)(2,1)S(1)}, bf16[64,256]{1,0:T(8,128)(2,1)S(1)}, u32[]{:S(2)}, u32[]{:S(2)}) collective-permute-start(bf16[64,256]{1,0:T(8,128)(2,1)S(1)} %get-tuple-element.68), channel_id=1, source_target_pairs={{0,1},{1,0},{2,3},{3,2},{4,5},{5,4},{6,7},{7,6},{8,9},{9,8},{10,11... | collective-permute-start | bytes 98312 | tf_op jit(solution)/shard_map/ppermute | solution.py:686
  75.2 0.5 collective-permute-start.7
  75.7 1.9 %shard_map.142 = f32[2,256,1024]{2,1,0:T(8,128)} custom-call(f32[2,16,256]{2,1,0:T(8,128)S(1)} %get-tuple-element.69.left_ref, f32[2,16,1024]{2,1,0:T(8,128)S(1)} %get-tuple-element.70.right_ref, f32[2,256,1024]{2,1,0:T(8,128)S(1)} %bitcast.17), custom_call_target="tpu_custom_call" | custom-call | flops 50331648 | bytes 4194304 | tf_op jit(solution)/shard_map/pallas_call | solution.py:588
  77.6 1.5 %collective-permute-done.7 = bf16[64,256]{1,0:T(8,128)(2,1)S(1)} collective-permute-done((bf16[64,256]{1,0:T(8,128)(2,1)S(1)}, bf16[64,256]{1,0:T(8,128)(2,1)S(1)}, u32[]{:S(2)}, u32[]{:S(2)}) %collective-permute-start.7) | collective-permute-done | bytes 32800 | tf_op jit(solution)/shard_map/ppermute | solution.py:685
  79.2 1.3 %collective-permute-done.10.twin_ref = bf16[4,64,256]{2,1,0:T(8,128)(2,1)S(1)} collective-permute-done((bf16[4,64,256]{2,1,0:T(8,128)(2,1)S(1)}, bf16[4,64,256]{2,1,0:T(8,128)(2,1)S(1)}, u32[]{:S(2)}, u32[]{:S(2)}) %collective-permute-start.10) | collective-permute-done | bytes 131104 | tf_op jit(solution)/shard_map/ppermute | solution.py:763
  80.5 1.8 %shard_map.143 = f32[448,1024]{1,0:T(8,128)} custom-call(bf16[64,448]{1,0:T(8,128)(2,1)S(1)} %get-tuple-element.56.block_ref, bf16[64,1024]{1,0:T(8,128)(2,1)S(1)} %get-tuple-element.67.out_grad_ref, bf16[4,64,256]{2,1,0:T(8,128)(2,1)S(1)} %pad_maximum_fusion.mine_ref, bf16[4,64,256]{2,1,0:T(8,128)(2,1)S(1)} %collective-permute-done.10.twin_ref), custom_call_target="tpu_custom_call" | custom-call | flops 58720256 | bytes 1835008 | tf_op jit(solution)/shard_map/pallas_call | solution.py:673
  (44 shorter events, 0.7 us)
Async XLA Ops:
  0.6 9.7 %copy-start.5 = (bf16[8,64,1536]{2,1,0:T(8,128)(2,1)S(1)}, bf16[8,64,1536]{2,1,0:T(8,128)(2,1)}, u32[]{:S(2)}) copy-start(bf16[8,64,1536]{2,1,0:T(8,128)(2,1)} %param.14) | copy-start | bytes 4718596
  3.3 37.7 %copy-start.6 = (s32[4,16,128]{2,1,0:T(8,128)S(1)}, s32[4,16,128]{2,1,0:T(8,128)}, u32[]{:S(2)}) copy-start(s32[4,16,128]{2,1,0:T(8,128)} %param.21) | copy-start | bytes 98308
  3.3 31.0 %all-to-all-start = ((bf16[8,464,128]{2,1,0:T(8,128)(2,1)}), bf16[8,464,128]{2,1,0:T(8,128)(2,1)S(1)}, u32[]{:S(2)}, u32[]{:S(2)}) async-start(bf16[8,464,128]{2,1,0:T(8,128)(2,1)} %shard_map.137), calls=%async_computation | async-start | bytes 1900544 | tf_op jit(solution)/shard_map/all_to_all | solution.py:716
  10.3 18.8 %copy-start.7 = (s32[4,16,1]{1,2,0:T(1,128)S(1)}, s32[4,16,1]{1,2,0:T(1,128)}, u32[]{:S(2)}) copy-start(s32[4,16,1]{1,2,0:T(1,128)} %param.19) | copy-start | bytes 772
  10.3 19.2 %copy-start.8 = (s32[8]{0:T(128)S(1)}, s32[8]{0:T(128)}, u32[]{:S(2)}) copy-start(s32[8]{0:T(128)} %param.20) | copy-start | bytes 100
  29.1 26.7 %copy-start = (f32[1,2,256,1024]{3,2,1,0:T(8,128)S(1)}, f32[1,2,256,1024]{3,2,1,0:T(8,128)}, u32[]{:S(2)}) copy-start(f32[1,2,256,1024]{3,2,1,0:T(8,128)} %param.17) | copy-start | bytes 6291460
  29.1 1.3 %collective-permute-start = (f32[8,1536]{1,0:T(8,128)S(1)}, f32[8,1536]{1,0:T(8,128)S(1)}, u32[]{:S(2)}, u32[]{:S(2)}) collective-permute-start(f32[8,1536]{1,0:T(8,128)S(1)} %get-tuple-element.94), channel_id=1, source_target_pairs={{0,8},{8,0},{16,24},{24,16},{1,9},{9,1},{17,25},{25,17},{2,10},{10... | collective-permute-start | bytes 147464 | tf_op jit(solution)/shard_map/ppermute | solution.py:718
  30.4 3.9 %collective-permute-start.1 = (bf16[8,1536]{1,0:T(8,128)(2,1)S(1)}, bf16[8,1536]{1,0:T(8,128)(2,1)S(1)}, u32[]{:S(2)}, u32[]{:S(2)}) collective-permute-start(bf16[8,1536]{1,0:T(8,128)(2,1)S(1)} %add_convert_fusion), channel_id=1, source_target_pairs={{0,16},{8,24},{16,0},{24,8},{1,17},{9,25},{17,1},{25,9},{2,18},{10... | collective-permute-start | bytes 73736 | tf_op jit(solution)/shard_map/ppermute | solution.py:720
  35.0 13.5 %all-to-all-start.1 = ((bf16[8,8,1280]{2,1,0:T(8,128)(2,1)}), bf16[8,8,1280]{2,1,0:T(8,128)(2,1)S(1)}, u32[]{:S(2)}, u32[]{:S(2)}) async-start(bf16[8,8,1280]{2,1,0:T(8,128)(2,1)} %broadcast_in_dim.26), calls=%async_computation.1 | async-start | bytes 327680 | tf_op jit(solution)/shard_map/all_to_all | solution.py:695
  48.5 1.4 %collective-permute-start.2 = (bf16[8,8,1280]{2,1,0:T(8,128)(2,1)S(1)}, bf16[8,8,1280]{2,1,0:T(8,128)(2,1)S(1)}, u32[]{:S(2)}, u32[]{:S(2)}) collective-permute-start(bf16[8,8,1280]{2,1,0:T(8,128)(2,1)S(1)} %all-to-all-done.1.mine_ref), channel_id=1, source_target_pairs={{0,8},{8,0},{16,24},{24,16},{1,9},{9,1},{17,25},{25,17},{2,10},{10... | collective-permute-start | bytes 491528 | tf_op jit(solution)/shard_map/ppermute | solution.py:729
  48.5 9.4 %copy-start.2 = (bf16[1,256,1024]{2,1,0:T(8,128)(2,1)S(1)}, bf16[1,256,1024]{2,1,0:T(8,128)(2,1)}, u32[]{:S(2)}) copy-start(bf16[1,256,1024]{2,1,0:T(8,128)(2,1)} %param.18) | copy-start | bytes 1572868
  50.7 1.3 %collective-permute-start.3 = (f32[16,1024]{1,0:T(8,128)S(1)}, f32[16,1024]{1,0:T(8,128)S(1)}, u32[]{:S(2)}, u32[]{:S(2)}) collective-permute-start(f32[16,1024]{1,0:T(8,128)S(1)} %get-tuple-element.57), channel_id=1, source_target_pairs={{0,8},{8,0},{16,24},{24,16},{1,9},{9,1},{17,25},{25,17},{2,10},{10... | collective-permute-start | bytes 196616 | tf_op jit(solution)/shard_map/ppermute | solution.py:754
  52.0 5.9 %collective-permute-start.6 = (f32[8,1024]{1,0:T(8,128)S(1)}, f32[8,1024]{1,0:T(8,128)S(1)}, u32[]{:S(2)}, u32[]{:S(2)}) collective-permute-start(f32[8,1024]{1,0:T(8,128)S(1)} %get-tuple-element.89), channel_id=1, source_target_pairs={{0,17},{1,16},{2,19},{3,18},{4,21},{5,20},{6,23},{7,22},{8,25},{9,... | collective-permute-start | bytes 98312 | tf_op jit(solution)/shard_map/ppermute | solution.py:690
  52.1 5.9 %collective-permute-start.5 = (f32[8,1024]{1,0:T(8,128)S(1)}, f32[8,1024]{1,0:T(8,128)S(1)}, u32[]{:S(2)}, u32[]{:S(2)}) collective-permute-start(f32[8,1024]{1,0:T(8,128)S(1)} %get-tuple-element.89), channel_id=1, source_target_pairs={{0,1},{1,0},{2,3},{3,2},{4,5},{5,4},{6,7},{7,6},{8,9},{9,8},{10,11... | collective-permute-start | bytes 98312 | tf_op jit(solution)/shard_map/ppermute | solution.py:686
  53.5 4.4 %collective-permute-start.4 = (f32[8,1024]{1,0:T(8,128)S(1)}, f32[8,1024]{1,0:T(8,128)S(1)}, u32[]{:S(2)}, u32[]{:S(2)}) collective-permute-start(f32[8,1024]{1,0:T(8,128)S(1)} %get-tuple-element.88), channel_id=1, source_target_pairs={{0,16},{8,24},{16,0},{24,8},{1,17},{9,25},{17,1},{25,9},{2,18},{10... | collective-permute-start | bytes 98312 | tf_op jit(solution)/shard_map/ppermute | solution.py:685
  55.8 1.0 %copy-start.1 = (bf16[1,256,1024]{2,1,0:T(8,128)(2,1)S(1)}, bf16[1,256,1024]{2,1,0:T(8,128)(2,1)}, u32[]{:S(2)}) copy-start(bf16[1,256,1024]{2,1,0:T(8,128)(2,1)} %param.18) | copy-start | bytes 1572868
  72.1 5.4 %collective-permute-start.9 = (bf16[64,256]{1,0:T(8,128)(2,1)S(1)}, bf16[64,256]{1,0:T(8,128)(2,1)S(1)}, u32[]{:S(2)}, u32[]{:S(2)}) collective-permute-start(bf16[64,256]{1,0:T(8,128)(2,1)S(1)} %get-tuple-element.68), channel_id=1, source_target_pairs={{0,17},{1,16},{2,19},{3,18},{4,21},{5,20},{6,23},{7,22},{8,25},{9,... | collective-permute-start | bytes 98312 | tf_op jit(solution)/shard_map/ppermute | solution.py:690
  73.4 4.2 %collective-permute-start.8 = (bf16[64,256]{1,0:T(8,128)(2,1)S(1)}, bf16[64,256]{1,0:T(8,128)(2,1)S(1)}, u32[]{:S(2)}, u32[]{:S(2)}) collective-permute-start(bf16[64,256]{1,0:T(8,128)(2,1)S(1)} %get-tuple-element.68), channel_id=1, source_target_pairs={{0,1},{1,0},{2,3},{3,2},{4,5},{5,4},{6,7},{7,6},{8,9},{9,8},{10,11... | collective-permute-start | bytes 98312 | tf_op jit(solution)/shard_map/ppermute | solution.py:686
  75.2 3.9 %collective-permute-start.7 = (bf16[64,256]{1,0:T(8,128)(2,1)S(1)}, bf16[64,256]{1,0:T(8,128)(2,1)S(1)}, u32[]{:S(2)}, u32[]{:S(2)}) collective-permute-start(bf16[64,256]{1,0:T(8,128)(2,1)S(1)} %get-tuple-element.68), channel_id=1, source_target_pairs={{0,16},{8,24},{16,0},{24,8},{1,17},{9,25},{17,1},{25,9},{2,18},{10... | collective-permute-start | bytes 98312 | tf_op jit(solution)/shard_map/ppermute | solution.py:685
  79.1 1.4 %collective-permute-start.10 = (bf16[4,64,256]{2,1,0:T(8,128)(2,1)S(1)}, bf16[4,64,256]{2,1,0:T(8,128)(2,1)S(1)}, u32[]{:S(2)}, u32[]{:S(2)}) collective-permute-start(bf16[4,64,256]{2,1,0:T(8,128)(2,1)S(1)} %pad_maximum_fusion.mine_ref), channel_id=1, source_target_pairs={{0,8},{8,0},{16,24},{24,16},{1,9},{9,1},{17,25},{25,17},{2,10},{10... | collective-permute-start | bytes 393224 | tf_op jit(solution)/shard_map/ppermute | solution.py:763

commit v6 on v5

--- a/solution.py
+++ b/solution.py
@@ -18,6 +18,7 @@
 OWNED = 4 * CAP
 MIB = 1024 * 1024
 IMAGE_GROUP = 4
+PROJECT_LANES = 512
 LOG2_E = 1.4426950408889634
 SIDES = 2
 TILE = 8
@@ -68,71 +69,106 @@
         return carry
     lax.fori_loop(0, rows // row_step, body, 0)
 
-def image_kernel(flag_ref, image_ref, slot_ref, pooled_ref, w_in, w_out, wide, heads_mean):
-    step = pl.program_id(0)
-    item_count, model_width = pooled_ref.shape
+def image_kernel(
+    flag_ref, image_hbm, slot_hbm, pooled_ref, image, rows_in, rows_out, w_in, w_out, wide, normed, joined, heads_mean, semaphores
+):
+    item_count, patch_count, model_width = image.shape
     half_width = model_width // 2
     head_count = half_width // HEAD_IMG
-    group, patch_count, _ = image_ref.shape
-
-    @pl.when(step == 0)
-    def _():
-        unfold(slot_ref, 0, w_in, wide, 128)
-        unfold(slot_ref, model_width * 12, w_out, wide, 128)
-
-    tokens = image_ref[...].reshape(group * patch_count, model_width).astype(F32)
-    centred = tokens - jnp.mean(tokens, axis=1, keepdims=True)
-    variance = jnp.mean(centred * centred, axis=1, keepdims=True)
-    normed = (centred * lax.rsqrt(variance + norm_eps)).astype(BF16)
-    queries = (dot_nn(normed, w_in[:, :half_width]) * (LOG2_E / math.sqrt(HEAD_IMG))).astype(BF16)
-    keys = dot_nn(normed, w_in[:, half_width : 2 * half_width]).astype(BF16)
+    groups = item_count // IMAGE_GROUP
+    group_rows = IMAGE_GROUP * patch_count
+    in_rows, out_rows = rows_in.shape[1], rows_out.shape[1]
+    members = [pl.ds(index * IMAGE_GROUP, IMAGE_GROUP) for index in range(groups)]
+    fetches = [pltpu.make_async_copy(image_hbm.at[span], image.at[span], semaphores.at[index]) for index, span in enumerate(members)]
+    fetch_in = pltpu.make_async_copy(slot_hbm.at[:, pl.ds(0, in_rows)], rows_in, semaphores.at[groups])
+    fetch_out = pltpu.make_async_copy(slot_hbm.at[:, pl.ds(in_rows, out_rows)], rows_out, semaphores.at[groups + 1])
+    fetches[0].start()
+    fetch_in.start()
+    for fetch in fetches[1:]:
+        fetch.start()
+    fetch_out.start()
+    flag = flag_ref[0].astype(F32)
+
+    def normalize(index):
+        fetches[index].wait()
+        for member in range(index * IMAGE_GROUP, (index + 1) * IMAGE_GROUP):
+            tokens = image[member].astype(F32)
+            centred = tokens - jnp.mean(tokens, axis=1, keepdims=True)
+            variance = jnp.mean(centred * centred, axis=1, keepdims=True)
+            normed[member] = (centred * lax.rsqrt(variance + norm_eps)).astype(BF16)
+            pooled_ref[member : member + 1, :] = jnp.mean(tokens, axis=0, keepdims=True) * flag
+
+    def project(index, part):
+        lanes = slice(part * PROJECT_LANES, (part + 1) * PROJECT_LANES)
+        span = slice(index * IMAGE_GROUP, (index + 1) * IMAGE_GROUP)
+        result = dot_nn(normed[span].reshape(group_rows, model_width), w_in[:, lanes])
+        if (part + 1) * PROJECT_LANES <= half_width:
+            result = result * (LOG2_E / math.sqrt(HEAD_IMG))
+        joined[index, :, lanes] = result.astype(BF16)
+
+    parts = 2 * half_width // PROJECT_LANES
     row_ids = lax.broadcasted_iota(jnp.int32, (head_count, patch_count), 0)
-    flag = flag_ref[0].astype(F32)
-    for member in range(group):
-        rows = slice(member * patch_count, (member + 1) * patch_count)
-        weights = jnp.zeros((head_count, patch_count), F32)
-        for head in range(head_count):
-            span = slice(head * HEAD_IMG, (head + 1) * HEAD_IMG)
-            scores = dot_nt(queries[rows, span], keys[rows, span])
-            exps = jnp.exp2(scores - jnp.max(scores, axis=1, keepdims=True))
-            share = (1.0 / patch_count) / jnp.sum(exps, axis=1, keepdims=True)
-            mean_share = jnp.sum(exps * share, axis=0, keepdims=True)
-            weights = weights + jnp.where(row_ids == head, mean_share, 0.0)
-        item = step * group + member
-        heads_mean[pl.ds(item * head_count, head_count), :] = dot_two(weights, normed[rows])
-        pooled_ref[pl.ds(item, 1), :] = jnp.mean(tokens[rows], axis=0, keepdims=True) * flag
-
-    @pl.when(step == item_count // group - 1)
-    def _():
-        values = dot_two(heads_mean[...], w_in[:, 2 * half_width :])
-        rows = lax.broadcasted_iota(jnp.int32, values.shape, 0)
-        columns = lax.broadcasted_iota(jnp.int32, values.shape, 1)
-        values = jnp.where(rows % head_count == columns // HEAD_IMG, values, 0.0)
-        attended = jnp.sum(values.reshape(item_count, head_count, half_width), axis=1)
-        pooled_ref[...] += dot_two(attended, w_out[...])
+    normalize(0)
+    fetch_in.wait()
+    unfold(rows_in, 0, w_in, wide, 128)
+    for part in range(parts):
+        project(0, part)
+    units = IMAGE_GROUP * head_count
+    for index in range(groups):
+        if index + 1 < groups:
+            normalize(index + 1)
+        for member in range(IMAGE_GROUP):
+            rows = slice(member * patch_count, (member + 1) * patch_count)
+            weights = jnp.zeros((head_count, patch_count), F32)
+            for head in range(head_count):
+                unit = member * head_count + head
+                if index + 1 < groups and unit * parts % units < parts:
+                    project(index + 1, unit * parts // units)
+                span = slice(head * HEAD_IMG, (head + 1) * HEAD_IMG)
+                key_span = slice(half_width + head * HEAD_IMG, half_width + (head + 1) * HEAD_IMG)
+                scores = dot_nt(joined[index, rows, span], joined[index, rows, key_span])
+                exps = jnp.exp2(scores - jnp.max(scores, axis=1, keepdims=True))
+                share = (1.0 / patch_count) / jnp.sum(exps, axis=1, keepdims=True)
+                mean_share = jnp.sum(exps * share, axis=0, keepdims=True)
+                weights = weights + jnp.where(row_ids == head, mean_share, 0.0)
+            item = index * IMAGE_GROUP + member
+            heads_mean[item * head_count : (item + 1) * head_count, :] = dot_two(weights, normed[item])
+    fetch_out.wait()
+    unfold(rows_out, 0, w_out, wide, 128)
+    values = dot_two(heads_mean[...], w_in[:, 2 * half_width :])
+    rows = lax.broadcasted_iota(jnp.int32, values.shape, 0)
+    columns = lax.broadcasted_iota(jnp.int32, values.shape, 1)
+    values = jnp.where(rows % head_count == columns // HEAD_IMG, values, 0.0)
+    attended = jnp.sum(values.reshape(item_count, head_count, half_width), axis=1)
+    pooled_ref[...] += dot_two(attended, w_out[...])
+
 
 def image_pooled(images, slot, flag):
     item_count, patch_count, model_width = images.shape
     half_width = model_width // 2
     head_count = half_width // HEAD_IMG
+    groups = item_count // IMAGE_GROUP
+    anywhere = pl.BlockSpec(memory_space=pl.ANY)
     return pl.pallas_call(
         image_kernel,
-        grid=(item_count // IMAGE_GROUP,),
-        in_specs=[
-            pl.BlockSpec(memory_space=pltpu.SMEM),
-            pl.BlockSpec((IMAGE_GROUP, patch_count, model_width), lambda i: (i, 0, 0)),
-            pl.BlockSpec((1, 16 * model_width, 128), lambda i: (0, 0, 0), pipeline_mode=pl.Buffered(1)),
-        ],
-        out_specs=pl.BlockSpec((item_count, model_width), lambda i: (0, 0)),
+        in_specs=[pl.BlockSpec(memory_space=pltpu.SMEM), anywhere, anywhere],
+        out_specs=pl.BlockSpec(memory_space=pltpu.VMEM),
         out_shape=jax.ShapeDtypeStruct((item_count, model_width), F32),
         scratch_shapes=[
+            pltpu.VMEM(images.shape, BF16),
+            pltpu.VMEM((1, 12 * model_width, 128), BF16),
+            pltpu.VMEM((1, 4 * model_width, 128), BF16),
             pltpu.VMEM((model_width, 3 * half_width), BF16),
             pltpu.VMEM((half_width, model_width), BF16),
             pltpu.VMEM((128 * 12, 128), F32),
+            pltpu.VMEM(images.shape, BF16),
+            pltpu.VMEM((groups, IMAGE_GROUP * patch_count, 2 * half_width), BF16),
             pltpu.VMEM((item_count * head_count, model_width), F32),
+            pltpu.SemaphoreType.DMA((groups + 2,)),
         ],
-        compiler_params=pltpu.CompilerParams(vmem_limit_bytes=40 * 1024 * 1024),
+        compiler_params=pltpu.CompilerParams(vmem_limit_bytes=44 * 1024 * 1024),
     )(flag, images, slot)
+
 
 def rope_tables(tokens, repeats):
     half = HEAD_TXT // 2
@@ -291,7 +327,7 @@
 def message_kernel(groups, rows_ref, message_ref, built, semaphores):
     shard, segment = lax.axis_index("dp"), lax.axis_index("segment")
     copies, _, columns = message_ref.shape
-    shard_rows, width = rows_ref.shape
+    row_count, width = rows_ref.shape
     segment_count = width // (SIDES * columns)
     first_last = groups[0][0]
 
@@ -313,13 +349,14 @@
             def _(part=part, inside=inside, share=share):
                 for side in range(SIDES):
                     start = inside + share * (side * segment_count + part)
-                    for block in range(width // columns):
-                        lanes = slice(block * columns, (block + 1) * columns)
-                        spot = inside + block * share
-                        built[side, spot : spot + share, :] = rows_ref[start : start + share, lanes]
+                    low = start // 16 * 16
+                    high = min(row_count, -(-(start + share) // 16) * 16)
+                    taken = rows_ref[low:high, :].astype(F32)[start - low : start - low + share]
+                    pieces = [taken[:, block * columns : (block + 1) * columns] for block in range(width // columns)]
+                    built[side, inside:, :] = jnp.concatenate(pieces, axis=0).astype(BF16)
 
     sends = [
-        pltpu.make_async_copy(built.at[copy % SIDES], message_ref.at[copy, :shard_rows], semaphores.at[copy]) for copy in range(copies)
+        pltpu.make_async_copy(built.at[copy % SIDES], message_ref.at[copy, :row_count], semaphores.at[copy]) for copy in range(copies)
     ]
     for send in sends:
         send.start()
@@ -378,13 +415,12 @@
     hidden_ref[...] = hidden
     active = gelu_value(hidden).astype(BF16)
     active_ref[...] = active
-    offset = 0
+    lines = []
     for block, inside, _, share in groups:
-        for part in range(partial_ref.shape[1] // columns):
-            second_ref[offset : offset + share, part * columns : (part + 1) * columns] = weights[
-                block, inside + part * share : inside + (part + 1) * share, :
-            ]
-        offset += share
+        rows = weights[block, inside:shard_rows, :].astype(F32)
+        pieces = [rows[part * share : (part + 1) * share] for part in range(partial_ref.shape[1] // columns)]
+        lines.append(jnp.concatenate(pieces, axis=1))
+    second_ref[...] = jnp.concatenate(lines, axis=0).astype(BF16)
     partial_ref[...] = dot_nn(dot_nn(own_ref[...], active).astype(BF16), second_ref[...])
 
 

time: 82.9 us -> 82.3 us (level)
  transfers between devices with their start and end apart: 13 -> 13, of which waited for: 7 -> 8; matrix products, arithmetic and copies ran while one was open for 1% -> 1% of each run, Pallas kernels for 26% -> 26%
where the time goes in v6:
time: 82.3 us; the launch traced here: 81.9 us
  Pallas kernels  30.5 us (37%)
  starting transfers between devices  20.3 us (25%)
  waiting for transfers between devices  17.3 us (21%)
  blocking collectives  9.74 us (12%)
  local copies, waits for them, and re-layouts  2.12 us (3%)
  between operations  0.95 us (1%)
    pallas_call x1, Pallas kernels, image_pooled(): pl.pallas_call(image_kernel, in_specs=[pl.BlockSpec(memory_space=pltpu.SM...  18 us
    all_to_all x1, blocking collectives, spread(): lax.all_to_all(jnp.broadcast_to(rows[None], (count,) + rows.shape), axis_...  9.74 us
    all_to_all x1, waiting for transfers between devices, spread(): lax.all_to_all(jnp.broadcast_to(rows[None], (count,) + rows.shape), axis_...  7.36 us
    all_to_all x1, starting transfers between devices, per_device_parts(): pieces = lax.all_to_all(message, 'dp', 0, 0, tiled=True)  7.03 us
    all_to_all x1, starting transfers between devices, spread(): lax.all_to_all(jnp.broadcast_to(rows[None], (count,) + rows.shape), axis_...  5.77 us
    pallas_call x1, Pallas kernels, quantizer(): pl.pallas_call(functools.partial(quantizer_kernel, loss_scale), in_specs=...  4.03 us
    ppermute x1, waiting for transfers between devices, per_device_parts(): lax.ppermute(mine, 'segment', [(i, i ^ 2) for i in range(segment_count)])  3.8 us
    ppermute x2, starting transfers between devices, around(): side = lax.ppermute(across, 'dp', [(i, i ^ 1) for i in range(dp_count)])  3.27 us
  transfers between devices with their start and end apart: 13, of which 8 were waited for; matrix products, arithmetic and copies ran while one was open for 1% of the time, Pallas kernels for 26%

profile of v6, /device:TPU:0, one launch (start us, length us, event | category | flops | bytes accessed | tf_op | source)
XLA Modules:
  0.0 81.9 jit_solution(5387911493274955914)
XLA Ops:
  0.7 2.6 %shard_map.137 = bf16[8,464,128]{2,1,0:T(8,128)(2,1)} custom-call(bf16[448,1024]{1,0:T(8,128)(2,1)} %rows_ref.1), custom_call_target="tpu_custom_call" | custom-call | bytes 1835008 | tf_op jit(solution)/shard_map/pallas_call | solution.py:369
  3.3 7.0 %all-to-all-start = ((bf16[8,464,128]{2,1,0:T(8,128)(2,1)}), bf16[8,464,128]{2,1,0:T(8,128)(2,1)S(1)}, u32[]{:S(2)}, u32[]{:S(2)}) async-start(bf16[8,464,128]{2,1,0:T(8,128)(2,1)} %shard_map.137), calls=%async_computation | async-start | bytes 1900544 | tf_op jit(solution)/shard_map/all_to_all | solution.py:752
  10.3 18.2 %conditional.1 = (f32[8,1536]{1,0:T(8,128)S(1)}) conditional(s32[]{:T(128)} %convert_element_type.34, (s32[1]{0:T(128)}, bf16[8,64,1536]{2,1,0:T(8,128)(2,1)S(1)}, bf16[1,21504,128]{2,1,0:T(8,128)(2,1)}) %tuple.32, (s32[1]{0:T(128)}, bf16[8,256,1024]{2,1,0:T(8,128)(2,1)}, bf16[1,21504,128]{2,1,0:T(8,128)(2,1)}) %tuple.19), branch_computations={%region_0.1_spmd.clone, %region_1.2_spmd} | conditional | bytes 2097216 | solution.py:814
  10.3 18.0 %branch_1_fun.1 = f32[8,1024]{1,0:T(8,128)S(1)} custom-call(s32[1]{0:T(128)} %get-tuple-element.24.flag_ref, bf16[8,256,1024]{2,1,0:T(8,128)(2,1)} %get-tuple-element.81.image_hbm, bf16[1,21504,128]{2,1,0:T(8,128)(2,1)} %get-tuple-element.26.slot_hbm), custom_call_target="tpu_custom_call" | custom-call | tf_op jit(solution)/shard_map/cond/branch_1_fun/pallas_call | solution.py:152
  28.7 0.1 copy.27
  29.1 0.2 select_reduce_fusion
  29.3 0.6 collective-permute-done
  30.0 3.8 %collective-permute-done.1 = bf16[8,1536]{1,0:T(8,128)(2,1)S(1)} collective-permute-done((bf16[8,1536]{1,0:T(8,128)(2,1)S(1)}, bf16[8,1536]{1,0:T(8,128)(2,1)S(1)}, u32[]{:S(2)}, u32[]{:S(2)}) %collective-permute-start.1) | collective-permute-done | bytes 24608 | tf_op jit(solution)/shard_map/ppermute | solution.py:756
  33.8 0.2 all-to-all-done.weights
  34.0 0.7 broadcast_in_dim.26
  34.7 5.8 %all-to-all-start.1 = ((bf16[8,8,1280]{2,1,0:T(8,128)(2,1)}), bf16[8,8,1280]{2,1,0:T(8,128)(2,1)S(1)}, u32[]{:S(2)}, u32[]{:S(2)}) async-start(bf16[8,8,1280]{2,1,0:T(8,128)(2,1)} %broadcast_in_dim.26), calls=%async_computation.1 | async-start | bytes 327680 | tf_op jit(solution)/shard_map/all_to_all | solution.py:731
  40.5 0.1 fusion.1
  40.7 7.4 %all-to-all-done.1.mine_ref = bf16[8,8,1280]{2,1,0:T(8,128)(2,1)S(1)} async-done(((bf16[8,8,1280]{2,1,0:T(8,128)(2,1)}), bf16[8,8,1280]{2,1,0:T(8,128)(2,1)S(1)}, u32[]{:S(2)}, u32[]{:S(2)}) %all-to-all-start.1) | async-done | bytes 163872 | tf_op jit(solution)/shard_map/all_to_all | solution.py:731
  48.0 1.4 %collective-permute-done.2.twin_ref = bf16[8,8,1280]{2,1,0:T(8,128)(2,1)S(1)} collective-permute-done((bf16[8,8,1280]{2,1,0:T(8,128)(2,1)S(1)}, bf16[8,8,1280]{2,1,0:T(8,128)(2,1)S(1)}, u32[]{:S(2)}, u32[]{:S(2)}) %collective-permute-start.2) | collective-permute-done | bytes 163872 | tf_op jit(solution)/shard_map/ppermute | solution.py:765
  49.4 0.8 shard_map.138
  50.2 0.2 collective-permute-start.3
  50.3 1.1 %collective-permute-done.3 = f32[16,1024]{1,0:T(8,128)S(1)} collective-permute-done((f32[16,1024]{1,0:T(8,128)S(1)}, f32[16,1024]{1,0:T(8,128)S(1)}, u32[]{:S(2)}, u32[]{:S(2)}) %collective-permute-start.3) | collective-permute-done | bytes 65568 | tf_op jit(solution)/shard_map/ppermute | solution.py:790
  51.6 1.5 %collective-permute-start.5 = (f32[8,1024]{1,0:T(8,128)S(1)}, f32[8,1024]{1,0:T(8,128)S(1)}, u32[]{:S(2)}, u32[]{:S(2)}) collective-permute-start(f32[8,1024]{1,0:T(8,128)S(1)} %get-tuple-element.89), channel_id=1, source_target_pairs={{0,1},{1,0},{2,3},{3,2},{4,5},{5,4},{6,7},{7,6},{8,9},{9,8},{10,11... | collective-permute-start | bytes 98312 | tf_op jit(solution)/shard_map/ppermute | solution.py:722
  53.0 2.0 %collective-permute-start.4 = (f32[8,1024]{1,0:T(8,128)S(1)}, f32[8,1024]{1,0:T(8,128)S(1)}, u32[]{:S(2)}, u32[]{:S(2)}) collective-permute-start(f32[8,1024]{1,0:T(8,128)S(1)} %get-tuple-element.88), channel_id=1, source_target_pairs={{0,16},{8,24},{16,0},{24,8},{1,17},{9,25},{17,1},{25,9},{2,18},{10... | collective-permute-start | bytes 98312 | tf_op jit(solution)/shard_map/ppermute | solution.py:721
  55.0 0.2 convert_reduce_fusion.count_ref
  55.3 1.0 %copy-done.1 = bf16[1,256,1024]{2,1,0:T(8,128)(2,1)S(1)} copy-done((bf16[1,256,1024]{2,1,0:T(8,128)(2,1)S(1)}, bf16[1,256,1024]{2,1,0:T(8,128)(2,1)}, u32[]{:S(2)}) %copy-start.1) | copy-done | bytes 524312
  56.3 1.1 %shard_map.139 = (bf16[2,256,1024]{2,1,0:T(8,128)(2,1)S(1)}, bf16[2,256,1024]{2,1,0:T(8,128)(2,1)S(1)}, f32[2,8,256]{2,1,0:T(8,128)S(1)}, f32[8,256]{1,0:T(8,128)S(1)}) custom-call(f32[2,256,1024]{2,1,0:T(8,128)S(1)} %bitcast.16, bf16[256,1024]{1,0:T(8,128)(2,1)S(1)} %bitcast.18), custom_call_target="tpu_custom_call" | custom-call | bytes 6291456 | tf_op jit(solution)/shard_map/pallas_call | solution.py:498
  57.4 4.0 %shard_map.140 = (bf16[8,1024]{1,0:T(8,128)(2,1)S(1)}, f32[1]{0:T(128)}, f32[2,16,256]{2,1,0:T(8,128)S(1)}, f32[2,16,1024]{2,1,0:T(8,128)S(1)}) custom-call(f32[8,1024]{1,0:T(8,128)S(1)} %add_add_fusion.merged_ref, bf16[2,256,1024]{2,1,0:T(8,128)(2,1)S(1)} %get-tuple-element.59.highs, bf16[2,256,1024]{2,1,0:T(8,128)(2,1)S(1)} %get-tuple-element.60.lows, ...), custom_call_target="tpu_custom_call" | custom-call | flops 33554432 | bytes 2097152 | tf_op jit(solution)/shard_map/pallas_call | solution.py:594
  61.5 9.7 %all_to_all.15.gathered_ref = bf16[8,8,1024]{2,1,0:T(8,128)(2,1)S(1)} all-to-all(bf16[8,8,1024]{2,1,0:T(8,128)(2,1)S(1)} %broadcast_in_dim.50), channel_id=1, replica_groups=mesh['segment'=4,'dp'=8] {'dp'}, dimensions={0} | all-to-all | bytes 262144 | tf_op jit(solution)/shard_map/all_to_all | solution.py:731
  71.2 0.4 shard_map.141
  71.6 1.2 %collective-permute-start.9 = (bf16[64,256]{1,0:T(8,128)(2,1)S(1)}, bf16[64,256]{1,0:T(8,128)(2,1)S(1)}, u32[]{:S(2)}, u32[]{:S(2)}) collective-permute-start(bf16[64,256]{1,0:T(8,128)(2,1)S(1)} %get-tuple-element.68), channel_id=1, source_target_pairs={{0,17},{1,16},{2,19},{3,18},{4,21},{5,20},{6,23},{7,22},{8,25},{9,... | collective-permute-start | bytes 98312 | tf_op jit(solution)/shard_map/ppermute | solution.py:726
  72.9 1.8 %collective-permute-start.8 = (bf16[64,256]{1,0:T(8,128)(2,1)S(1)}, bf16[64,256]{1,0:T(8,128)(2,1)S(1)}, u32[]{:S(2)}, u32[]{:S(2)}) collective-permute-start(bf16[64,256]{1,0:T(8,128)(2,1)S(1)} %get-tuple-element.68), channel_id=1, source_target_pairs={{0,1},{1,0},{2,3},{3,2},{4,5},{5,4},{6,7},{7,6},{8,9},{9,8},{10,11... | collective-permute-start | bytes 98312 | tf_op jit(solution)/shard_map/ppermute | solution.py:722
  74.7 0.5 collective-permute-start.7
  75.2 1.9 %shard_map.142 = f32[2,256,1024]{2,1,0:T(8,128)} custom-call(f32[2,16,256]{2,1,0:T(8,128)S(1)} %get-tuple-element.69.left_ref, f32[2,16,1024]{2,1,0:T(8,128)S(1)} %get-tuple-element.70.right_ref, f32[2,256,1024]{2,1,0:T(8,128)S(1)} %bitcast.17), custom_call_target="tpu_custom_call" | custom-call | flops 50331648 | bytes 4194304 | tf_op jit(solution)/shard_map/pallas_call | solution.py:624
  77.0 1.5 %collective-permute-done.7 = bf16[64,256]{1,0:T(8,128)(2,1)S(1)} collective-permute-done((bf16[64,256]{1,0:T(8,128)(2,1)S(1)}, bf16[64,256]{1,0:T(8,128)(2,1)S(1)}, u32[]{:S(2)}, u32[]{:S(2)}) %collective-permute-start.7) | collective-permute-done | bytes 32800 | tf_op jit(solution)/shard_map/ppermute | solution.py:721
  78.7 1.3 %collective-permute-done.10.twin_ref = bf16[4,64,256]{2,1,0:T(8,128)(2,1)S(1)} collective-permute-done((bf16[4,64,256]{2,1,0:T(8,128)(2,1)S(1)}, bf16[4,64,256]{2,1,0:T(8,128)(2,1)S(1)}, u32[]{:S(2)}, u32[]{:S(2)}) %collective-permute-start.10) | collective-permute-done | bytes 131104 | tf_op jit(solution)/shard_map/ppermute | solution.py:799
  80.0 1.8 %shard_map.143 = f32[448,1024]{1,0:T(8,128)} custom-call(bf16[64,448]{1,0:T(8,128)(2,1)S(1)} %get-tuple-element.56.block_ref, bf16[64,1024]{1,0:T(8,128)(2,1)S(1)} %get-tuple-element.67.out_grad_ref, bf16[4,64,256]{2,1,0:T(8,128)(2,1)S(1)} %pad_maximum_fusion.mine_ref, bf16[4,64,256]{2,1,0:T(8,128)(2,1)S(1)} %collective-permute-done.10.twin_ref), custom_call_target="tpu_custom_call" | custom-call | flops 58720256 | bytes 1835008 | tf_op jit(solution)/shard_map/pallas_call | solution.py:709
  (44 shorter events, 0.8 us)
Async XLA Ops:
  0.6 9.7 %copy-start.5 = (bf16[8,64,1536]{2,1,0:T(8,128)(2,1)S(1)}, bf16[8,64,1536]{2,1,0:T(8,128)(2,1)}, u32[]{:S(2)}) copy-start(bf16[8,64,1536]{2,1,0:T(8,128)(2,1)} %param.14) | copy-start | bytes 4718596
  3.3 37.2 %copy-start.6 = (s32[4,16,128]{2,1,0:T(8,128)S(1)}, s32[4,16,128]{2,1,0:T(8,128)}, u32[]{:S(2)}) copy-start(s32[4,16,128]{2,1,0:T(8,128)} %param.21) | copy-start | bytes 98308
  3.3 30.7 %all-to-all-start = ((bf16[8,464,128]{2,1,0:T(8,128)(2,1)}), bf16[8,464,128]{2,1,0:T(8,128)(2,1)S(1)}, u32[]{:S(2)}, u32[]{:S(2)}) async-start(bf16[8,464,128]{2,1,0:T(8,128)(2,1)} %shard_map.137), calls=%async_computation | async-start | bytes 1900544 | tf_op jit(solution)/shard_map/all_to_all | solution.py:752
  10.3 18.4 %copy-start.7 = (s32[4,16,1]{1,2,0:T(1,128)S(1)}, s32[4,16,1]{1,2,0:T(1,128)}, u32[]{:S(2)}) copy-start(s32[4,16,1]{1,2,0:T(1,128)} %param.19) | copy-start | bytes 772
  10.3 18.7 %copy-start.8 = (s32[8]{0:T(128)S(1)}, s32[8]{0:T(128)}, u32[]{:S(2)}) copy-start(s32[8]{0:T(128)} %param.20) | copy-start | bytes 100
  28.6 26.7 %copy-start = (f32[1,2,256,1024]{3,2,1,0:T(8,128)S(1)}, f32[1,2,256,1024]{3,2,1,0:T(8,128)}, u32[]{:S(2)}) copy-start(f32[1,2,256,1024]{3,2,1,0:T(8,128)} %param.17) | copy-start | bytes 6291460
  28.6 1.3 %collective-permute-start = (f32[8,1536]{1,0:T(8,128)S(1)}, f32[8,1536]{1,0:T(8,128)S(1)}, u32[]{:S(2)}, u32[]{:S(2)}) collective-permute-start(f32[8,1536]{1,0:T(8,128)S(1)} %get-tuple-element.94), channel_id=1, source_target_pairs={{0,8},{8,0},{16,24},{24,16},{1,9},{9,1},{17,25},{25,17},{2,10},{10... | collective-permute-start | bytes 147464 | tf_op jit(solution)/shard_map/ppermute | solution.py:754
  29.9 3.9 %collective-permute-start.1 = (bf16[8,1536]{1,0:T(8,128)(2,1)S(1)}, bf16[8,1536]{1,0:T(8,128)(2,1)S(1)}, u32[]{:S(2)}, u32[]{:S(2)}) collective-permute-start(bf16[8,1536]{1,0:T(8,128)(2,1)S(1)} %add_convert_fusion), channel_id=1, source_target_pairs={{0,16},{8,24},{16,0},{24,8},{1,17},{9,25},{17,1},{25,9},{2,18},{10... | collective-permute-start | bytes 73736 | tf_op jit(solution)/shard_map/ppermute | solution.py:756
  34.7 13.3 %all-to-all-start.1 = ((bf16[8,8,1280]{2,1,0:T(8,128)(2,1)}), bf16[8,8,1280]{2,1,0:T(8,128)(2,1)S(1)}, u32[]{:S(2)}, u32[]{:S(2)}) async-start(bf16[8,8,1280]{2,1,0:T(8,128)(2,1)} %broadcast_in_dim.26), calls=%async_computation.1 | async-start | bytes 327680 | tf_op jit(solution)/shard_map/all_to_all | solution.py:731
  48.0 1.4 %collective-permute-start.2 = (bf16[8,8,1280]{2,1,0:T(8,128)(2,1)S(1)}, bf16[8,8,1280]{2,1,0:T(8,128)(2,1)S(1)}, u32[]{:S(2)}, u32[]{:S(2)}) collective-permute-start(bf16[8,8,1280]{2,1,0:T(8,128)(2,1)S(1)} %all-to-all-done.1.mine_ref), channel_id=1, source_target_pairs={{0,8},{8,0},{16,24},{24,16},{1,9},{9,1},{17,25},{25,17},{2,10},{10... | collective-permute-start | bytes 491528 | tf_op jit(solution)/shard_map/ppermute | solution.py:765
  48.0 9.4 %copy-start.2 = (bf16[1,256,1024]{2,1,0:T(8,128)(2,1)S(1)}, bf16[1,256,1024]{2,1,0:T(8,128)(2,1)}, u32[]{:S(2)}) copy-start(bf16[1,256,1024]{2,1,0:T(8,128)(2,1)} %param.18) | copy-start | bytes 1572868
  50.2 1.3 %collective-permute-start.3 = (f32[16,1024]{1,0:T(8,128)S(1)}, f32[16,1024]{1,0:T(8,128)S(1)}, u32[]{:S(2)}, u32[]{:S(2)}) collective-permute-start(f32[16,1024]{1,0:T(8,128)S(1)} %get-tuple-element.57), channel_id=1, source_target_pairs={{0,8},{8,0},{16,24},{24,16},{1,9},{9,1},{17,25},{25,17},{2,10},{10... | collective-permute-start | bytes 196616 | tf_op jit(solution)/shard_map/ppermute | solution.py:790
  51.5 5.9 %collective-permute-start.6 = (f32[8,1024]{1,0:T(8,128)S(1)}, f32[8,1024]{1,0:T(8,128)S(1)}, u32[]{:S(2)}, u32[]{:S(2)}) collective-permute-start(f32[8,1024]{1,0:T(8,128)S(1)} %get-tuple-element.89), channel_id=1, source_target_pairs={{0,17},{1,16},{2,19},{3,18},{4,21},{5,20},{6,23},{7,22},{8,25},{9,... | collective-permute-start | bytes 98312 | tf_op jit(solution)/shard_map/ppermute | solution.py:726
  51.6 5.9 %collective-permute-start.5 = (f32[8,1024]{1,0:T(8,128)S(1)}, f32[8,1024]{1,0:T(8,128)S(1)}, u32[]{:S(2)}, u32[]{:S(2)}) collective-permute-start(f32[8,1024]{1,0:T(8,128)S(1)} %get-tuple-element.89), channel_id=1, source_target_pairs={{0,1},{1,0},{2,3},{3,2},{4,5},{5,4},{6,7},{7,6},{8,9},{9,8},{10,11... | collective-permute-start | bytes 98312 | tf_op jit(solution)/shard_map/ppermute | solution.py:722
  53.0 4.4 %collective-permute-start.4 = (f32[8,1024]{1,0:T(8,128)S(1)}, f32[8,1024]{1,0:T(8,128)S(1)}, u32[]{:S(2)}, u32[]{:S(2)}) collective-permute-start(f32[8,1024]{1,0:T(8,128)S(1)} %get-tuple-element.88), channel_id=1, source_target_pairs={{0,16},{8,24},{16,0},{24,8},{1,17},{9,25},{17,1},{25,9},{2,18},{10... | collective-permute-start | bytes 98312 | tf_op jit(solution)/shard_map/ppermute | solution.py:721
  55.3 1.0 %copy-start.1 = (bf16[1,256,1024]{2,1,0:T(8,128)(2,1)S(1)}, bf16[1,256,1024]{2,1,0:T(8,128)(2,1)}, u32[]{:S(2)}) copy-start(bf16[1,256,1024]{2,1,0:T(8,128)(2,1)} %param.18) | copy-start | bytes 1572868
  71.6 5.4 %collective-permute-start.9 = (bf16[64,256]{1,0:T(8,128)(2,1)S(1)}, bf16[64,256]{1,0:T(8,128)(2,1)S(1)}, u32[]{:S(2)}, u32[]{:S(2)}) collective-permute-start(bf16[64,256]{1,0:T(8,128)(2,1)S(1)} %get-tuple-element.68), channel_id=1, source_target_pairs={{0,17},{1,16},{2,19},{3,18},{4,21},{5,20},{6,23},{7,22},{8,25},{9,... | collective-permute-start | bytes 98312 | tf_op jit(solution)/shard_map/ppermute | solution.py:726
  72.9 4.2 %collective-permute-start.8 = (bf16[64,256]{1,0:T(8,128)(2,1)S(1)}, bf16[64,256]{1,0:T(8,128)(2,1)S(1)}, u32[]{:S(2)}, u32[]{:S(2)}) collective-permute-start(bf16[64,256]{1,0:T(8,128)(2,1)S(1)} %get-tuple-element.68), channel_id=1, source_target_pairs={{0,1},{1,0},{2,3},{3,2},{4,5},{5,4},{6,7},{7,6},{8,9},{9,8},{10,11... | collective-permute-start | bytes 98312 | tf_op jit(solution)/shard_map/ppermute | solution.py:722
  74.7 3.9 %collective-permute-start.7 = (bf16[64,256]{1,0:T(8,128)(2,1)S(1)}, bf16[64,256]{1,0:T(8,128)(2,1)S(1)}, u32[]{:S(2)}, u32[]{:S(2)}) collective-permute-start(bf16[64,256]{1,0:T(8,128)(2,1)S(1)} %get-tuple-element.68), channel_id=1, source_target_pairs={{0,16},{8,24},{16,0},{24,8},{1,17},{9,25},{17,1},{25,9},{2,18},{10... | collective-permute-start | bytes 98312 | tf_op jit(solution)/shard_map/ppermute | solution.py:721
  78.6 1.4 %collective-permute-start.10 = (bf16[4,64,256]{2,1,0:T(8,128)(2,1)S(1)}, bf16[4,64,256]{2,1,0:T(8,128)(2,1)S(1)}, u32[]{:S(2)}, u32[]{:S(2)}) collective-permute-start(bf16[4,64,256]{2,1,0:T(8,128)(2,1)S(1)} %pad_maximum_fusion.mine_ref), channel_id=1, source_target_pairs={{0,8},{8,0},{16,24},{24,16},{1,9},{9,1},{17,25},{25,17},{2,10},{10... | collective-permute-start | bytes 393224 | tf_op jit(solution)/shard_map/ppermute | solution.py:799

commit v7 on v6

--- a/solution.py
+++ b/solution.py
@@ -18,7 +18,8 @@
 OWNED = 4 * CAP
 MIB = 1024 * 1024
 IMAGE_GROUP = 4
-PROJECT_LANES = 512
+PROJECT_LANES = 256
+OUT_STEP = 128
 LOG2_E = 1.4426950408889634
 SIDES = 2
 TILE = 8
@@ -56,18 +57,25 @@
     both = dot_nn(two_parts(value), weights)
     return both[:rows] + both[rows:]
 
+def unfold_step(slot_ref, first, out_ref, wide_ref, row_step, step):
+    blocks = out_ref.shape[1] // 128
+    start = step * row_step
+    source = first + step * (row_step * blocks)
+    if not isinstance(step, int):
+        start, source = pl.multiple_of(start, row_step), pl.multiple_of(source, 16)
+    wide_ref[0 : row_step * blocks, :] = slot_ref[0, pl.ds(source, row_step * blocks), :].astype(F32)
+    for block in range(blocks):
+        piece = wide_ref[pl.ds(block, row_step, stride=blocks), :]
+        out_ref[pl.ds(start, row_step), block * 128 : (block + 1) * 128] = piece.astype(BF16)
+
+
 def unfold(slot_ref, first, out_ref, wide_ref, row_step):
-    rows, columns = out_ref.shape
-    blocks = columns // 128
     def body(step, carry):
-        start = pl.multiple_of(step * row_step, row_step)
-        source = pl.multiple_of(first + step * (row_step * blocks), 16)
-        wide_ref[0 : row_step * blocks, :] = slot_ref[0, pl.ds(source, row_step * blocks), :].astype(F32)
-        for block in range(blocks):
-            piece = wide_ref[pl.ds(block, row_step, stride=blocks), :]
-            out_ref[pl.ds(start, row_step), block * 128 : (block + 1) * 128] = piece.astype(BF16)
+        unfold_step(slot_ref, first, out_ref, wide_ref, row_step, step)
         return carry
-    lax.fori_loop(0, rows // row_step, body, 0)
+
+    lax.fori_loop(0, out_ref.shape[0] // row_step, body, 0)
+
 
 def image_kernel(
     flag_ref, image_hbm, slot_hbm, pooled_ref, image, rows_in, rows_out, w_in, w_out, wide, normed, joined, heads_mean, semaphores
@@ -89,9 +97,8 @@
     fetch_out.start()
     flag = flag_ref[0].astype(F32)
 
-    def normalize(index):
-        fetches[index].wait()
-        for member in range(index * IMAGE_GROUP, (index + 1) * IMAGE_GROUP):
+    def normalize(first, last):
+        for member in range(first, last):
             tokens = image[member].astype(F32)
             centred = tokens - jnp.mean(tokens, axis=1, keepdims=True)
             variance = jnp.mean(centred * centred, axis=1, keepdims=True)
@@ -108,15 +115,22 @@
 
     parts = 2 * half_width // PROJECT_LANES
     row_ids = lax.broadcasted_iota(jnp.int32, (head_count, patch_count), 0)
-    normalize(0)
+    fetches[0].wait()
+    normalize(0, IMAGE_GROUP)
     fetch_in.wait()
     unfold(rows_in, 0, w_in, wide, 128)
+    for fetch in fetches[1:]:
+        fetch.wait()
+    fetch_out.wait()
+    half = IMAGE_GROUP + IMAGE_GROUP // 2
     for part in range(parts):
         project(0, part)
+        if part == 0:
+            normalize(IMAGE_GROUP, half)
+    normalize(half, item_count)
+    out_steps = half_width // OUT_STEP
     units = IMAGE_GROUP * head_count
     for index in range(groups):
-        if index + 1 < groups:
-            normalize(index + 1)
         for member in range(IMAGE_GROUP):
             rows = slice(member * patch_count, (member + 1) * patch_count)
             weights = jnp.zeros((head_count, patch_count), F32)
@@ -124,6 +138,8 @@
                 unit = member * head_count + head
                 if index + 1 < groups and unit * parts % units < parts:
                     project(index + 1, unit * parts // units)
+                if index + 1 == groups and unit * out_steps % units < out_steps:
+                    unfold_step(rows_out, 0, w_out, wide, OUT_STEP, unit * out_steps // units)
                 span = slice(head * HEAD_IMG, (head + 1) * HEAD_IMG)
                 key_span = slice(half_width + head * HEAD_IMG, half_width + (head + 1) * HEAD_IMG)
                 scores = dot_nt(joined[index, rows, span], joined[index, rows, key_span])
@@ -133,8 +149,6 @@
                 weights = weights + jnp.where(row_ids == head, mean_share, 0.0)
             item = index * IMAGE_GROUP + member
             heads_mean[item * head_count : (item + 1) * head_count, :] = dot_two(weights, normed[item])
-    fetch_out.wait()
-    unfold(rows_out, 0, w_out, wide, 128)
     values = dot_two(heads_mean[...], w_in[:, 2 * half_width :])
     rows = lax.broadcasted_iota(jnp.int32, values.shape, 0)
     columns = lax.broadcasted_iota(jnp.int32, values.shape, 1)

time: 82.3 us -> 80.5 us (0.978)
  starting transfers between devices: 20.3 us -> 18.4 us
  Pallas kernels: 30.5 us -> 28.6 us
  waiting for transfers between devices: 17.3 us -> 18.9 us
    pallas_call x1, Pallas kernels: 18 us -> 16.1 us  [image_pooled(): pl.pallas_call(image_kernel, in_specs=[pl.BlockSpec(memory_space=pltpu.SM...]
    all_to_all x1, waiting for transfers between devices: 0.19 us -> 2.07 us  [per_device_parts(): pieces = lax.all_to_all(message, 'dp', 0, 0, tiled=True)]
    all_to_all x1, starting transfers between devices: 5.77 us -> 3.91 us  [spread(): lax.all_to_all(jnp.broadcast_to(rows[None], (count,) + rows.shape), axis_...]
  transfers between devices with their start and end apart: 13 -> 13, of which waited for: 8 -> 9; matrix products, arithmetic and copies ran while one was open for 1% -> 1% of each run, Pallas kernels for 26% -> 24%
where the time goes in v7:
time: 80.5 us; the launch traced here: 80 us
  Pallas kernels  28.6 us (36%)
  waiting for transfers between devices  18.9 us (23%)
  starting transfers between devices  18.4 us (23%)
  blocking collectives  10.1 us (13%)
  local copies, waits for them, and re-layouts  2.12 us (3%)
  between operations  0.91 us (1%)
    pallas_call x1, Pallas kernels, image_pooled(): pl.pallas_call(image_kernel, in_specs=[pl.BlockSpec(memory_space=pltpu.SM...  16.1 us
    all_to_all x1, blocking collectives, spread(): lax.all_to_all(jnp.broadcast_to(rows[None], (count,) + rows.shape), axis_...  10.1 us
    all_to_all x1, waiting for transfers between devices, spread(): lax.all_to_all(jnp.broadcast_to(rows[None], (count,) + rows.shape), axis_...  7.36 us
    all_to_all x1, starting transfers between devices, per_device_parts(): pieces = lax.all_to_all(message, 'dp', 0, 0, tiled=True)  7.03 us
    pallas_call x1, Pallas kernels, quantizer(): pl.pallas_call(functools.partial(quantizer_kernel, loss_scale), in_specs=...  4.03 us
    all_to_all x1, starting transfers between devices, spread(): lax.all_to_all(jnp.broadcast_to(rows[None], (count,) + rows.shape), axis_...  3.91 us
    ppermute x1, waiting for transfers between devices, per_device_parts(): lax.ppermute(mine, 'segment', [(i, i ^ 2) for i in range(segment_count)])  3.8 us
    ppermute x2, starting transfers between devices, around(): side = lax.ppermute(across, 'dp', [(i, i ^ 1) for i in range(dp_count)])  2.95 us
  transfers between devices with their start and end apart: 13, of which 9 were waited for; matrix products, arithmetic and copies ran while one was open for 1% of the time, Pallas kernels for 24%

profile of v7, /device:TPU:0, one launch (start us, length us, event | category | flops | bytes accessed | tf_op | source)
XLA Modules:
  0.0 80.0 jit_solution(15176269439554598293)
XLA Ops:
  0.7 2.6 %shard_map.137 = bf16[8,464,128]{2,1,0:T(8,128)(2,1)} custom-call(bf16[448,1024]{1,0:T(8,128)(2,1)} %rows_ref.1), custom_call_target="tpu_custom_call" | custom-call | bytes 1835008 | tf_op jit(solution)/shard_map/pallas_call | solution.py:383
  3.3 7.0 %all-to-all-start = ((bf16[8,464,128]{2,1,0:T(8,128)(2,1)}), bf16[8,464,128]{2,1,0:T(8,128)(2,1)S(1)}, u32[]{:S(2)}, u32[]{:S(2)}) async-start(bf16[8,464,128]{2,1,0:T(8,128)(2,1)} %shard_map.137), calls=%async_computation | async-start | bytes 1900544 | tf_op jit(solution)/shard_map/all_to_all | solution.py:766
  10.3 16.4 %conditional.1 = (f32[8,1536]{1,0:T(8,128)S(1)}) conditional(s32[]{:T(128)} %convert_element_type.34, (s32[1]{0:T(128)}, bf16[8,64,1536]{2,1,0:T(8,128)(2,1)S(1)}, bf16[1,21504,128]{2,1,0:T(8,128)(2,1)}) %tuple.32, (s32[1]{0:T(128)}, bf16[8,256,1024]{2,1,0:T(8,128)(2,1)}, bf16[1,21504,128]{2,1,0:T(8,128)(2,1)}) %tuple.19), branch_computations={%region_0.1_spmd.clone, %region_1.2_spmd} | conditional | bytes 2097216 | solution.py:828
  10.3 16.1 %branch_1_fun.1 = f32[8,1024]{1,0:T(8,128)S(1)} custom-call(s32[1]{0:T(128)} %get-tuple-element.24.flag_ref, bf16[8,256,1024]{2,1,0:T(8,128)(2,1)} %get-tuple-element.81.image_hbm, bf16[1,21504,128]{2,1,0:T(8,128)(2,1)} %get-tuple-element.26.slot_hbm), custom_call_target="tpu_custom_call" | custom-call | tf_op jit(solution)/shard_map/cond/branch_1_fun/pallas_call | solution.py:166
  27.2 0.2 select_reduce_fusion
  27.4 0.6 collective-permute-done
  28.1 3.8 %collective-permute-done.1 = bf16[8,1536]{1,0:T(8,128)(2,1)S(1)} collective-permute-done((bf16[8,1536]{1,0:T(8,128)(2,1)S(1)}, bf16[8,1536]{1,0:T(8,128)(2,1)S(1)}, u32[]{:S(2)}, u32[]{:S(2)}) %collective-permute-start.1) | collective-permute-done | bytes 24608 | tf_op jit(solution)/shard_map/ppermute | solution.py:770
  31.9 2.1 %all-to-all-done.weights = bf16[8,464,128]{2,1,0:T(8,128)(2,1)S(1)} async-done(((bf16[8,464,128]{2,1,0:T(8,128)(2,1)}), bf16[8,464,128]{2,1,0:T(8,128)(2,1)S(1)}, u32[]{:S(2)}, u32[]{:S(2)}) %all-to-all-start) | async-done | bytes 950304 | tf_op jit(solution)/shard_map/all_to_all | solution.py:766
  34.0 0.7 broadcast_in_dim.26
  34.7 3.9 %all-to-all-start.1 = ((bf16[8,8,1280]{2,1,0:T(8,128)(2,1)}), bf16[8,8,1280]{2,1,0:T(8,128)(2,1)S(1)}, u32[]{:S(2)}, u32[]{:S(2)}) async-start(bf16[8,8,1280]{2,1,0:T(8,128)(2,1)} %broadcast_in_dim.26), calls=%async_computation.1 | async-start | bytes 327680 | tf_op jit(solution)/shard_map/all_to_all | solution.py:745
  38.8 7.4 %all-to-all-done.1.mine_ref = bf16[8,8,1280]{2,1,0:T(8,128)(2,1)S(1)} async-done(((bf16[8,8,1280]{2,1,0:T(8,128)(2,1)}), bf16[8,8,1280]{2,1,0:T(8,128)(2,1)S(1)}, u32[]{:S(2)}, u32[]{:S(2)}) %all-to-all-start.1) | async-done | bytes 163872 | tf_op jit(solution)/shard_map/all_to_all | solution.py:745
  46.2 1.4 %collective-permute-done.2.twin_ref = bf16[8,8,1280]{2,1,0:T(8,128)(2,1)S(1)} collective-permute-done((bf16[8,8,1280]{2,1,0:T(8,128)(2,1)S(1)}, bf16[8,8,1280]{2,1,0:T(8,128)(2,1)S(1)}, u32[]{:S(2)}, u32[]{:S(2)}) %collective-permute-start.2) | collective-permute-done | bytes 163872 | tf_op jit(solution)/shard_map/ppermute | solution.py:779
  47.6 0.8 shard_map.138
  48.3 0.2 collective-permute-start.3
  48.5 1.1 %collective-permute-done.3 = f32[16,1024]{1,0:T(8,128)S(1)} collective-permute-done((f32[16,1024]{1,0:T(8,128)S(1)}, f32[16,1024]{1,0:T(8,128)S(1)}, u32[]{:S(2)}, u32[]{:S(2)}) %collective-permute-start.3) | collective-permute-done | bytes 65568 | tf_op jit(solution)/shard_map/ppermute | solution.py:804
  49.6 1.6 %collective-permute-start.6 = (f32[8,1024]{1,0:T(8,128)S(1)}, f32[8,1024]{1,0:T(8,128)S(1)}, u32[]{:S(2)}, u32[]{:S(2)}) collective-permute-start(f32[8,1024]{1,0:T(8,128)S(1)} %get-tuple-element.89), channel_id=1, source_target_pairs={{0,17},{1,16},{2,19},{3,18},{4,21},{5,20},{6,23},{7,22},{8,25},{9,... | collective-permute-start | bytes 98312 | tf_op jit(solution)/shard_map/ppermute | solution.py:740
  51.2 1.1 %collective-permute-start.5 = (f32[8,1024]{1,0:T(8,128)S(1)}, f32[8,1024]{1,0:T(8,128)S(1)}, u32[]{:S(2)}, u32[]{:S(2)}) collective-permute-start(f32[8,1024]{1,0:T(8,128)S(1)} %get-tuple-element.89), channel_id=1, source_target_pairs={{0,1},{1,0},{2,3},{3,2},{4,5},{5,4},{6,7},{7,6},{8,9},{9,8},{10,11... | collective-permute-start | bytes 98312 | tf_op jit(solution)/shard_map/ppermute | solution.py:736
  52.3 0.8 %collective-permute-start.4 = (f32[8,1024]{1,0:T(8,128)S(1)}, f32[8,1024]{1,0:T(8,128)S(1)}, u32[]{:S(2)}, u32[]{:S(2)}) collective-permute-start(f32[8,1024]{1,0:T(8,128)S(1)} %get-tuple-element.88), channel_id=1, source_target_pairs={{0,16},{8,24},{16,0},{24,8},{1,17},{9,25},{17,1},{25,9},{2,18},{10... | collective-permute-start | bytes 98312 | tf_op jit(solution)/shard_map/ppermute | solution.py:735
  53.2 0.2 convert_reduce_fusion.count_ref
  53.4 1.0 %copy-done.1 = bf16[1,256,1024]{2,1,0:T(8,128)(2,1)S(1)} copy-done((bf16[1,256,1024]{2,1,0:T(8,128)(2,1)S(1)}, bf16[1,256,1024]{2,1,0:T(8,128)(2,1)}, u32[]{:S(2)}) %copy-start.1) | copy-done | bytes 524312
  54.5 1.1 %shard_map.139 = (bf16[2,256,1024]{2,1,0:T(8,128)(2,1)S(1)}, bf16[2,256,1024]{2,1,0:T(8,128)(2,1)S(1)}, f32[2,8,256]{2,1,0:T(8,128)S(1)}, f32[8,256]{1,0:T(8,128)S(1)}) custom-call(f32[2,256,1024]{2,1,0:T(8,128)S(1)} %bitcast.16, bf16[256,1024]{1,0:T(8,128)(2,1)S(1)} %bitcast.18), custom_call_target="tpu_custom_call" | custom-call | bytes 6291456 | tf_op jit(solution)/shard_map/pallas_call | solution.py:512
  55.5 0.7 collective-permute-done.4
  56.3 4.0 %shard_map.140 = (bf16[8,1024]{1,0:T(8,128)(2,1)S(1)}, f32[1]{0:T(128)}, f32[2,16,256]{2,1,0:T(8,128)S(1)}, f32[2,16,1024]{2,1,0:T(8,128)S(1)}) custom-call(f32[8,1024]{1,0:T(8,128)S(1)} %add_add_fusion.merged_ref, bf16[2,256,1024]{2,1,0:T(8,128)(2,1)S(1)} %get-tuple-element.59.highs, bf16[2,256,1024]{2,1,0:T(8,128)(2,1)S(1)} %get-tuple-element.60.lows, ...), custom_call_target="tpu_custom_call" | custom-call | flops 33554432 | bytes 2097152 | tf_op jit(solution)/shard_map/pallas_call | solution.py:608
  60.3 10.1 %all_to_all.15.gathered_ref = bf16[8,8,1024]{2,1,0:T(8,128)(2,1)S(1)} all-to-all(bf16[8,8,1024]{2,1,0:T(8,128)(2,1)S(1)} %broadcast_in_dim.50), channel_id=1, replica_groups=mesh['segment'=4,'dp'=8] {'dp'}, dimensions={0} | all-to-all | bytes 262144 | tf_op jit(solution)/shard_map/all_to_all | solution.py:745
  70.4 0.4 shard_map.141
  70.8 0.3 collective-permute-start.9
  71.0 1.8 %collective-permute-start.8 = (bf16[64,256]{1,0:T(8,128)(2,1)S(1)}, bf16[64,256]{1,0:T(8,128)(2,1)S(1)}, u32[]{:S(2)}, u32[]{:S(2)}) collective-permute-start(bf16[64,256]{1,0:T(8,128)(2,1)S(1)} %get-tuple-element.68), channel_id=1, source_target_pairs={{0,1},{1,0},{2,3},{3,2},{4,5},{5,4},{6,7},{7,6},{8,9},{9,8},{10,11... | collective-permute-start | bytes 98312 | tf_op jit(solution)/shard_map/ppermute | solution.py:736
  72.8 1.5 %collective-permute-start.7 = (bf16[64,256]{1,0:T(8,128)(2,1)S(1)}, bf16[64,256]{1,0:T(8,128)(2,1)S(1)}, u32[]{:S(2)}, u32[]{:S(2)}) collective-permute-start(bf16[64,256]{1,0:T(8,128)(2,1)S(1)} %get-tuple-element.68), channel_id=1, source_target_pairs={{0,16},{8,24},{16,0},{24,8},{1,17},{9,25},{17,1},{25,9},{2,18},{10... | collective-permute-start | bytes 98312 | tf_op jit(solution)/shard_map/ppermute | solution.py:735
  74.3 1.9 %shard_map.142 = f32[2,256,1024]{2,1,0:T(8,128)} custom-call(f32[2,16,256]{2,1,0:T(8,128)S(1)} %get-tuple-element.69.left_ref, f32[2,16,1024]{2,1,0:T(8,128)S(1)} %get-tuple-element.70.right_ref, f32[2,256,1024]{2,1,0:T(8,128)S(1)} %bitcast.17), custom_call_target="tpu_custom_call" | custom-call | flops 50331648 | bytes 4194304 | tf_op jit(solution)/shard_map/pallas_call | solution.py:638
  76.2 0.5 collective-permute-done.7
  76.9 1.3 %collective-permute-done.10.twin_ref = bf16[4,64,256]{2,1,0:T(8,128)(2,1)S(1)} collective-permute-done((bf16[4,64,256]{2,1,0:T(8,128)(2,1)S(1)}, bf16[4,64,256]{2,1,0:T(8,128)(2,1)S(1)}, u32[]{:S(2)}, u32[]{:S(2)}) %collective-permute-start.10) | collective-permute-done | bytes 131104 | tf_op jit(solution)/shard_map/ppermute | solution.py:813
  78.2 1.8 %shard_map.143 = f32[448,1024]{1,0:T(8,128)} custom-call(bf16[64,448]{1,0:T(8,128)(2,1)S(1)} %get-tuple-element.56.block_ref, bf16[64,1024]{1,0:T(8,128)(2,1)S(1)} %get-tuple-element.67.out_grad_ref, bf16[4,64,256]{2,1,0:T(8,128)(2,1)S(1)} %pad_maximum_fusion.mine_ref, bf16[4,64,256]{2,1,0:T(8,128)(2,1)S(1)} %collective-permute-done.10.twin_ref), custom_call_target="tpu_custom_call" | custom-call | flops 58720256 | bytes 1835008 | tf_op jit(solution)/shard_map/pallas_call | solution.py:723
  (44 shorter events, 1.0 us)
Async XLA Ops:
  0.6 9.7 %copy-start.5 = (bf16[8,64,1536]{2,1,0:T(8,128)(2,1)S(1)}, bf16[8,64,1536]{2,1,0:T(8,128)(2,1)}, u32[]{:S(2)}) copy-start(bf16[8,64,1536]{2,1,0:T(8,128)(2,1)} %param.14) | copy-start | bytes 4718596
  3.3 35.4 %copy-start.6 = (s32[4,16,128]{2,1,0:T(8,128)S(1)}, s32[4,16,128]{2,1,0:T(8,128)}, u32[]{:S(2)}) copy-start(s32[4,16,128]{2,1,0:T(8,128)} %param.21) | copy-start | bytes 98308
  3.3 30.7 %all-to-all-start = ((bf16[8,464,128]{2,1,0:T(8,128)(2,1)}), bf16[8,464,128]{2,1,0:T(8,128)(2,1)S(1)}, u32[]{:S(2)}, u32[]{:S(2)}) async-start(bf16[8,464,128]{2,1,0:T(8,128)(2,1)} %shard_map.137), calls=%async_computation | async-start | bytes 1900544 | tf_op jit(solution)/shard_map/all_to_all | solution.py:766
  10.3 16.5 %copy-start.7 = (s32[4,16,1]{1,2,0:T(1,128)S(1)}, s32[4,16,1]{1,2,0:T(1,128)}, u32[]{:S(2)}) copy-start(s32[4,16,1]{1,2,0:T(1,128)} %param.19) | copy-start | bytes 772
  10.3 16.8 %copy-start.8 = (s32[8]{0:T(128)S(1)}, s32[8]{0:T(128)}, u32[]{:S(2)}) copy-start(s32[8]{0:T(128)} %param.20) | copy-start | bytes 100
  26.7 26.7 %copy-start = (f32[1,2,256,1024]{3,2,1,0:T(8,128)S(1)}, f32[1,2,256,1024]{3,2,1,0:T(8,128)}, u32[]{:S(2)}) copy-start(f32[1,2,256,1024]{3,2,1,0:T(8,128)} %param.17) | copy-start | bytes 6291460
  26.7 1.3 %collective-permute-start = (f32[8,1536]{1,0:T(8,128)S(1)}, f32[8,1536]{1,0:T(8,128)S(1)}, u32[]{:S(2)}, u32[]{:S(2)}) collective-permute-start(f32[8,1536]{1,0:T(8,128)S(1)} %get-tuple-element.94), channel_id=1, source_target_pairs={{0,8},{8,0},{16,24},{24,16},{1,9},{9,1},{17,25},{25,17},{2,10},{10... | collective-permute-start | bytes 147464 | tf_op jit(solution)/shard_map/ppermute | solution.py:768
  28.0 3.9 %collective-permute-start.1 = (bf16[8,1536]{1,0:T(8,128)(2,1)S(1)}, bf16[8,1536]{1,0:T(8,128)(2,1)S(1)}, u32[]{:S(2)}, u32[]{:S(2)}) collective-permute-start(bf16[8,1536]{1,0:T(8,128)(2,1)S(1)} %add_convert_fusion), channel_id=1, source_target_pairs={{0,16},{8,24},{16,0},{24,8},{1,17},{9,25},{17,1},{25,9},{2,18},{10... | collective-permute-start | bytes 73736 | tf_op jit(solution)/shard_map/ppermute | solution.py:770
  34.7 11.5 %all-to-all-start.1 = ((bf16[8,8,1280]{2,1,0:T(8,128)(2,1)}), bf16[8,8,1280]{2,1,0:T(8,128)(2,1)S(1)}, u32[]{:S(2)}, u32[]{:S(2)}) async-start(bf16[8,8,1280]{2,1,0:T(8,128)(2,1)} %broadcast_in_dim.26), calls=%async_computation.1 | async-start | bytes 327680 | tf_op jit(solution)/shard_map/all_to_all | solution.py:745
  46.2 1.4 %collective-permute-start.2 = (bf16[8,8,1280]{2,1,0:T(8,128)(2,1)S(1)}, bf16[8,8,1280]{2,1,0:T(8,128)(2,1)S(1)}, u32[]{:S(2)}, u32[]{:S(2)}) collective-permute-start(bf16[8,8,1280]{2,1,0:T(8,128)(2,1)S(1)} %all-to-all-done.1.mine_ref), channel_id=1, source_target_pairs={{0,8},{8,0},{16,24},{24,16},{1,9},{9,1},{17,25},{25,17},{2,10},{10... | collective-permute-start | bytes 491528 | tf_op jit(solution)/shard_map/ppermute | solution.py:779
  46.2 10.1 %copy-start.2 = (bf16[1,256,1024]{2,1,0:T(8,128)(2,1)S(1)}, bf16[1,256,1024]{2,1,0:T(8,128)(2,1)}, u32[]{:S(2)}) copy-start(bf16[1,256,1024]{2,1,0:T(8,128)(2,1)} %param.18) | copy-start | bytes 1572868
  48.3 1.3 %collective-permute-start.3 = (f32[16,1024]{1,0:T(8,128)S(1)}, f32[16,1024]{1,0:T(8,128)S(1)}, u32[]{:S(2)}, u32[]{:S(2)}) collective-permute-start(f32[16,1024]{1,0:T(8,128)S(1)} %get-tuple-element.57), channel_id=1, source_target_pairs={{0,8},{8,0},{16,24},{24,16},{1,9},{9,1},{17,25},{25,17},{2,10},{10... | collective-permute-start | bytes 196616 | tf_op jit(solution)/shard_map/ppermute | solution.py:804
  49.6 6.6 %collective-permute-start.6 = (f32[8,1024]{1,0:T(8,128)S(1)}, f32[8,1024]{1,0:T(8,128)S(1)}, u32[]{:S(2)}, u32[]{:S(2)}) collective-permute-start(f32[8,1024]{1,0:T(8,128)S(1)} %get-tuple-element.89), channel_id=1, source_target_pairs={{0,17},{1,16},{2,19},{3,18},{4,21},{5,20},{6,23},{7,22},{8,25},{9,... | collective-permute-start | bytes 98312 | tf_op jit(solution)/shard_map/ppermute | solution.py:740
  51.2 5.1 %collective-permute-start.5 = (f32[8,1024]{1,0:T(8,128)S(1)}, f32[8,1024]{1,0:T(8,128)S(1)}, u32[]{:S(2)}, u32[]{:S(2)}) collective-permute-start(f32[8,1024]{1,0:T(8,128)S(1)} %get-tuple-element.89), channel_id=1, source_target_pairs={{0,1},{1,0},{2,3},{3,2},{4,5},{5,4},{6,7},{7,6},{8,9},{9,8},{10,11... | collective-permute-start | bytes 98312 | tf_op jit(solution)/shard_map/ppermute | solution.py:736
  52.3 3.9 %collective-permute-start.4 = (f32[8,1024]{1,0:T(8,128)S(1)}, f32[8,1024]{1,0:T(8,128)S(1)}, u32[]{:S(2)}, u32[]{:S(2)}) collective-permute-start(f32[8,1024]{1,0:T(8,128)S(1)} %get-tuple-element.88), channel_id=1, source_target_pairs={{0,16},{8,24},{16,0},{24,8},{1,17},{9,25},{17,1},{25,9},{2,18},{10... | collective-permute-start | bytes 98312 | tf_op jit(solution)/shard_map/ppermute | solution.py:735
  53.4 1.0 %copy-start.1 = (bf16[1,256,1024]{2,1,0:T(8,128)(2,1)S(1)}, bf16[1,256,1024]{2,1,0:T(8,128)(2,1)}, u32[]{:S(2)}) copy-start(bf16[1,256,1024]{2,1,0:T(8,128)(2,1)} %param.18) | copy-start | bytes 1572868
  70.8 5.4 %collective-permute-start.9 = (bf16[64,256]{1,0:T(8,128)(2,1)S(1)}, bf16[64,256]{1,0:T(8,128)(2,1)S(1)}, u32[]{:S(2)}, u32[]{:S(2)}) collective-permute-start(bf16[64,256]{1,0:T(8,128)(2,1)S(1)} %get-tuple-element.68), channel_id=1, source_target_pairs={{0,17},{1,16},{2,19},{3,18},{4,21},{5,20},{6,23},{7,22},{8,25},{9,... | collective-permute-start | bytes 98312 | tf_op jit(solution)/shard_map/ppermute | solution.py:740
  71.0 5.2 %collective-permute-start.8 = (bf16[64,256]{1,0:T(8,128)(2,1)S(1)}, bf16[64,256]{1,0:T(8,128)(2,1)S(1)}, u32[]{:S(2)}, u32[]{:S(2)}) collective-permute-start(bf16[64,256]{1,0:T(8,128)(2,1)S(1)} %get-tuple-element.68), channel_id=1, source_target_pairs={{0,1},{1,0},{2,3},{3,2},{4,5},{5,4},{6,7},{7,6},{8,9},{9,8},{10,11... | collective-permute-start | bytes 98312 | tf_op jit(solution)/shard_map/ppermute | solution.py:736
  72.8 3.9 %collective-permute-start.7 = (bf16[64,256]{1,0:T(8,128)(2,1)S(1)}, bf16[64,256]{1,0:T(8,128)(2,1)S(1)}, u32[]{:S(2)}, u32[]{:S(2)}) collective-permute-start(bf16[64,256]{1,0:T(8,128)(2,1)S(1)} %get-tuple-element.68), channel_id=1, source_target_pairs={{0,16},{8,24},{16,0},{24,8},{1,17},{9,25},{17,1},{25,9},{2,18},{10... | collective-permute-start | bytes 98312 | tf_op jit(solution)/shard_map/ppermute | solution.py:735
  76.8 1.4 %collective-permute-start.10 = (bf16[4,64,256]{2,1,0:T(8,128)(2,1)S(1)}, bf16[4,64,256]{2,1,0:T(8,128)(2,1)S(1)}, u32[]{:S(2)}, u32[]{:S(2)}) collective-permute-start(bf16[4,64,256]{2,1,0:T(8,128)(2,1)S(1)} %pad_maximum_fusion.mine_ref), channel_id=1, source_target_pairs={{0,8},{8,0},{16,24},{24,16},{1,9},{9,1},{17,25},{25,17},{2,10},{10... | collective-permute-start | bytes 393224 | tf_op jit(solution)/shard_map/ppermute | solution.py:813

commit v8 on v7

--- a/solution.py
+++ b/solution.py
@@ -20,6 +20,7 @@
 IMAGE_GROUP = 4
 PROJECT_LANES = 256
 OUT_STEP = 128
+GRAD_ROWS = 128
 LOG2_E = 1.4426950408889634
 SIDES = 2
 TILE = 8
@@ -122,12 +123,9 @@
     for fetch in fetches[1:]:
         fetch.wait()
     fetch_out.wait()
-    half = IMAGE_GROUP + IMAGE_GROUP // 2
     for part in range(parts):
         project(0, part)
-        if part == 0:
-            normalize(IMAGE_GROUP, half)
-    normalize(half, item_count)
+        normalize(IMAGE_GROUP + part, IMAGE_GROUP + part + 1)
     out_steps = half_width // OUT_STEP
     units = IMAGE_GROUP * head_count
     for index in range(groups):
@@ -673,7 +671,7 @@
 
 
 def weight_grad_kernel(
-    groups, block_ref, out_grad_ref, mine_ref, twin_ref, grad_ref, hidden_grad, active
+    groups, block_ref, out_grad_ref, mine_ref, twin_ref, grad_ref, hidden_grad, active, built, semaphores
 ):
     shard, segment = lax.axis_index("dp"), lax.axis_index("segment")
     _, items, doubled = mine_ref.shape
@@ -706,14 +704,29 @@
                     offset += share
 
     place_units(hidden_grad, 0)
-    grad_ref[...] = dot_tn(block_ref[...], hidden_grad[...])
-    for group_shard, inside, base, _ in groups:
-
-        @pl.when(shard == group_shard)
-        def _(inside=inside, base=base):
-            place_units(active, columns)
-            wanted = active[:, base : base + shard_rows - inside]
-            grad_ref[inside:, :] = dot_tn(wanted, out_grad_ref[...])
+
+    @pl.when(shard >= groups[0][0])
+    def _():
+        place_units(active, columns)
+
+    edges = [*range(0, shard_rows, GRAD_ROWS), shard_rows]
+    sends = []
+    for index, (low, high) in enumerate(zip(edges[:-1], edges[1:])):
+        built[low:high, :] = dot_tn(block_ref[:, low:high], hidden_grad[...])
+        for group_shard, inside, base, _ in groups:
+            if high > inside:
+                first = max(low, inside)
+
+                @pl.when(shard == group_shard)
+                def _(inside=inside, base=base, first=first, high=high):
+                    wanted = active[:, base + first - inside : base + high - inside]
+                    built[first:high, :] = dot_tn(wanted, out_grad_ref[...])
+
+        send = pltpu.make_async_copy(built.at[low:high], grad_ref.at[low:high], semaphores.at[index])
+        send.start()
+        sends.append(send)
+    for send in sends:
+        send.wait()
 
 
 def weight_grad(block, out_grad, mine, twin, groups):
@@ -723,9 +736,14 @@
     return pl.pallas_call(
         functools.partial(weight_grad_kernel, groups),
         in_specs=[vm] * 4,
-        out_specs=vm,
+        out_specs=pl.BlockSpec(memory_space=pl.ANY),
         out_shape=jax.ShapeDtypeStruct((shard_rows, width), F32),
-        scratch_shapes=[pltpu.VMEM((items, width), BF16), pltpu.VMEM((items, width), BF16)],
+        scratch_shapes=[
+            pltpu.VMEM((items, width), BF16),
+            pltpu.VMEM((items, width), BF16),
+            pltpu.VMEM((shard_rows, width), F32),
+            pltpu.SemaphoreType.DMA((-(-shard_rows // GRAD_ROWS),)),
+        ],
         cost_estimate=cost(2 * items * shard_rows * width, 4 * shard_rows * width),
         compiler_params=pltpu.CompilerParams(vmem_limit_bytes=8 * MIB),
     )(block, out_grad, mine, twin)

time: 80.5 us -> 80.8 us (level)
  no operation moved by 1% of the time
where the time goes in v8:
time: 80.8 us; the launch traced here: 80.4 us
  Pallas kernels  28.8 us (36%)
  waiting for transfers between devices  18.9 us (23%)
  starting transfers between devices  18.4 us (23%)
  blocking collectives  10.1 us (12%)
  local copies, waits for them, and re-layouts  2.12 us (3%)
  between operations  1.09 us (1%)
    pallas_call x1, Pallas kernels, image_pooled(): pl.pallas_call(image_kernel, in_specs=[pl.BlockSpec(memory_space=pltpu.SM...  16.1 us
    all_to_all x1, blocking collectives, spread(): lax.all_to_all(jnp.broadcast_to(rows[None], (count,) + rows.shape), axis_...  10.1 us
    all_to_all x1, waiting for transfers between devices, spread(): lax.all_to_all(jnp.broadcast_to(rows[None], (count,) + rows.shape), axis_...  7.36 us
    all_to_all x1, starting transfers between devices, per_device_parts(): pieces = lax.all_to_all(message, 'dp', 0, 0, tiled=True)  7.03 us
    pallas_call x1, Pallas kernels, quantizer(): pl.pallas_call(functools.partial(quantizer_kernel, loss_scale), in_specs=...  4.03 us
    all_to_all x1, starting transfers between devices, spread(): lax.all_to_all(jnp.broadcast_to(rows[None], (count,) + rows.shape), axis_...  3.91 us
    ppermute x1, waiting for transfers between devices, per_device_parts(): lax.ppermute(mine, 'segment', [(i, i ^ 2) for i in range(segment_count)])  3.8 us
    ppermute x2, starting transfers between devices, around(): side = lax.ppermute(across, 'dp', [(i, i ^ 1) for i in range(dp_count)])  2.95 us
  transfers between devices with their start and end apart: 13, of which 9 were waited for; matrix products, arithmetic and copies ran while one was open for 1% of the time, Pallas kernels for 24%

profile of v8, /device:TPU:0, one launch (start us, length us, event | category | flops | bytes accessed | tf_op | source)
XLA Modules:
  0.0 80.4 jit_solution(3611921989799099427)
XLA Ops:
  0.7 2.6 %shard_map.137 = bf16[8,464,128]{2,1,0:T(8,128)(2,1)} custom-call(bf16[448,1024]{1,0:T(8,128)(2,1)} %rows_ref.1), custom_call_target="tpu_custom_call" | custom-call | bytes 1835008 | tf_op jit(solution)/shard_map/pallas_call | solution.py:381
  3.3 7.0 %all-to-all-start = ((bf16[8,464,128]{2,1,0:T(8,128)(2,1)}), bf16[8,464,128]{2,1,0:T(8,128)(2,1)S(1)}, u32[]{:S(2)}, u32[]{:S(2)}) async-start(bf16[8,464,128]{2,1,0:T(8,128)(2,1)} %shard_map.137), calls=%async_computation | async-start | bytes 1900544 | tf_op jit(solution)/shard_map/all_to_all | solution.py:784
  10.3 16.4 %conditional.1 = (f32[8,1536]{1,0:T(8,128)S(1)}) conditional(s32[]{:T(128)} %convert_element_type.34, (s32[1]{0:T(128)}, bf16[8,64,1536]{2,1,0:T(8,128)(2,1)S(1)}, bf16[1,21504,128]{2,1,0:T(8,128)(2,1)}) %tuple.32, (s32[1]{0:T(128)}, bf16[8,256,1024]{2,1,0:T(8,128)(2,1)}, bf16[1,21504,128]{2,1,0:T(8,128)(2,1)}) %tuple.19), branch_computations={%region_0.1_spmd.clone, %region_1.2_spmd} | conditional | bytes 2097216 | solution.py:846
  10.3 16.1 %branch_1_fun.1 = f32[8,1024]{1,0:T(8,128)S(1)} custom-call(s32[1]{0:T(128)} %get-tuple-element.24.flag_ref, bf16[8,256,1024]{2,1,0:T(8,128)(2,1)} %get-tuple-element.81.image_hbm, bf16[1,21504,128]{2,1,0:T(8,128)(2,1)} %get-tuple-element.26.slot_hbm), custom_call_target="tpu_custom_call" | custom-call | tf_op jit(solution)/shard_map/cond/branch_1_fun/pallas_call | solution.py:164
  27.2 0.2 select_reduce_fusion
  27.4 0.6 collective-permute-done
  28.1 3.8 %collective-permute-done.1 = bf16[8,1536]{1,0:T(8,128)(2,1)S(1)} collective-permute-done((bf16[8,1536]{1,0:T(8,128)(2,1)S(1)}, bf16[8,1536]{1,0:T(8,128)(2,1)S(1)}, u32[]{:S(2)}, u32[]{:S(2)}) %collective-permute-start.1) | collective-permute-done | bytes 24608 | tf_op jit(solution)/shard_map/ppermute | solution.py:788
  31.9 2.1 %all-to-all-done.weights = bf16[8,464,128]{2,1,0:T(8,128)(2,1)S(1)} async-done(((bf16[8,464,128]{2,1,0:T(8,128)(2,1)}), bf16[8,464,128]{2,1,0:T(8,128)(2,1)S(1)}, u32[]{:S(2)}, u32[]{:S(2)}) %all-to-all-start) | async-done | bytes 950304 | tf_op jit(solution)/shard_map/all_to_all | solution.py:784
  34.0 0.7 broadcast_in_dim.26
  34.7 3.9 %all-to-all-start.1 = ((bf16[8,8,1280]{2,1,0:T(8,128)(2,1)}), bf16[8,8,1280]{2,1,0:T(8,128)(2,1)S(1)}, u32[]{:S(2)}, u32[]{:S(2)}) async-start(bf16[8,8,1280]{2,1,0:T(8,128)(2,1)} %broadcast_in_dim.26), calls=%async_computation.1 | async-start | bytes 327680 | tf_op jit(solution)/shard_map/all_to_all | solution.py:763
  38.8 7.4 %all-to-all-done.1.mine_ref = bf16[8,8,1280]{2,1,0:T(8,128)(2,1)S(1)} async-done(((bf16[8,8,1280]{2,1,0:T(8,128)(2,1)}), bf16[8,8,1280]{2,1,0:T(8,128)(2,1)S(1)}, u32[]{:S(2)}, u32[]{:S(2)}) %all-to-all-start.1) | async-done | bytes 163872 | tf_op jit(solution)/shard_map/all_to_all | solution.py:763
  46.2 1.4 %collective-permute-done.2.twin_ref = bf16[8,8,1280]{2,1,0:T(8,128)(2,1)S(1)} collective-permute-done((bf16[8,8,1280]{2,1,0:T(8,128)(2,1)S(1)}, bf16[8,8,1280]{2,1,0:T(8,128)(2,1)S(1)}, u32[]{:S(2)}, u32[]{:S(2)}) %collective-permute-start.2) | collective-permute-done | bytes 163872 | tf_op jit(solution)/shard_map/ppermute | solution.py:797
  47.6 0.8 shard_map.138
  48.3 0.2 collective-permute-start.3
  48.5 1.1 %collective-permute-done.3 = f32[16,1024]{1,0:T(8,128)S(1)} collective-permute-done((f32[16,1024]{1,0:T(8,128)S(1)}, f32[16,1024]{1,0:T(8,128)S(1)}, u32[]{:S(2)}, u32[]{:S(2)}) %collective-permute-start.3) | collective-permute-done | bytes 65568 | tf_op jit(solution)/shard_map/ppermute | solution.py:822
  49.6 1.6 %collective-permute-start.6 = (f32[8,1024]{1,0:T(8,128)S(1)}, f32[8,1024]{1,0:T(8,128)S(1)}, u32[]{:S(2)}, u32[]{:S(2)}) collective-permute-start(f32[8,1024]{1,0:T(8,128)S(1)} %get-tuple-element.89), channel_id=1, source_target_pairs={{0,17},{1,16},{2,19},{3,18},{4,21},{5,20},{6,23},{7,22},{8,25},{9,... | collective-permute-start | bytes 98312 | tf_op jit(solution)/shard_map/ppermute | solution.py:758
  51.2 1.1 %collective-permute-start.5 = (f32[8,1024]{1,0:T(8,128)S(1)}, f32[8,1024]{1,0:T(8,128)S(1)}, u32[]{:S(2)}, u32[]{:S(2)}) collective-permute-start(f32[8,1024]{1,0:T(8,128)S(1)} %get-tuple-element.89), channel_id=1, source_target_pairs={{0,1},{1,0},{2,3},{3,2},{4,5},{5,4},{6,7},{7,6},{8,9},{9,8},{10,11... | collective-permute-start | bytes 98312 | tf_op jit(solution)/shard_map/ppermute | solution.py:754
  52.3 0.8 %collective-permute-start.4 = (f32[8,1024]{1,0:T(8,128)S(1)}, f32[8,1024]{1,0:T(8,128)S(1)}, u32[]{:S(2)}, u32[]{:S(2)}) collective-permute-start(f32[8,1024]{1,0:T(8,128)S(1)} %get-tuple-element.88), channel_id=1, source_target_pairs={{0,16},{8,24},{16,0},{24,8},{1,17},{9,25},{17,1},{25,9},{2,18},{10... | collective-permute-start | bytes 98312 | tf_op jit(solution)/shard_map/ppermute | solution.py:753
  53.2 0.2 convert_reduce_fusion.count_ref
  53.4 1.0 %copy-done.1 = bf16[1,256,1024]{2,1,0:T(8,128)(2,1)S(1)} copy-done((bf16[1,256,1024]{2,1,0:T(8,128)(2,1)S(1)}, bf16[1,256,1024]{2,1,0:T(8,128)(2,1)}, u32[]{:S(2)}) %copy-start.1) | copy-done | bytes 524312
  54.5 1.1 %shard_map.139 = (bf16[2,256,1024]{2,1,0:T(8,128)(2,1)S(1)}, bf16[2,256,1024]{2,1,0:T(8,128)(2,1)S(1)}, f32[2,8,256]{2,1,0:T(8,128)S(1)}, f32[8,256]{1,0:T(8,128)S(1)}) custom-call(f32[2,256,1024]{2,1,0:T(8,128)S(1)} %bitcast.16, bf16[256,1024]{1,0:T(8,128)(2,1)S(1)} %bitcast.18), custom_call_target="tpu_custom_call" | custom-call | bytes 6291456 | tf_op jit(solution)/shard_map/pallas_call | solution.py:510
  55.5 0.7 collective-permute-done.4
  56.3 4.0 %shard_map.140 = (bf16[8,1024]{1,0:T(8,128)(2,1)S(1)}, f32[1]{0:T(128)}, f32[2,16,256]{2,1,0:T(8,128)S(1)}, f32[2,16,1024]{2,1,0:T(8,128)S(1)}) custom-call(f32[8,1024]{1,0:T(8,128)S(1)} %add_add_fusion.merged_ref, bf16[2,256,1024]{2,1,0:T(8,128)(2,1)S(1)} %get-tuple-element.59.highs, bf16[2,256,1024]{2,1,0:T(8,128)(2,1)S(1)} %get-tuple-element.60.lows, ...), custom_call_target="tpu_custom_call" | custom-call | flops 33554432 | bytes 2097152 | tf_op jit(solution)/shard_map/pallas_call | solution.py:606
  60.3 10.1 %all_to_all.15.gathered_ref = bf16[8,8,1024]{2,1,0:T(8,128)(2,1)S(1)} all-to-all(bf16[8,8,1024]{2,1,0:T(8,128)(2,1)S(1)} %broadcast_in_dim.50), channel_id=1, replica_groups=mesh['segment'=4,'dp'=8] {'dp'}, dimensions={0} | all-to-all | bytes 262144 | tf_op jit(solution)/shard_map/all_to_all | solution.py:763
  70.4 0.4 shard_map.141
  70.8 0.3 collective-permute-start.9
  71.0 1.8 %collective-permute-start.8 = (bf16[64,256]{1,0:T(8,128)(2,1)S(1)}, bf16[64,256]{1,0:T(8,128)(2,1)S(1)}, u32[]{:S(2)}, u32[]{:S(2)}) collective-permute-start(bf16[64,256]{1,0:T(8,128)(2,1)S(1)} %get-tuple-element.68), channel_id=1, source_target_pairs={{0,1},{1,0},{2,3},{3,2},{4,5},{5,4},{6,7},{7,6},{8,9},{9,8},{10,11... | collective-permute-start | bytes 98312 | tf_op jit(solution)/shard_map/ppermute | solution.py:754
  72.8 1.5 %collective-permute-start.7 = (bf16[64,256]{1,0:T(8,128)(2,1)S(1)}, bf16[64,256]{1,0:T(8,128)(2,1)S(1)}, u32[]{:S(2)}, u32[]{:S(2)}) collective-permute-start(bf16[64,256]{1,0:T(8,128)(2,1)S(1)} %get-tuple-element.68), channel_id=1, source_target_pairs={{0,16},{8,24},{16,0},{24,8},{1,17},{9,25},{17,1},{25,9},{2,18},{10... | collective-permute-start | bytes 98312 | tf_op jit(solution)/shard_map/ppermute | solution.py:753
  74.3 1.9 %shard_map.142 = f32[2,256,1024]{2,1,0:T(8,128)} custom-call(f32[2,16,256]{2,1,0:T(8,128)S(1)} %get-tuple-element.69.left_ref, f32[2,16,1024]{2,1,0:T(8,128)S(1)} %get-tuple-element.70.right_ref, f32[2,256,1024]{2,1,0:T(8,128)S(1)} %bitcast.17), custom_call_target="tpu_custom_call" | custom-call | flops 50331648 | bytes 4194304 | tf_op jit(solution)/shard_map/pallas_call | solution.py:636
  76.2 0.5 collective-permute-done.7
  76.9 1.3 %collective-permute-done.10.twin_ref = bf16[4,64,256]{2,1,0:T(8,128)(2,1)S(1)} collective-permute-done((bf16[4,64,256]{2,1,0:T(8,128)(2,1)S(1)}, bf16[4,64,256]{2,1,0:T(8,128)(2,1)S(1)}, u32[]{:S(2)}, u32[]{:S(2)}) %collective-permute-start.10) | collective-permute-done | bytes 131104 | tf_op jit(solution)/shard_map/ppermute | solution.py:831
  78.2 2.0 %shard_map.143 = f32[448,1024]{1,0:T(8,128)} custom-call(bf16[64,448]{1,0:T(8,128)(2,1)S(1)} %get-tuple-element.56.block_ref, bf16[64,1024]{1,0:T(8,128)(2,1)S(1)} %get-tuple-element.67.out_grad_ref, bf16[4,64,256]{2,1,0:T(8,128)(2,1)S(1)} %pad_maximum_fusion.mine_ref, bf16[4,64,256]{2,1,0:T(8,128)(2,1)S(1)} %collective-permute-done.10.twin_ref), custom_call_target="tpu_custom_call" | custom-call | flops 58720256 | bytes 1835008 | tf_op jit(solution)/shard_map/pallas_call | solution.py:736
  (44 shorter events, 1.0 us)
Async XLA Ops:
  0.6 9.7 %copy-start.5 = (bf16[8,64,1536]{2,1,0:T(8,128)(2,1)S(1)}, bf16[8,64,1536]{2,1,0:T(8,128)(2,1)}, u32[]{:S(2)}) copy-start(bf16[8,64,1536]{2,1,0:T(8,128)(2,1)} %param.14) | copy-start | bytes 4718596
  3.3 35.4 %copy-start.6 = (s32[4,16,128]{2,1,0:T(8,128)S(1)}, s32[4,16,128]{2,1,0:T(8,128)}, u32[]{:S(2)}) copy-start(s32[4,16,128]{2,1,0:T(8,128)} %param.21) | copy-start | bytes 98308
  3.3 30.7 %all-to-all-start = ((bf16[8,464,128]{2,1,0:T(8,128)(2,1)}), bf16[8,464,128]{2,1,0:T(8,128)(2,1)S(1)}, u32[]{:S(2)}, u32[]{:S(2)}) async-start(bf16[8,464,128]{2,1,0:T(8,128)(2,1)} %shard_map.137), calls=%async_computation | async-start | bytes 1900544 | tf_op jit(solution)/shard_map/all_to_all | solution.py:784
  10.3 16.5 %copy-start.7 = (s32[4,16,1]{1,2,0:T(1,128)S(1)}, s32[4,16,1]{1,2,0:T(1,128)}, u32[]{:S(2)}) copy-start(s32[4,16,1]{1,2,0:T(1,128)} %param.19) | copy-start | bytes 772
  10.3 16.8 %copy-start.8 = (s32[8]{0:T(128)S(1)}, s32[8]{0:T(128)}, u32[]{:S(2)}) copy-start(s32[8]{0:T(128)} %param.20) | copy-start | bytes 100
  26.7 26.7 %copy-start = (f32[1,2,256,1024]{3,2,1,0:T(8,128)S(1)}, f32[1,2,256,1024]{3,2,1,0:T(8,128)}, u32[]{:S(2)}) copy-start(f32[1,2,256,1024]{3,2,1,0:T(8,128)} %param.17) | copy-start | bytes 6291460
  26.7 1.3 %collective-permute-start = (f32[8,1536]{1,0:T(8,128)S(1)}, f32[8,1536]{1,0:T(8,128)S(1)}, u32[]{:S(2)}, u32[]{:S(2)}) collective-permute-start(f32[8,1536]{1,0:T(8,128)S(1)} %get-tuple-element.94), channel_id=1, source_target_pairs={{0,8},{8,0},{16,24},{24,16},{1,9},{9,1},{17,25},{25,17},{2,10},{10... | collective-permute-start | bytes 147464 | tf_op jit(solution)/shard_map/ppermute | solution.py:786
  28.0 3.9 %collective-permute-start.1 = (bf16[8,1536]{1,0:T(8,128)(2,1)S(1)}, bf16[8,1536]{1,0:T(8,128)(2,1)S(1)}, u32[]{:S(2)}, u32[]{:S(2)}) collective-permute-start(bf16[8,1536]{1,0:T(8,128)(2,1)S(1)} %add_convert_fusion), channel_id=1, source_target_pairs={{0,16},{8,24},{16,0},{24,8},{1,17},{9,25},{17,1},{25,9},{2,18},{10... | collective-permute-start | bytes 73736 | tf_op jit(solution)/shard_map/ppermute | solution.py:788
  34.7 11.5 %all-to-all-start.1 = ((bf16[8,8,1280]{2,1,0:T(8,128)(2,1)}), bf16[8,8,1280]{2,1,0:T(8,128)(2,1)S(1)}, u32[]{:S(2)}, u32[]{:S(2)}) async-start(bf16[8,8,1280]{2,1,0:T(8,128)(2,1)} %broadcast_in_dim.26), calls=%async_computation.1 | async-start | bytes 327680 | tf_op jit(solution)/shard_map/all_to_all | solution.py:763
  46.2 1.4 %collective-permute-start.2 = (bf16[8,8,1280]{2,1,0:T(8,128)(2,1)S(1)}, bf16[8,8,1280]{2,1,0:T(8,128)(2,1)S(1)}, u32[]{:S(2)}, u32[]{:S(2)}) collective-permute-start(bf16[8,8,1280]{2,1,0:T(8,128)(2,1)S(1)} %all-to-all-done.1.mine_ref), channel_id=1, source_target_pairs={{0,8},{8,0},{16,24},{24,16},{1,9},{9,1},{17,25},{25,17},{2,10},{10... | collective-permute-start | bytes 491528 | tf_op jit(solution)/shard_map/ppermute | solution.py:797
  46.2 10.1 %copy-start.2 = (bf16[1,256,1024]{2,1,0:T(8,128)(2,1)S(1)}, bf16[1,256,1024]{2,1,0:T(8,128)(2,1)}, u32[]{:S(2)}) copy-start(bf16[1,256,1024]{2,1,0:T(8,128)(2,1)} %param.18) | copy-start | bytes 1572868
  48.3 1.3 %collective-permute-start.3 = (f32[16,1024]{1,0:T(8,128)S(1)}, f32[16,1024]{1,0:T(8,128)S(1)}, u32[]{:S(2)}, u32[]{:S(2)}) collective-permute-start(f32[16,1024]{1,0:T(8,128)S(1)} %get-tuple-element.57), channel_id=1, source_target_pairs={{0,8},{8,0},{16,24},{24,16},{1,9},{9,1},{17,25},{25,17},{2,10},{10... | collective-permute-start | bytes 196616 | tf_op jit(solution)/shard_map/ppermute | solution.py:822
  49.6 6.6 %collective-permute-start.6 = (f32[8,1024]{1,0:T(8,128)S(1)}, f32[8,1024]{1,0:T(8,128)S(1)}, u32[]{:S(2)}, u32[]{:S(2)}) collective-permute-start(f32[8,1024]{1,0:T(8,128)S(1)} %get-tuple-element.89), channel_id=1, source_target_pairs={{0,17},{1,16},{2,19},{3,18},{4,21},{5,20},{6,23},{7,22},{8,25},{9,... | collective-permute-start | bytes 98312 | tf_op jit(solution)/shard_map/ppermute | solution.py:758
  51.2 5.1 %collective-permute-start.5 = (f32[8,1024]{1,0:T(8,128)S(1)}, f32[8,1024]{1,0:T(8,128)S(1)}, u32[]{:S(2)}, u32[]{:S(2)}) collective-permute-start(f32[8,1024]{1,0:T(8,128)S(1)} %get-tuple-element.89), channel_id=1, source_target_pairs={{0,1},{1,0},{2,3},{3,2},{4,5},{5,4},{6,7},{7,6},{8,9},{9,8},{10,11... | collective-permute-start | bytes 98312 | tf_op jit(solution)/shard_map/ppermute | solution.py:754
  52.3 3.9 %collective-permute-start.4 = (f32[8,1024]{1,0:T(8,128)S(1)}, f32[8,1024]{1,0:T(8,128)S(1)}, u32[]{:S(2)}, u32[]{:S(2)}) collective-permute-start(f32[8,1024]{1,0:T(8,128)S(1)} %get-tuple-element.88), channel_id=1, source_target_pairs={{0,16},{8,24},{16,0},{24,8},{1,17},{9,25},{17,1},{25,9},{2,18},{10... | collective-permute-start | bytes 98312 | tf_op jit(solution)/shard_map/ppermute | solution.py:753
  53.4 1.0 %copy-start.1 = (bf16[1,256,1024]{2,1,0:T(8,128)(2,1)S(1)}, bf16[1,256,1024]{2,1,0:T(8,128)(2,1)}, u32[]{:S(2)}) copy-start(bf16[1,256,1024]{2,1,0:T(8,128)(2,1)} %param.18) | copy-start | bytes 1572868
  70.8 5.4 %collective-permute-start.9 = (bf16[64,256]{1,0:T(8,128)(2,1)S(1)}, bf16[64,256]{1,0:T(8,128)(2,1)S(1)}, u32[]{:S(2)}, u32[]{:S(2)}) collective-permute-start(bf16[64,256]{1,0:T(8,128)(2,1)S(1)} %get-tuple-element.68), channel_id=1, source_target_pairs={{0,17},{1,16},{2,19},{3,18},{4,21},{5,20},{6,23},{7,22},{8,25},{9,... | collective-permute-start | bytes 98312 | tf_op jit(solution)/shard_map/ppermute | solution.py:758
  71.0 5.2 %collective-permute-start.8 = (bf16[64,256]{1,0:T(8,128)(2,1)S(1)}, bf16[64,256]{1,0:T(8,128)(2,1)S(1)}, u32[]{:S(2)}, u32[]{:S(2)}) collective-permute-start(bf16[64,256]{1,0:T(8,128)(2,1)S(1)} %get-tuple-element.68), channel_id=1, source_target_pairs={{0,1},{1,0},{2,3},{3,2},{4,5},{5,4},{6,7},{7,6},{8,9},{9,8},{10,11... | collective-permute-start | bytes 98312 | tf_op jit(solution)/shard_map/ppermute | solution.py:754
  72.8 3.9 %collective-permute-start.7 = (bf16[64,256]{1,0:T(8,128)(2,1)S(1)}, bf16[64,256]{1,0:T(8,128)(2,1)S(1)}, u32[]{:S(2)}, u32[]{:S(2)}) collective-permute-start(bf16[64,256]{1,0:T(8,128)(2,1)S(1)} %get-tuple-element.68), channel_id=1, source_target_pairs={{0,16},{8,24},{16,0},{24,8},{1,17},{9,25},{17,1},{25,9},{2,18},{10... | collective-permute-start | bytes 98312 | tf_op jit(solution)/shard_map/ppermute | solution.py:753
  76.8 1.4 %collective-permute-start.10 = (bf16[4,64,256]{2,1,0:T(8,128)(2,1)S(1)}, bf16[4,64,256]{2,1,0:T(8,128)(2,1)S(1)}, u32[]{:S(2)}, u32[]{:S(2)}) collective-permute-start(bf16[4,64,256]{2,1,0:T(8,128)(2,1)S(1)} %pad_maximum_fusion.mine_ref), channel_id=1, source_target_pairs={{0,8},{8,0},{16,24},{24,16},{1,9},{9,1},{17,25},{25,17},{2,10},{10... | collective-permute-start | bytes 393224 | tf_op jit(solution)/shard_map/ppermute | solution.py:831
